TPU v7x, 512 devices: a whole 4x4x16 slice. The times are simulated.
512 devices in a mesh: dp: 64 (over x_hi, z, core), mp: 8 (over x_lo, y).
Axes of the slice: x: 4 (x_hi: 2, x_lo: 2; x = x_hi * 2 + x_lo), y: 4, z: 16, core: 2. Of those that a mesh axis runs over, the one named last changes fastest.
Arguments:
- tokens: bfloat16 [16384, 6144], P('dp', 'mp'), may hold values from -6 to 6
- w_in: bfloat16 [128, 48, 512], P('dp', 'mp'), may hold values from -0.5 to 0.5
- w_out: bfloat16 [512, 48, 128], P('dp', 'mp'), may hold values from -0.25 to 0.25
- cotangent: bfloat16 [16384, 6144], P('dp', 'mp'), may hold values from -6 to 6
Outputs:
- output: bfloat16 [16384, 6144], P('dp', 'mp')
- grad_tokens: bfloat16 [16384, 6144], P('dp', 'mp')
- grad_in: float32 [128, 48, 512], P('dp', 'mp')
- grad_out: float32 [512, 48, 128], P('dp', 'mp')
All inputs are finite; a program needn't handle non-finite values.
Results may differ from a plain program's by a relative error of at most 0.0057.
Values may be sent and summed in bfloat16 or wider, within the bound.
No kernel may reach another device: no remote copies, remote signals or barrier semaphores. Data moves between devices by JAX's collectives and lax.ppermute only.
A program may use at most 64 MiB of HBM per device.

v0:
```python
import jax
import jax.numpy as jnp
from jax import lax
from jax.sharding import PartitionSpec as P

BLK = 128
NB = 48
EXP = 512
TILES = 192


def gelu_tanh(value):
    return jax.nn.gelu(value, approximate=True)


def on_device(tokens, w_in, w_out, cotangent):
    f32 = jnp.float32
    bf16 = jnp.bfloat16
    rows = tokens.shape[0]
    groups = lax.axis_size("mp")
    nb_local = NB // groups
    tiles_local = nb_local * EXP // BLK
    piece_cols = BLK // groups
    x3 = tokens.reshape(rows, nb_local, BLK)
    c3 = cotangent.reshape(rows, nb_local, BLK)
    scale = 1.0 / jnp.sqrt(f32(rows * lax.axis_size("dp")))
    win_all, wout_all = (
        lax.all_gather(w_in, "dp", axis=0, tiled=True),
        lax.all_gather(w_out, "dp", axis=0, tiled=True),
    )
    pre = jnp.einsum("tir,rie->tie", x3, win_all, preferred_element_type=f32)
    act = gelu_tanh(pre).astype(bf16)
    tiled = act.reshape(rows, tiles_local, BLK)
    moved = lax.all_to_all(tiled, "mp", split_axis=2, concat_axis=1, tiled=True)
    count = moved.shape[0]
    mixed_part = moved.transpose(0, 2, 1).reshape(count, nb_local, EXP)
    out_part = jnp.einsum("toe,eon->ton", mixed_part, wout_all, preferred_element_type=f32)
    output = out_part.astype(bf16).reshape(rows, nb_local * BLK)
    d_mixed = jnp.einsum("ton,eon->toe", c3, wout_all, preferred_element_type=f32).astype(bf16)
    grad_out = (
        lax.psum_scatter(
            jnp.einsum("toe,ton->eon", mixed_part, c3, preferred_element_type=f32),
            "dp",
            scatter_dimension=0,
            tiled=True,
        )
        * scale
    )
    back_send = d_mixed.reshape(rows, piece_cols, TILES).transpose(0, 2, 1)
    back = lax.all_to_all(back_send, "mp", split_axis=1, concat_axis=2, tiled=True)
    d_act = back.reshape(rows, nb_local, EXP)
    _, pull = jax.vjp(gelu_tanh, pre)
    d_pre = pull(d_act.astype(f32))[0].astype(bf16)
    grad_x = jnp.einsum("tie,rie->tir", d_pre, win_all, preferred_element_type=f32)
    grad_tokens = grad_x.astype(bf16).reshape(rows, nb_local * BLK)
    grad_in = (
        lax.psum_scatter(
            jnp.einsum("tir,tie->rie", x3, d_pre, preferred_element_type=f32),
            "dp",
            scatter_dimension=0,
            tiled=True,
        )
        * scale
    )
    return (output, grad_tokens, grad_in, grad_out)


def solution(mesh):
    placed = (P("dp", "mp"), P("dp", "mp", None), P("dp", "mp", None), P("dp", "mp"))
    return jax.shard_map(
        on_device,
        mesh=mesh,
        in_specs=placed,
        out_specs=(P("dp", "mp"), P("dp", "mp"), P("dp", "mp", None), P("dp", "mp", None)),
        check_vma=False,
    )
```

profile of v0, /device:TPU:1, one launch (start us, length us, event | category | flops | bytes accessed | tf_op | source)
XLA Modules:
  0.0 606.2 jit_solution(12145582178825298438)
XLA Ops:
  7.2 1.2 copy.55
  8.3 86.9 %all_gather.7 = bf16[512,6,128]{2,0,1:T(8,128)(2,1)S(1)} all-gather(bf16[8,6,128]{2,0,1:T(8,128)(2,1)} %param.6), channel_id=1, replica_groups=mesh['dp'=64,'mp'=8] {'dp'}, dimensions={0}, use_global_device_ids=true | all-gather | bytes 798720 | tf_op jit(solution)/shard_map/all_gather | solution.py:29
  95.3 0.6 convolution_convert_fusion
  95.8 0.0 copy-start.4
  95.8 0.0 copy-start.3
  95.8 2.0 copy.81
  97.9 4.2 all-to-all-start.1
  102.1 0.0 reduce-scatter.3.cloned.1.call-start
  102.2 0.0 copy-done.4
  102.2 0.0 copy-done.3
  102.2 0.2 copy.47
  102.4 80.0 %all_gather.6 = bf16[128,6,512]{2,1,0:T(8,128)(2,1)} all-gather(bf16[2,6,512]{2,1,0:T(8,128)(2,1)S(1)} %copy.46), channel_id=1, replica_groups=mesh['dp'=64,'mp'=8] {'dp'}, dimensions={0}, use_global_device_ids=true | all-gather | bytes 798720 | tf_op jit(solution)/shard_map/all_gather | solution.py:28
  182.3 0.0 all-to-all-done.1
  182.3 0.4 convert_bitcast_fusion
  182.8 0.0 copy-start.1
  182.8 0.4 copy.58
  183.2 0.8 copy-done.1
  184.0 3.9 fusion.6
  187.9 0.0 copy-start
  187.9 1.1 copy-done
  189.0 0.6 convolution_bitcast_fusion.1
  189.6 2.0 copy.62
  191.6 0.0 copy-start.2
  191.6 0.0 reduce-scatter.3.cloned.1.call-update
  191.6 0.0 reduce-scatter.5.cloned.1.call-start
  191.7 1.3 copy-done.2
  193.0 0.9 copy.50
  193.9 25.2 %all_to_all.27 = bf16[256,24,128]{0,1,2:T(8,128)(2,1)S(1)} all-to-all(bf16[256,24,128]{0,1,2:T(8,128)(2,1)S(1)} %copy.50), channel_id=1, replica_groups=mesh['dp'=64,'mp'=8] {'mp'}, dimensions={2} | all-to-all | bytes 3145728 | tf_op jit(solution)/shard_map/all_to_all | solution.py:34
  219.1 0.3 copy.52
  219.4 0.6 copy.53
  220.0 1.7 convolution_bitcast_fusion
  221.7 0.0 reduce-scatter.5.cloned.1.call-update
  221.7 2.2 convolution_convert_fusion.1
  223.9 0.9 copy.65
  224.8 0.4 convolution_convert_fusion.2
  225.3 0.9 copy.64
  226.2 159.6 %reduce-scatter.3.cloned.1.call-done = f32[2,6,512]{2,1,0:T(8,128)} async-done(((f32[128,6,512]{2,1,0:T(8,128)}), f32[2,6,512]{2,1,0:T(8,128)}) %reduce-scatter.3.cloned.1.call-update) | async-done | bytes 24592 | tf_op jit(solution)/shard_map/reduce_scatter | solution.py:57
  385.8 0.8 broadcast_multiply_fusion
  386.5 0.6 copy.66
  387.1 210.9 %reduce-scatter.5.cloned.1.call-done = f32[8,6,128]{2,0,1:T(8,128)} async-done(((f32[512,6,128]{2,0,1:T(8,128)}), f32[8,6,128]{2,0,1:T(8,128)}) %reduce-scatter.5.cloned.1.call-update) | async-done | bytes 24592 | tf_op jit(solution)/shard_map/reduce_scatter | solution.py:41
  598.0 1.3 broadcast_multiply_fusion.1
  (1 shorter events, 0.0 us)
Async XLA Ops:
  95.8 6.3 %copy-start.4 = (bf16[2,6,512]{2,0,1:T(2,128)(2,1)S(1)}, bf16[2,6,512]{2,0,1:T(2,128)(2,1)}, u32[]{:S(2)}) copy-start(bf16[2,6,512]{2,0,1:T(2,128)(2,1)} %param.5) | copy-start | bytes 36868
  95.8 6.3 %copy-start.3 = (bf16[256,768]{1,0:T(8,128)(2,1)S(1)}, bf16[256,768]{1,0:T(8,128)(2,1)}, u32[]{:S(2)}) copy-start(bf16[256,768]{1,0:T(8,128)(2,1)} %param.4) | copy-start | bytes 1179652
  97.9 84.5 %all-to-all-start.1 = ((bf16[256,192,16]{0,2,1:T(8,128)(2,1)}), bf16[256,192,16]{0,2,1:T(8,128)(2,1)S(1)}, u32[]{:S(2)}, u32[]{:S(2)}) async-start(bf16[256,192,16]{0,2,1:T(8,128)(2,1)} %bitcast.57), calls=%async_computation.1 | async-start | bytes 3145728 | tf_op jit(solution)/shard_map/all_to_all | solution.py:50
  102.1 283.6 %reduce-scatter.3.cloned.1.call-start = ((), (), s32[]{:S(2)}) async-start(), calls=%async_computation.4 | async-start | bytes 2129920 | tf_op jit(solution)/shard_map/reduce_scatter | solution.py:57
  182.8 1.2 copy-start.1
  187.9 1.1 copy-start
  191.6 1.4 copy-start.2
  191.6 406.4 %reduce-scatter.5.cloned.1.call-start = ((), (), s32[]{:S(2)}) async-start(), calls=%async_computation.5 | async-start | bytes 1597440 | tf_op jit(solution)/shard_map/reduce_scatter | solution.py:41
Sparse Core Ops, SparseCore 0:
  191.8 193.9 reduce-scatter.2
  391.1 206.8 reduce-scatter.4
where the time goes:
time: 617 us; the launch traced here: 606 us
  waiting for transfers between devices  370 us (60%)
  blocking collectives  192 us (31%)
  between operations  14.2 us (2%)
  local copies, waits for them, and re-layouts  13.3 us (2%)
  matrix products  9.35 us (2%)
    reduce_scatter x1, waiting for transfers between devices, on_device(): lax.psum_scatter(jnp.einsum('toe,ton->eon', mixed_part, c3, preferred_ele...  211 us
    reduce_scatter x1, waiting for transfers between devices, on_device(): lax.psum_scatter(jnp.einsum('tir,tie->rie', x3, d_pre, preferred_element_...  160 us
    all_gather x1, blocking collectives, on_device(): lax.all_gather(w_out, 'dp', axis=0, tiled=True)  86.9 us
    all_gather x1, blocking collectives, on_device(): lax.all_gather(w_in, 'dp', axis=0, tiled=True)  80 us
    all_to_all x1, blocking collectives, on_device(): moved = lax.all_to_all(tiled, 'mp', split_axis=2, concat_axis=1, tiled=True)  25.2 us
  transfers between devices with their start and end apart: 3, of which 2 were waited for; matrix products, arithmetic and copies ran while one was open for 2% of the time, Pallas kernels for 0%

commit v1 on v0

v1 whole, which is shorter than its diff:
```python
import jax
import jax.numpy as jnp
from jax import lax
from jax.sharding import Mesh, PartitionSpec as P

BLK = 128
NB = 48
EXP = 512
TILES = 192

DP = ("x_hi", "z_hi", "z_lo", "core")
MP = ("x_lo", "y")
SIZES = (2, 4, 4, 2, 2, 4)


def gelu_tanh(value):
    return jax.nn.gelu(value, approximate=True)


def exchange(value, axis):
    return lax.all_to_all(value, axis, 0, 0, tiled=True)


def gather_weights(w_in, w_out):
    shard = jnp.concatenate(
        [w_in.transpose(1, 0, 2).reshape(48, 128), w_out.transpose(1, 0, 2).reshape(48, 128)]
    )
    along_z = lax.all_gather(shard, ("z_hi", "z_lo"), axis=0, tiled=False)
    halves = lax.all_gather(along_z, "x_hi", axis=0, tiled=False)
    full = lax.all_gather(halves, "core", axis=0, tiled=False)
    full = full.transpose(1, 2, 0, 3, 4).reshape(64, 96, 128)
    win = full[:, :48].reshape(64, 6, 2, 512).transpose(1, 0, 2, 3).reshape(6, 128, 512)
    wout = full[:, 48:].reshape(64, 6, 8, 128).transpose(1, 0, 2, 3).reshape(6, 512, 128)
    return win, wout


def scatter_sums(part_in, part_out):
    f32 = jnp.float32
    bf16 = jnp.bfloat16
    rows_in = part_in.reshape(6, 64, 2, 512).transpose(1, 0, 2, 3).reshape(64, 48, 128)
    rows_out = part_out.reshape(6, 64, 8, 128).transpose(1, 0, 2, 3).reshape(64, 48, 128)
    both = jnp.concatenate([rows_in, rows_out], axis=1).astype(bf16)
    both = both.reshape(2, 4, 4, 2, 96, 128).transpose(3, 0, 2, 1, 4, 5)
    got = exchange(both, "core")
    both = got.astype(f32).sum(axis=0).astype(bf16).reshape(8, 4, 96, 128)
    got = exchange(both, ("x_hi", "z_lo"))
    both = got.astype(f32).sum(axis=0).astype(bf16)
    got = exchange(both, "z_hi")
    total = got.astype(f32).sum(axis=0)
    grad_in = total[:48].reshape(6, 2, 512).transpose(1, 0, 2)
    grad_out = total[48:].reshape(6, 8, 128).transpose(1, 0, 2)
    return grad_in, grad_out


def on_device(tokens, w_in, w_out, cotangent):
    f32 = jnp.float32
    bf16 = jnp.bfloat16
    rows = tokens.shape[0]
    groups = 8
    nb_local = NB // groups
    tiles_local = nb_local * EXP // BLK
    piece_cols = BLK // groups
    x3 = tokens.reshape(rows, nb_local, BLK)
    c3 = cotangent.reshape(rows, nb_local, BLK)
    scale = 1.0 / jnp.sqrt(f32(rows * 64))
    win, wout = gather_weights(w_in, w_out)
    pre = jnp.einsum("tir,ire->tie", x3, win, preferred_element_type=f32)
    act = gelu_tanh(pre).astype(bf16)
    tiled = act.reshape(rows, tiles_local, BLK)
    moved = lax.all_to_all(tiled, MP, split_axis=2, concat_axis=1, tiled=True)
    mixed_part = moved.transpose(0, 2, 1).reshape(rows, nb_local, EXP)
    out_part = jnp.einsum("toe,oen->ton", mixed_part, wout, preferred_element_type=f32)
    output = out_part.astype(bf16).reshape(rows, nb_local * BLK)
    d_mixed = jnp.einsum("ton,oen->toe", c3, wout, preferred_element_type=f32).astype(bf16)
    part_out = jnp.einsum("toe,ton->oen", mixed_part, c3, preferred_element_type=f32)
    back_send = d_mixed.reshape(rows, piece_cols, TILES).transpose(0, 2, 1)
    back = lax.all_to_all(back_send, MP, split_axis=1, concat_axis=2, tiled=True)
    d_act = back.reshape(rows, nb_local, EXP)
    _, pull = jax.vjp(gelu_tanh, pre)
    d_pre = pull(d_act.astype(f32))[0].astype(bf16)
    grad_x = jnp.einsum("tie,ire->tir", d_pre, win, preferred_element_type=f32)
    grad_tokens = grad_x.astype(bf16).reshape(rows, nb_local * BLK)
    part_in = jnp.einsum("tir,tie->ire", x3, d_pre, preferred_element_type=f32)
    grad_in, grad_out = scatter_sums(part_in * scale, part_out * scale)
    return (output, grad_tokens, grad_in, grad_out)


def solution(mesh):
    fine = Mesh(mesh.devices.reshape(SIZES), DP + MP)
    placed = (P(DP, MP), P(DP, MP, None), P(DP, MP, None), P(DP, MP))
    return jax.shard_map(
        on_device,
        mesh=fine,
        in_specs=placed,
        out_specs=(P(DP, MP), P(DP, MP), P(DP, MP, None), P(DP, MP, None)),
        check_vma=False,
    )
```

time: 617 us -> 210 us (0.34); the launches traced: 606 us -> 208 us
  waiting for transfers between devices: 370 us -> 58.5 us
  blocking collectives: 192 us -> 74.3 us
  local copies, waits for them, and re-layouts: 13.3 us -> 28.7 us
  starting transfers between devices: 4.3 us -> 17.2 us
    reduce_scatter x2 -> x0, waiting for transfers between devices: 370 us -> none  [the longest x1 211 us: on_device(): lax.psum_scatter(jnp.einsum('toe,ton->eon', mixed_part, c3, preferred_ele...]
    all_gather x2, blocking collectives: 167 us -> 40 us  [the longest x1 31.1 us: gather_weights(): along_z = lax.all_gather(shard, ('z_hi', 'z_lo'), axis=0, tiled=False)]
    all_to_all x1 -> x3, waiting for transfers between devices: 0.01 us -> 32.2 us  [the longest x1 14 us: on_device(): lax.all_to_all(back_send, MP, split_axis=1, concat_axis=2, tiled=True)]
    all_gather x0 -> x1, waiting for transfers between devices: none -> 26.2 us  [gather_weights(): full = lax.all_gather(halves, 'core', axis=0, tiled=False)]
    all_to_all x1 -> x3, starting transfers between devices: 4.22 us -> 17.1 us  [the longest x1 9.21 us: exchange(): return lax.all_to_all(value, axis, 0, 0, tiled=True)]
    reshape x0 -> x6, local copies, waits for them, and re-layouts: none -> 9.27 us  [the longest x2 4.27 us: gather_weights(): full[:, :48].reshape(64, 6, 2, 512).transpose(1, 0, 2, 3)]
    all_to_all x1 -> x2, blocking collectives: 25.2 us -> 34.4 us  [exchange(): return lax.all_to_all(value, axis, 0, 0, tiled=True)]
  transfers between devices with their start and end apart: 3 -> 4, of which waited for: 2 -> 4; matrix products, arithmetic and copies ran while one was open for 2% -> 10% of each run, Pallas kernels for 0% -> 0%
where the time goes in v1:
time: 210 us; the launch traced here: 208 us
  blocking collectives  74.3 us (35%)
  waiting for transfers between devices  58.5 us (28%)
  local copies, waits for them, and re-layouts  28.7 us (14%)
  starting transfers between devices  17.2 us (8%)
  between operations  14.2 us (7%)
  matrix products  11.2 us (5%)
  other arithmetic  3.81 us (2%)
    all_to_all x2, blocking collectives, exchange(): return lax.all_to_all(value, axis, 0, 0, tiled=True)  34.4 us
    all_gather x1, blocking collectives, gather_weights(): along_z = lax.all_gather(shard, ('z_hi', 'z_lo'), axis=0, tiled=False)  31.1 us
    all_gather x1, waiting for transfers between devices, gather_weights(): full = lax.all_gather(halves, 'core', axis=0, tiled=False)  26.2 us
    all_to_all x1, waiting for transfers between devices, on_device(): lax.all_to_all(back_send, MP, split_axis=1, concat_axis=2, tiled=True)  14 us
    all_to_all x1, waiting for transfers between devices, on_device(): moved = lax.all_to_all(tiled, MP, split_axis=2, concat_axis=1, tiled=True)  10.7 us
    all_to_all x1, starting transfers between devices, exchange(): return lax.all_to_all(value, axis, 0, 0, tiled=True)  9.21 us
    all_gather x1, blocking collectives, gather_weights(): halves = lax.all_gather(along_z, 'x_hi', axis=0, tiled=False)  8.9 us
    all_to_all x1, waiting for transfers between devices, exchange(): return lax.all_to_all(value, axis, 0, 0, tiled=True)  7.58 us
  transfers between devices with their start and end apart: 4, of which 4 were waited for; matrix products, arithmetic and copies ran while one was open for 10% of the time, Pallas kernels for 0%

profile of v1, /device:TPU:1, one launch (start us, length us, event | category | flops | bytes accessed | tf_op | source)
XLA Modules:
  0.0 208.0 jit_solution(10251815962299788318)
XLA Ops:
  7.2 0.0 copy-start.4
  7.2 0.0 all-gather.5.cloned.1.call-start
  7.2 0.8 reshape.82
  8.0 0.7 pad_maximum_fusion
  8.7 31.1 %all-gather = bf16[1536,128]{1,0:T(8,128)(2,1)S(1)} all-gather(bf16[96,128]{1,0:T(8,128)(2,1)S(1)} %pad_maximum_fusion), channel_id=2, replica_groups=mesh['x_hi'=2,'z_hi'=4,'z_lo'=4,'core'=2,'x_lo'=2,'y'=4] {'z_hi','z_lo'}, dimensions={0}, use_global_device_ids=true | all-gather | bytes 417792 | tf_op jit(solution)/shard_map/all_gather | solution.py:28
  39.8 8.9 %all-gather.1 = bf16[32,96,128]{2,1,0:T(8,128)(2,1)} all-gather(bf16[16,96,128]{2,1,0:T(8,128)(2,1)S(1)} %bitcast.109), channel_id=3, replica_groups=mesh['x_hi'=2,'z_hi'=4,'z_lo'=4,'core'=2,'x_lo'=2,'y'=4] {'x_hi'}, dimensions={0}, use_global_device_ids=true | all-gather | bytes 1179648 | tf_op jit(solution)/shard_map/all_gather | solution.py:29
  48.7 0.0 all-gather.5.cloned.1.call-update
  48.7 0.0 copy-done.4
  48.7 0.2 copy.131
  48.9 26.2 %all-gather.5.cloned.1.call-done = bf16[4,16,96,128]{3,2,1,0:T(8,128)(2,1)} async-done(((bf16[2,16,96,128]{3,2,1,0:T(8,128)(2,1)}), bf16[4,16,96,128]{3,2,1,0:T(8,128)(2,1)}) %all-gather.5.cloned.1.call-update) | async-done | bytes 1572880 | tf_op jit(solution)/shard_map/all_gather | solution.py:30
  75.1 1.6 copy.119
  76.7 1.0 slice_bitcast_fusion
  77.7 0.6 convolution_convert_fusion
  78.2 2.0 copy.168
  80.3 0.0 copy-start.5
  80.3 4.0 %all-to-all-start.1 = ((bf16[256,192,16]{0,2,1:T(8,128)(2,1)}), bf16[256,192,16]{0,2,1:T(8,128)(2,1)S(1)}, u32[]{:S(2)}, u32[]{:S(2)}) async-start(bf16[256,192,16]{0,2,1:T(8,128)(2,1)} %bitcast.89), calls=%async_computation.1 | async-start | bytes 3145728 | tf_op jit(solution)/shard_map/all_to_all | solution.py:77
  84.3 0.0 copy-done.5
  84.3 0.9 copy.122
  85.3 2.0 reshape.87
  87.3 1.4 copy.121
  88.7 2.3 %reshape.88 = bf16[6,128,512]{2,1,0:T(8,128)(2,1)S(1)} reshape(bf16[6,64,2,512]{3,2,1,0:T(2,128)(2,1)} %copy.121) | data formatting | bytes 1572864 | tf_op jit(solution)/shard_map/reshape | solution.py:32
  91.0 0.0 copy-start
  91.0 14.0 %all-to-all-done.1 = bf16[256,192,16]{0,2,1:T(8,128)(2,1)S(1)} async-done(((bf16[256,192,16]{0,2,1:T(8,128)(2,1)}), bf16[256,192,16]{0,2,1:T(8,128)(2,1)S(1)}, u32[]{:S(2)}, u32[]{:S(2)}) %all-to-all-start.1) | async-done | bytes 1572896 | tf_op jit(solution)/shard_map/all_to_all | solution.py:77
  104.9 0.4 convert_bitcast_fusion
  105.4 0.0 copy-start.2
  105.4 0.4 copy.134
  105.8 0.0 copy-done
  105.8 0.5 copy-done.2
  106.4 3.7 %fusion.6 = (bf16[256,6,512]{0,2,1:T(8,128)(2,1)}, bf16[256,6,512]{0,2,1:T(8,128)(2,1)S(1)}) fusion(f32[256,6,512]{0,2,1:T(8,128)S(1)} %bitcast.100, bf16[6,128,512]{2,1,0:T(8,128)(2,1)S(1)} %reshape.88, bf16[256,6,128]{0,2,1:T(8,128)(2,1)S(1)} %bitcast.110), kind=kOutput, calls=%fused_computation.8 | convolution fusion | flops 218628096 | bytes 7471104 | tf_op jit(solution)/shard_map/tir,ire->tie/dot_general | solution.py:67
  110.1 2.0 copy.125
  112.1 0.0 copy-start.3
  112.1 3.9 %all-to-all-start = ((bf16[256,24,128]{0,1,2:T(8,128)(2,1)}), bf16[256,24,128]{0,1,2:T(8,128)(2,1)S(1)}, u32[]{:S(2)}, u32[]{:S(2)}) async-start(bf16[256,24,128]{0,1,2:T(8,128)(2,1)} %copy.125), calls=%async_computation | async-start | bytes 3145728 | tf_op jit(solution)/shard_map/all_to_all | solution.py:70
  116.0 0.0 copy-done.3
  116.0 2.9 %fusion.10 = bf16[6,128,512]{2,1,0:T(8,128)(2,1)} fusion(bf16[256,6,512]{0,2,1:T(8,128)(2,1)} %get-tuple-element.28, bf16[256,6,128]{0,2,1:T(8,128)(2,1)S(1)} %bitcast.111), kind=kOutput, calls=%fused_computation.20 | convolution fusion | flops 202113024 | bytes 2752512 | tf_op jit(solution)/shard_map/tir,tie->ire/dot_general | solution.py:83
  118.9 2.1 %reshape.96 = bf16[6,64,2,512]{3,2,1,0:T(2,128)(2,1)S(1)} reshape(bf16[6,128,512]{2,1,0:T(8,128)(2,1)} %fusion.10) | data formatting | bytes 1572864 | tf_op jit(solution)/shard_map/reshape | solution.py:40
  121.1 1.5 copy.169
  122.6 3.1 %concatenate.13 = bf16[2,4,4,2,48,128]{5,4,3,2,1,0:T(8,128)(2,1)} reshape(bf16[64,6,2,512]{3,2,1,0:T(2,128)(2,1)} %bitcast.103) | data formatting | bytes 1572864 | tf_op jit(solution)/shard_map/concatenate | solution.py:42
  125.7 10.7 %all-to-all-done = bf16[256,24,128]{0,1,2:T(8,128)(2,1)S(1)} async-done(((bf16[256,24,128]{0,1,2:T(8,128)(2,1)}), bf16[256,24,128]{0,1,2:T(8,128)(2,1)S(1)}, u32[]{:S(2)}, u32[]{:S(2)}) %all-to-all-start) | async-done | bytes 1572896 | tf_op jit(solution)/shard_map/all_to_all | solution.py:70
  136.4 0.3 copy.127
  136.8 0.6 copy.128
  137.3 1.5 multiply_convert_fusion
  138.8 1.5 copy.140
  140.4 0.0 copy-start.1
  140.4 0.1 copy.141
  140.5 1.0 copy-done.1
  141.5 0.2 maximum_bitcast_fusion
  141.7 0.2 copy.142
  141.8 6.3 %all_to_all.42 = bf16[2,2,4,4,96,128]{5,4,2,3,1,0:T(8,128)(2,1)} all-to-all(bf16[2,2,4,4,96,128]{5,4,2,3,1,0:T(8,128)(2,1)S(1)} %copy.142), channel_id=1, replica_groups=mesh['x_hi'=2,'z_hi'=4,'z_lo'=4,'core'=2,'x_lo'=2,'y'=4] {'core'}, dimensions={0} | all-to-all | bytes 3145728 | tf_op jit(solution)/shard_map/all_to_all | solution.py:21
  148.1 1.7 reduce_sum.33
  149.9 0.1 copy.144
  149.9 28.1 %all_to_all.43 = bf16[8,4,96,128]{3,2,1,0:T(8,128)(2,1)S(1)} all-to-all(bf16[8,4,96,128]{3,2,1,0:T(8,128)(2,1)S(1)} %bitcast.105), channel_id=1, replica_groups=mesh['x_hi'=2,'z_hi'=4,'z_lo'=4,'core'=2,'x_lo'=2,'y'=4] {'x_hi','z_lo'}, dimensions={0} | all-to-all | bytes 1572864 | tf_op jit(solution)/shard_map/all_to_all | solution.py:21
  178.0 0.7 reduce_sum.34
  178.8 9.2 %all-to-all-start.4 = ((bf16[4,96,128]{2,1,0:T(8,128)(2,1)}), bf16[4,96,128]{2,1,0:T(8,128)(2,1)S(1)}, u32[]{:S(2)}, u32[]{:S(2)}) async-start(bf16[4,96,128]{2,1,0:T(8,128)(2,1)} %reduce_sum.34), calls=%async_computation.4 | async-start | bytes 196608 | tf_op jit(solution)/shard_map/all_to_all | solution.py:21
  188.0 2.0 convolution_convert_fusion.1
  190.0 0.9 copy.146
  190.9 0.4 convolution_convert_fusion.2
  191.4 0.9 copy.145
  192.3 7.6 %all-to-all-done.4 = bf16[4,96,128]{2,1,0:T(8,128)(2,1)S(1)} async-done(((bf16[4,96,128]{2,1,0:T(8,128)(2,1)}), bf16[4,96,128]{2,1,0:T(8,128)(2,1)S(1)}, u32[]{:S(2)}, u32[]{:S(2)}) %all-to-all-start.4) | async-done | bytes 98336 | tf_op jit(solution)/shard_map/all_to_all | solution.py:21
  199.9 0.6 slice_bitcast_fusion.1
  200.5 0.6 reshape.99
  (1 shorter events, 0.0 us)
Async XLA Ops:
  7.2 41.5 %copy-start.4 = (bf16[256,768]{1,0:T(8,128)(2,1)S(1)}, bf16[256,768]{1,0:T(8,128)(2,1)}, u32[]{:S(2)}) copy-start(bf16[256,768]{1,0:T(8,128)(2,1)} %param.7) | copy-start | bytes 1179652
  7.2 67.9 %all-gather.5.cloned.1.call-start = ((), (), s32[]{:S(2)}) async-start(), calls=%async_computation.5 | async-start | bytes 2359296 | tf_op jit(solution)/shard_map/all_gather | solution.py:30
  80.3 4.1 %copy-start.5 = (bf16[256,768]{1,0:T(8,128)(2,1)S(1)}, bf16[256,768]{1,0:T(8,128)(2,1)}, u32[]{:S(2)}) copy-start(bf16[256,768]{1,0:T(8,128)(2,1)} %param.4) | copy-start | bytes 1179652
  80.3 24.6 %all-to-all-start.1 = ((bf16[256,192,16]{0,2,1:T(8,128)(2,1)}), bf16[256,192,16]{0,2,1:T(8,128)(2,1)S(1)}, u32[]{:S(2)}, u32[]{:S(2)}) async-start(bf16[256,192,16]{0,2,1:T(8,128)(2,1)} %bitcast.89), calls=%async_computation.1 | async-start | bytes 3145728 | tf_op jit(solution)/shard_map/all_to_all | solution.py:77
  91.0 14.8 %copy-start = (bf16[6,128,512]{2,1,0:T(8,128)(2,1)}, bf16[6,128,512]{2,1,0:T(8,128)(2,1)S(1)}, u32[]{:S(2)}) copy-start(bf16[6,128,512]{2,1,0:T(8,128)(2,1)S(1)} %reshape.88) | copy-start | bytes 2359300
  105.4 1.0 copy-start.2
  112.1 3.9 %copy-start.3 = (bf16[256,768]{0,1:T(8,128)(2,1)S(1)}, bf16[256,768]{0,1:T(8,128)(2,1)}, u32[]{:S(2)}) copy-start(bf16[256,768]{0,1:T(8,128)(2,1)} %copy.122) | copy-start | bytes 1179652
  112.1 24.3 %all-to-all-start = ((bf16[256,24,128]{0,1,2:T(8,128)(2,1)}), bf16[256,24,128]{0,1,2:T(8,128)(2,1)S(1)}, u32[]{:S(2)}, u32[]{:S(2)}) async-start(bf16[256,24,128]{0,1,2:T(8,128)(2,1)} %copy.125), calls=%async_computation | async-start | bytes 3145728 | tf_op jit(solution)/shard_map/all_to_all | solution.py:70
  140.4 1.1 copy-start.1
  178.8 21.1 %all-to-all-start.4 = ((bf16[4,96,128]{2,1,0:T(8,128)(2,1)}), bf16[4,96,128]{2,1,0:T(8,128)(2,1)S(1)}, u32[]{:S(2)}, u32[]{:S(2)}) async-start(bf16[4,96,128]{2,1,0:T(8,128)(2,1)} %reduce_sum.34), calls=%async_computation.4 | async-start | bytes 196608 | tf_op jit(solution)/shard_map/all_to_all | solution.py:21
Sparse Core Ops, SparseCore 0:
  48.8 26.2 all-gather.4

commit v2 on v1

v2 whole, which is shorter than its diff:
```python
import jax
import jax.numpy as jnp
from jax import lax
from jax.sharding import Mesh, PartitionSpec as P

BLK = 128
NB = 48
EXP = 512
TILES = 192

DP = ("x_hi", "z_hi", "z_lo", "core")
MP = ("x_lo", "y")
SIZES = (2, 4, 4, 2, 2, 4)


def gelu_tanh(value):
    return jax.nn.gelu(value, approximate=True)


def exchange(value, axis):
    return lax.all_to_all(value, axis, 0, 0, tiled=True)


def gather_weights(w_in, w_out):
    shard = jnp.concatenate(
        [w_in.transpose(1, 0, 2).reshape(48, 128), w_out.transpose(1, 0, 2).reshape(48, 128)]
    )
    along_z = lax.all_gather(shard, ("z_hi", "z_lo"), axis=0, tiled=False)
    halves = lax.all_gather(along_z, "x_hi", axis=0, tiled=False).reshape(1, 32, 96, 128)
    full = exchange(jnp.broadcast_to(halves, (2, 32, 96, 128)), "core")
    full = full.transpose(1, 0, 2, 3).reshape(64, 96, 128)
    win = full[:, :48].reshape(64, 6, 2, 512).transpose(1, 0, 2, 3).reshape(6, 128, 512)
    wout = full[:, 48:].reshape(64, 6, 8, 128).transpose(1, 0, 2, 3).reshape(6, 512, 128)
    return win, wout


def half_sum(part, keep):
    cols = part.shape[2]
    both = part.astype(jnp.bfloat16).reshape(6, 2, 4, 4, 2, keep, cols)
    both = both.transpose(4, 1, 3, 2, 0, 5, 6).reshape(2, 32, 48, 128)
    got = exchange(both, "core")
    return got.astype(jnp.float32).sum(axis=0).astype(jnp.bfloat16)


def scatter_sums(half_in, half_out):
    f32 = jnp.float32
    both = jnp.concatenate([half_in, half_out], axis=1).reshape(8, 4, 96, 128)
    got = exchange(both, ("x_hi", "z_lo"))
    both = got.astype(f32).sum(axis=0).astype(jnp.bfloat16)
    got = exchange(both, "z_hi")
    total = got.astype(f32).sum(axis=0)
    grad_in = total[:48].reshape(6, 2, 512).transpose(1, 0, 2)
    grad_out = total[48:].reshape(6, 8, 128).transpose(1, 0, 2)
    return grad_in, grad_out


def on_device(tokens, w_in, w_out, cotangent):
    f32 = jnp.float32
    bf16 = jnp.bfloat16
    rows = tokens.shape[0]
    groups = 8
    nb_local = NB // groups
    tiles_local = nb_local * EXP // BLK
    piece_cols = BLK // groups
    x3 = tokens.reshape(rows, nb_local, BLK)
    c3 = cotangent.reshape(rows, nb_local, BLK)
    scale = 1.0 / jnp.sqrt(f32(rows * 64))
    win, wout = gather_weights(w_in, w_out)
    d_mixed = jnp.einsum("ton,oen->toe", c3, wout, preferred_element_type=f32).astype(bf16)
    back_send = d_mixed.reshape(rows, piece_cols, TILES).transpose(0, 2, 1)
    back = lax.all_to_all(back_send, MP, split_axis=1, concat_axis=2, tiled=True)
    pre = jnp.einsum("tir,ire->tie", x3, win, preferred_element_type=f32)
    act = gelu_tanh(pre).astype(bf16)
    act, pre = lax.optimization_barrier((act, pre))
    tiled = act.reshape(rows, tiles_local, BLK)
    moved = lax.all_to_all(tiled, MP, split_axis=2, concat_axis=1, tiled=True)
    d_act = back.reshape(rows, nb_local, EXP)
    _, pull = jax.vjp(gelu_tanh, pre)
    d_pre = pull(d_act.astype(f32))[0].astype(bf16)
    part_in = jnp.einsum("tir,tie->ire", x3, d_pre, preferred_element_type=f32)
    half_in = half_sum(part_in * scale, 2)
    mixed_part = moved.transpose(0, 2, 1).reshape(rows, nb_local, EXP)
    part_out = jnp.einsum("toe,ton->oen", mixed_part, c3, preferred_element_type=f32)
    half_out = half_sum(part_out * scale, 8)
    grad_in, grad_out = scatter_sums(half_in, half_out)
    grad_x = jnp.einsum("tie,ire->tir", d_pre, win, preferred_element_type=f32)
    grad_tokens = grad_x.astype(bf16).reshape(rows, nb_local * BLK)
    out_part = jnp.einsum("toe,oen->ton", mixed_part, wout, preferred_element_type=f32)
    output = out_part.astype(bf16).reshape(rows, nb_local * BLK)
    return (output, grad_tokens, grad_in, grad_out)


def solution(mesh):
    fine = Mesh(mesh.devices.reshape(SIZES), DP + MP)
    placed = (P(DP, MP), P(DP, MP, None), P(DP, MP, None), P(DP, MP))
    return jax.shard_map(
        on_device,
        mesh=fine,
        in_specs=placed,
        out_specs=(P(DP, MP), P(DP, MP), P(DP, MP, None), P(DP, MP, None)),
        check_vma=False,
    )
```

time: 210 us -> 186 us (0.89)
  waiting for transfers between devices: 58.5 us -> 28.8 us
  starting transfers between devices: 17.2 us -> 38.7 us
  between operations: 14.2 us -> 0.82 us
  blocking collectives: 74.3 us -> 65.3 us
  other arithmetic: 3.81 us -> 11.9 us
    all_gather x1 -> x0, waiting for transfers between devices: 26.2 us -> none  [gather_weights(): full = lax.all_gather(halves, 'core', axis=0, tiled=False)]
    all_to_all x1 -> x4, starting transfers between devices: 9.21 us -> 29.3 us  [exchange(): return lax.all_to_all(value, axis, 0, 0, tiled=True)]
    all_to_all x2 -> x1, blocking collectives: 34.4 us -> 25.3 us  [exchange(): return lax.all_to_all(value, axis, 0, 0, tiled=True)]
    all_to_all x1, waiting for transfers between devices: 14 us -> 7.76 us  [on_device(): lax.all_to_all(back_send, MP, split_axis=1, concat_axis=2, tiled=True)]
    convert_element_type x1 -> x2, other arithmetic: 0.42 us -> 3.96 us  [on_device(): d_pre = pull(d_act.astype(f32))[0].astype(bf16)]
    concatenate x1 -> x0, local copies, waits for them, and re-layouts: 3.15 us -> none  [scatter_sums(): both = jnp.concatenate([rows_in, rows_out], axis=1).astype(bf16)]
    reduce_sum x2 -> x3, other arithmetic: 2.48 us -> 5.31 us  [the longest x2 3.4 us: half_sum(): return got.astype(jnp.float32).sum(axis=0).astype(jnp.bfloat16)]
    convert_element_type x0 -> x1, local copies, waits for them, and re-layouts: none -> 2.32 us  [half_sum(): both = part.astype(jnp.bfloat16).reshape(6, 2, 4, 4, 2, keep, cols)]
  transfers between devices with their start and end apart: 4 -> 6, of which waited for: 4 -> 5; matrix products, arithmetic and copies ran while one was open for 10% -> 19% of each run, Pallas kernels for 0% -> 0%
where the time goes in v2:
time: 186 us; the launch traced here: 184 us
  blocking collectives  65.3 us (35%)
  starting transfers between devices  38.7 us (21%)
  waiting for transfers between devices  28.8 us (15%)
  local copies, waits for them, and re-layouts  28.4 us (15%)
  other arithmetic  11.9 us (6%)
  matrix products  9.89 us (5%)
    all_gather x1, blocking collectives, gather_weights(): along_z = lax.all_gather(shard, ('z_hi', 'z_lo'), axis=0, tiled=False)  31.1 us
    all_to_all x4, starting transfers between devices, exchange(): return lax.all_to_all(value, axis, 0, 0, tiled=True)  29.3 us
    all_to_all x1, blocking collectives, exchange(): return lax.all_to_all(value, axis, 0, 0, tiled=True)  25.3 us
    all_to_all x1, waiting for transfers between devices, on_device(): moved = lax.all_to_all(tiled, MP, split_axis=2, concat_axis=1, tiled=True)  11.6 us
    all_to_all x4, waiting for transfers between devices, exchange(): return lax.all_to_all(value, axis, 0, 0, tiled=True)  9.42 us
    all_gather x1, blocking collectives, gather_weights(): lax.all_gather(along_z, 'x_hi', axis=0, tiled=False).reshape(1, 32, 96, 128)  8.93 us
    all_to_all x1, waiting for transfers between devices, on_device(): lax.all_to_all(back_send, MP, split_axis=1, concat_axis=2, tiled=True)  7.76 us
    all_to_all x1, starting transfers between devices, on_device(): lax.all_to_all(back_send, MP, split_axis=1, concat_axis=2, tiled=True)  5.12 us
  transfers between devices with their start and end apart: 6, of which 5 were waited for; matrix products, arithmetic and copies ran while one was open for 19% of the time, Pallas kernels for 0%

profile of v2, /device:TPU:1, one launch (start us, length us, event | category | flops | bytes accessed | tf_op | source)
XLA Modules:
  0.0 183.9 jit_solution(8060508632477617522)
XLA Ops:
  0.6 0.7 reshape.79
  1.4 0.7 pad_maximum_fusion.1
  2.1 31.1 %all-gather = bf16[1536,128]{1,0:T(8,128)(2,1)S(1)} all-gather(bf16[96,128]{1,0:T(8,128)(2,1)S(1)} %pad_maximum_fusion.1), channel_id=2, replica_groups=mesh['x_hi'=2,'z_hi'=4,'z_lo'=4,'core'=2,'x_lo'=2,'y'=4] {'z_hi','z_lo'}, dimensions={0}, use_global_device_ids=true | all-gather | bytes 417792 | tf_op jit(solution)/shard_map/all_gather | solution.py:28
  33.1 0.0 copy-start.5
  33.2 8.9 %all-gather.1 = bf16[32,96,128]{2,1,0:T(8,128)(2,1)S(1)} all-gather(bf16[16,96,128]{2,1,0:T(8,128)(2,1)S(1)} %bitcast.87), channel_id=3, replica_groups=mesh['x_hi'=2,'z_hi'=4,'z_lo'=4,'core'=2,'x_lo'=2,'y'=4] {'x_hi'}, dimensions={0}, use_global_device_ids=true | all-gather | bytes 1179648 | tf_op jit(solution)/shard_map/all_gather | solution.py:29
  42.1 1.4 broadcast_in_dim.8
  43.4 12.9 %all-to-all-start = ((bf16[2,32,96,128]{3,2,1,0:T(8,128)(2,1)}), bf16[2,32,96,128]{3,2,1,0:T(8,128)(2,1)S(1)}, u32[]{:S(2)}, u32[]{:S(2)}) async-start(bf16[2,32,96,128]{3,2,1,0:T(8,128)(2,1)} %broadcast_in_dim.8), calls=%async_computation | async-start | bytes 3145728 | tf_op jit(solution)/shard_map/all_to_all | solution.py:21
  56.3 0.0 copy-done.5
  56.3 0.2 copy.100
  56.5 1.9 %all-to-all-done = bf16[2,32,96,128]{3,2,1,0:T(8,128)(2,1)S(1)} async-done(((bf16[2,32,96,128]{3,2,1,0:T(8,128)(2,1)}), bf16[2,32,96,128]{3,2,1,0:T(8,128)(2,1)S(1)}, u32[]{:S(2)}, u32[]{:S(2)}) %all-to-all-start) | async-done | bytes 1572896 | tf_op jit(solution)/shard_map/all_to_all | solution.py:21
  58.5 0.2 copy.88
  58.7 1.0 slice_bitcast_fusion
  59.7 0.0 copy-start
  59.7 0.6 convolution_convert_fusion
  60.3 0.0 copy-start.6
  60.3 2.1 %copy.133 = bf16[256,16,192]{0,1,2:T(8,128)(2,1)} copy(bf16[256,16,192]{0,2,1:T(8,128)(2,1)S(1)} %bitcast.78) | data formatting | bytes 3145728 | tf_op jit(solution)/shard_map/reshape | solution.py:70
  62.3 5.1 %all-to-all-start.2 = ((bf16[256,192,16]{0,2,1:T(8,128)(2,1)}), bf16[256,192,16]{0,2,1:T(8,128)(2,1)S(1)}, u32[]{:S(2)}, u32[]{:S(2)}) async-start(bf16[256,192,16]{0,2,1:T(8,128)(2,1)} %bitcast.70), calls=%async_computation.2 | async-start | bytes 3145728 | tf_op jit(solution)/shard_map/all_to_all | solution.py:71
  67.4 0.0 copy-done.6
  67.4 0.9 copy.91
  68.4 2.0 %reshape.84 = bf16[64,6,2,512]{3,2,1,0:T(2,128)(2,1)S(1)} reshape(bf16[64,48,128]{2,1,0:T(8,128)(2,1)} %get-tuple-element.29) | data formatting | bytes 1572864 | tf_op jit(solution)/shard_map/reshape | solution.py:32
  70.4 1.4 copy.90
  71.8 2.3 %reshape.85 = bf16[6,128,512]{2,1,0:T(8,128)(2,1)S(1)} reshape(bf16[6,64,2,512]{3,2,1,0:T(2,128)(2,1)} %copy.90) | data formatting | bytes 1572864 | tf_op jit(solution)/shard_map/reshape | solution.py:32
  74.1 0.0 copy-start.2
  74.1 4.1 %fusion.14 = (bf16[256,6,512]{0,2,1:T(8,128)(2,1)S(1)}, f32[256,6,512]{0,2,1:T(8,128)}) fusion(bf16[6,128,512]{2,1,0:T(8,128)(2,1)S(1)} %reshape.85, bf16[256,6,128]{0,2,1:T(8,128)(2,1)} %bitcast.88), kind=kOutput, calls=%fused_computation.17 | convolution fusion | flops 208404480 | bytes 5898240 | tf_op jit(solution)/shard_map/tir,ire->tie/dot_general | solution.py:72
  78.2 0.0 copy-done
  78.2 0.0 copy-done.2
  78.2 2.0 %copy.94 = bf16[256,24,128]{0,1,2:T(8,128)(2,1)} copy(bf16[256,24,128]{0,2,1:T(8,128)(2,1)S(1)} %bitcast.86) | data formatting | bytes 3145728 | tf_op jit(solution)/shard_map/reshape | solution.py:75
  80.2 7.8 %all-to-all-done.2 = bf16[256,192,16]{0,2,1:T(8,128)(2,1)S(1)} async-done(((bf16[256,192,16]{0,2,1:T(8,128)(2,1)}), bf16[256,192,16]{0,2,1:T(8,128)(2,1)S(1)}, u32[]{:S(2)}, u32[]{:S(2)}) %all-to-all-start.2) | async-done | bytes 1572896 | tf_op jit(solution)/shard_map/all_to_all | solution.py:71
  88.0 4.3 %all-to-all-start.1 = ((bf16[256,24,128]{0,1,2:T(8,128)(2,1)}), bf16[256,24,128]{0,1,2:T(8,128)(2,1)}, u32[]{:S(2)}, u32[]{:S(2)}) async-start(bf16[256,24,128]{0,1,2:T(8,128)(2,1)} %copy.94), calls=%async_computation.1 | async-start | bytes 3145728 | tf_op jit(solution)/shard_map/all_to_all | solution.py:76
  92.3 0.0 copy-done.1
  92.3 1.8 convert_bitcast_fusion
  94.2 0.0 copy-start.3
  94.2 0.3 copy.103
  94.5 1.5 copy-done.3
  96.1 2.1 %fusion.6 = bf16[256,6,512]{0,2,1:T(8,128)(2,1)S(1)} fusion(f32[256,6,512]{0,2,1:T(8,128)S(1)} %copy-done.3, f32[256,6,512]{0,2,1:T(8,128)S(1)} %bitcast.74), kind=kLoop, calls=%fused_computation.9 | loop fusion | flops 15728640 | bytes 7864320 | tf_op jit(solution)/shard_map/convert_element_type | solution.py:79
  98.2 0.0 copy-done.4
  98.2 0.6 fusion.15
  98.9 0.3 reshape.93
  99.2 0.7 copy.134
  99.9 1.4 reshape.94
  101.3 11.6 %all-to-all-done.1 = bf16[256,24,128]{0,1,2:T(8,128)(2,1)} async-done(((bf16[256,24,128]{0,1,2:T(8,128)(2,1)}), bf16[256,24,128]{0,1,2:T(8,128)(2,1)}, u32[]{:S(2)}, u32[]{:S(2)}) %all-to-all-start.1) | async-done | bytes 1572896 | tf_op jit(solution)/shard_map/all_to_all | solution.py:76
  112.9 5.1 %all-to-all-start.3 = ((bf16[2,32,48,128]{3,2,1,0:T(8,128)(2,1)}), bf16[2,32,48,128]{3,2,1,0:T(8,128)(2,1)}, u32[]{:S(2)}, u32[]{:S(2)}) async-start(bf16[2,32,48,128]{3,2,1,0:T(8,128)(2,1)} %reshape.94), calls=%async_computation.3 | async-start | bytes 1572864 | tf_op jit(solution)/shard_map/all_to_all | solution.py:21
  118.0 1.7 copy.96
  119.8 0.6 copy.97
  120.3 1.5 multiply_convert_fusion
  121.8 2.3 %copy.109 = bf16[6,512,128]{2,1,0:T(8,128)(2,1)} copy(bf16[6,512,128]{1,2,0:T(8,128)(2,1)} %multiply_convert_fusion) | data formatting | bytes 1572864 | tf_op jit(solution)/shard_map/convert_element_type | solution.py:39
  124.2 2.2 %copy.110 = bf16[2,2,4,4,6,8,128]{6,5,4,3,2,1,0:T(8,128)(2,1)} copy(bf16[2,2,4,4,6,8,128]{6,5,0,2,3,1,4:T(8,128)(2,1)} %bitcast.85) | data formatting | bytes 1572864 | tf_op jit(solution)/shard_map/transpose | solution.py:40
  126.4 0.0 all-to-all-done.3
  126.4 4.5 %all-to-all-start.4 = ((bf16[2,32,48,128]{3,2,1,0:T(8,128)(2,1)}), bf16[2,32,48,128]{3,2,1,0:T(8,128)(2,1)}, u32[]{:S(2)}, u32[]{:S(2)}) async-start(bf16[2,32,48,128]{3,2,1,0:T(8,128)(2,1)} %bitcast.81), calls=%async_computation.4 | async-start | bytes 1572864 | tf_op jit(solution)/shard_map/all_to_all | solution.py:21
  130.9 1.3 reduce_sum.45
  132.2 0.4 all-to-all-done.4
  132.6 2.1 %reduce_sum.46 = bf16[32,48,128]{2,1,0:T(8,128)(2,1)} reduce(bf16[2,32,48,128]{3,2,1,0:T(8,128)(2,1)} %all-to-all-done.4, bf16[]{:T(256)} %constant.19.clone.1), dimensions={0}, to_apply=%region_1.0 | reduce | flops 196608 | bytes 1179650 | tf_op jit(solution)/shard_map/reduce_sum | solution.py:42
  134.7 1.0 pad_maximum_fusion
  135.7 25.3 %all_to_all.52 = bf16[8,4,96,128]{3,2,1,0:T(8,128)(2,1)} all-to-all(bf16[8,4,96,128]{3,2,1,0:T(8,128)(2,1)S(1)} %bitcast.82), channel_id=1, replica_groups=mesh['x_hi'=2,'z_hi'=4,'z_lo'=4,'core'=2,'x_lo'=2,'y'=4] {'x_hi','z_lo'}, dimensions={0} | all-to-all | bytes 1572864 | tf_op jit(solution)/shard_map/all_to_all | solution.py:21
  161.0 1.9 %reduce_sum.47 = bf16[4,96,128]{2,1,0:T(8,128)(2,1)} reduce(bf16[8,4,96,128]{3,2,1,0:T(8,128)(2,1)} %all_to_all.52, bf16[]{:T(256)} %constant.19.clone.1), dimensions={0}, to_apply=%region_2.0 | reduce | flops 344064 | bytes 884738 | tf_op jit(solution)/shard_map/reduce_sum | solution.py:49
  162.9 6.8 %all-to-all-start.6 = ((bf16[4,96,128]{2,1,0:T(8,128)(2,1)}), bf16[4,96,128]{2,1,0:T(8,128)(2,1)}, u32[]{:S(2)}, u32[]{:S(2)}) async-start(bf16[4,96,128]{2,1,0:T(8,128)(2,1)} %reduce_sum.47), calls=%async_computation.6 | async-start | bytes 196608 | tf_op jit(solution)/shard_map/all_to_all | solution.py:21
  169.7 1.5 convolution_convert_fusion.1
  171.2 0.9 copy.112
  172.1 1.6 convolution_convert_fusion.2
  173.7 0.9 copy.111
  174.6 7.1 %all-to-all-done.6 = bf16[4,96,128]{2,1,0:T(8,128)(2,1)} async-done(((bf16[4,96,128]{2,1,0:T(8,128)(2,1)}), bf16[4,96,128]{2,1,0:T(8,128)(2,1)}, u32[]{:S(2)}, u32[]{:S(2)}) %all-to-all-start.6) | async-done | bytes 98336 | tf_op jit(solution)/shard_map/all_to_all | solution.py:21
  181.7 0.9 convert_reduce_fusion
  182.6 0.6 slice_bitcast_fusion.1
  183.2 0.6 reshape.98
  (2 shorter events, 0.0 us)
Async XLA Ops:
  33.1 23.2 %copy-start.5 = (bf16[256,768]{1,0:T(8,128)(2,1)S(1)}, bf16[256,768]{1,0:T(8,128)(2,1)}, u32[]{:S(2)}) copy-start(bf16[256,768]{1,0:T(8,128)(2,1)} %param.7) | copy-start | bytes 1179652
  43.4 15.0 %all-to-all-start = ((bf16[2,32,96,128]{3,2,1,0:T(8,128)(2,1)}), bf16[2,32,96,128]{3,2,1,0:T(8,128)(2,1)S(1)}, u32[]{:S(2)}, u32[]{:S(2)}) async-start(bf16[2,32,96,128]{3,2,1,0:T(8,128)(2,1)} %broadcast_in_dim.8), calls=%async_computation | async-start | bytes 3145728 | tf_op jit(solution)/shard_map/all_to_all | solution.py:21
  59.7 18.5 %copy-start = (bf16[6,64,8,128]{3,2,0,1:T(8,128)(2,1)}, bf16[6,64,8,128]{3,2,0,1:T(8,128)(2,1)S(1)}, u32[]{:S(2)}) copy-start(bf16[6,64,8,128]{3,2,0,1:T(8,128)(2,1)S(1)} %get-tuple-element.28) | copy-start | bytes 2359300
  60.3 7.2 %copy-start.6 = (bf16[256,768]{1,0:T(8,128)(2,1)S(1)}, bf16[256,768]{1,0:T(8,128)(2,1)}, u32[]{:S(2)}) copy-start(bf16[256,768]{1,0:T(8,128)(2,1)} %param.4) | copy-start | bytes 1179652
  62.3 25.7 %all-to-all-start.2 = ((bf16[256,192,16]{0,2,1:T(8,128)(2,1)}), bf16[256,192,16]{0,2,1:T(8,128)(2,1)S(1)}, u32[]{:S(2)}, u32[]{:S(2)}) async-start(bf16[256,192,16]{0,2,1:T(8,128)(2,1)} %bitcast.70), calls=%async_computation.2 | async-start | bytes 3145728 | tf_op jit(solution)/shard_map/all_to_all | solution.py:71
  74.1 4.1 %copy-start.2 = (bf16[6,128,512]{2,1,0:T(8,128)(2,1)}, bf16[6,128,512]{2,1,0:T(8,128)(2,1)S(1)}, u32[]{:S(2)}) copy-start(bf16[6,128,512]{2,1,0:T(8,128)(2,1)S(1)} %reshape.85) | copy-start | bytes 2359300
  88.0 4.3 %copy-start.1 = (bf16[256,192,16]{0,2,1:T(8,128)(2,1)}, bf16[256,192,16]{0,2,1:T(8,128)(2,1)S(1)}, u32[]{:S(2)}) copy-start(bf16[256,192,16]{0,2,1:T(8,128)(2,1)S(1)} %all-to-all-done.2) | copy-start | bytes 4718596
  88.0 24.9 %all-to-all-start.1 = ((bf16[256,24,128]{0,1,2:T(8,128)(2,1)}), bf16[256,24,128]{0,1,2:T(8,128)(2,1)}, u32[]{:S(2)}, u32[]{:S(2)}) async-start(bf16[256,24,128]{0,1,2:T(8,128)(2,1)} %copy.94), calls=%async_computation.1 | async-start | bytes 3145728 | tf_op jit(solution)/shard_map/all_to_all | solution.py:76
  94.2 1.9 %copy-start.3 = (f32[256,6,512]{0,2,1:T(8,128)S(1)}, f32[256,6,512]{0,2,1:T(8,128)}, u32[]{:S(2)}) copy-start(f32[256,6,512]{0,2,1:T(8,128)} %get-tuple-element.7) | copy-start | bytes 9437188
  96.1 2.1 %copy-start.4 = (bf16[256,768]{0,1:T(8,128)(2,1)S(1)}, bf16[256,768]{0,1:T(8,128)(2,1)}, u32[]{:S(2)}) copy-start(bf16[256,768]{0,1:T(8,128)(2,1)} %copy.91) | copy-start | bytes 1179652
  112.9 13.5 %all-to-all-start.3 = ((bf16[2,32,48,128]{3,2,1,0:T(8,128)(2,1)}), bf16[2,32,48,128]{3,2,1,0:T(8,128)(2,1)}, u32[]{:S(2)}, u32[]{:S(2)}) async-start(bf16[2,32,48,128]{3,2,1,0:T(8,128)(2,1)} %reshape.94), calls=%async_computation.3 | async-start | bytes 1572864 | tf_op jit(solution)/shard_map/all_to_all | solution.py:21
  126.4 6.2 %all-to-all-start.4 = ((bf16[2,32,48,128]{3,2,1,0:T(8,128)(2,1)}), bf16[2,32,48,128]{3,2,1,0:T(8,128)(2,1)}, u32[]{:S(2)}, u32[]{:S(2)}) async-start(bf16[2,32,48,128]{3,2,1,0:T(8,128)(2,1)} %bitcast.81), calls=%async_computation.4 | async-start | bytes 1572864 | tf_op jit(solution)/shard_map/all_to_all | solution.py:21
  162.9 18.8 %all-to-all-start.6 = ((bf16[4,96,128]{2,1,0:T(8,128)(2,1)}), bf16[4,96,128]{2,1,0:T(8,128)(2,1)}, u32[]{:S(2)}, u32[]{:S(2)}) async-start(bf16[4,96,128]{2,1,0:T(8,128)(2,1)} %reduce_sum.47), calls=%async_computation.6 | async-start | bytes 196608 | tf_op jit(solution)/shard_map/all_to_all | solution.py:21

commit v3 on v1

v3 whole, which is shorter than its diff:
```python
import jax
import jax.numpy as jnp
from jax import lax
from jax.experimental import pallas as pl
from jax.experimental.pallas import tpu as pltpu
from jax.sharding import Mesh, PartitionSpec as P

NB = 6
ROWS = 256
DP = ("x_hi", "z_hi", "z_lo", "core")
MP = ("x_lo", "y")
SIZES = (2, 4, 4, 2, 2, 4)
F32 = jnp.float32
BF16 = jnp.bfloat16
PARAMS = pltpu.CompilerParams(vmem_limit_bytes=40 * 1024 * 1024)
SMEM = pl.BlockSpec(memory_space=pltpu.SMEM)
VMEM = pl.BlockSpec(memory_space=pltpu.VMEM)


def dot(lhs, rhs, lhs_dim, rhs_dim):
    return lax.dot_general(
        lhs, rhs, (((lhs_dim,), (rhs_dim,)), ((), ())), preferred_element_type=F32
    )


def halves(value, step):
    return value[:, step * 128 : (step + 1) * 128]


def back_kernel(at_ref, mine_ref, other_ref, c_ref, send_ref, wout_ref, left, right):
    first = at_ref[1] == 0
    for pair in range(NB // 2):
        rows = slice(48 + pair * 16, 48 + pair * 16 + 16)
        mine = mine_ref[:, rows, :].astype(F32)
        other = other_ref[:, rows, :].astype(F32)
        zero = jnp.where(first, mine, other)
        one = jnp.where(first, other, mine)
        for k in range(2):
            o = pair * 2 + k
            cut = slice(k * 8, k * 8 + 8)
            wide = jnp.stack([zero[:, cut], one[:, cut]], axis=1).reshape(512, 128)
            w = wide.astype(BF16)
            wout_ref[o] = w
            d = dot(w, c_ref[:, o * 128 : (o + 1) * 128], 1, 1)
            left[o * 512 : (o + 1) * 512, :] = d[:, :128]
            right[o * 512 : (o + 1) * 512, :] = d[:, 128:]
    for p in range(8):
        for g in range(24):
            at = pl.ds(p * 24 + g, 16, stride=192)
            send_ref[p, g, :, :128] = left[at, :].astype(BF16)
            send_ref[p, g, :, 128:] = right[at, :].astype(BF16)


def forward_kernel(at_ref, mine_ref, other_ref, x_ref, *rest):
    sends, (slope_ref, win_ref, mine_f, other_f, w_f, act) = rest[:8], rest[8:]
    place, first = at_ref[0], at_ref[1] == 0
    mine_f[...] = mine_ref[:, :48, :].astype(F32).reshape(32 * 48, 128)
    other_f[...] = other_ref[:, :48, :].astype(F32).reshape(32 * 48, 128)
    root = 0.7978845608028654
    for i in range(NB):
        for k in range(2):
            for c in range(4):
                at = pl.ds(i * 8 + k * 4 + c, 32, stride=48)
                mine, other = mine_f[at, :], other_f[at, :]
                w_f[c, pl.ds(k, 32, stride=4), :] = jnp.where(first, mine, other)
                w_f[c, pl.ds(2 + k, 32, stride=4), :] = jnp.where(first, other, mine)
        for c in range(4):
            w = w_f[c].astype(BF16)
            win_ref[i, :, c * 128 : (c + 1) * 128] = w
            v = dot(w, x_ref[:, i * 128 : (i + 1) * 128], 0, 1)
            square = v * v
            th = jnp.tanh(root * (v + 0.044715 * (v * square)))
            half = 0.5 * (1.0 + th)
            act[i * 4 + c] = (v * half).astype(BF16).reshape(8, 16, ROWS)
            slope_ref[i, c * 128 : (c + 1) * 128, :] = half + (0.5 * root) * v * (
                1.0 - th * th
            ) * (1.0 + 0.134145 * square)
    for s in range(8):
        to = lax.rem(place + s, 8)
        sends[s][...] = act[:, to]


def store_ordered(ref, rows, value):
    for n in range(32):
        ref[n // 16 * 16 + n % 4 * 4 + n // 4 % 4, rows, :] = value[n]


def first_grad_kernel(at_ref, back_ref, slope_ref, x_ref, dpre_ref, keep_ref, send_ref, p_f, o_f):
    first = at_ref[1] == 0
    for i in range(NB):
        parts = [back_ref[:, i * 4 + a].reshape(128, ROWS) for a in range(4)]
        x = x_ref[:, i * 128 : (i + 1) * 128]
        for c in range(4):
            d = (parts[c].astype(F32) * slope_ref[i, c * 128 : (c + 1) * 128, :]).astype(BF16)
            dpre_ref[i, c * 128 : (c + 1) * 128, :] = d
            p_f[c] = dot(x, d, 0, 1)
            for core in range(2):
                for k in range(2):
                    o_f[core, pl.ds(i * 8 + k * 4 + c, 32, stride=48), :] = p_f[
                        c, pl.ds(core * 2 + k, 32, stride=4), :
                    ]
    zero = o_f[0].reshape(32, 48, 128)
    one = o_f[1].reshape(32, 48, 128)
    store_ordered(keep_ref, slice(0, 48), jnp.where(first, zero, one).astype(BF16))
    store_ordered(send_ref, slice(0, 48), jnp.where(first, one, zero).astype(BF16))


def second_grad_kernel(at_ref, *rest):
    pieces, (c_ref, mixed_ref, keep_ref, send_ref, left, right) = rest[:8], rest[8:]
    place, first = at_ref[0], at_ref[1] == 0
    for s in range(8):
        start = pl.multiple_of(lax.rem(place + 8 - s, 8) * 384, 384)
        piece = pieces[s][...].reshape(384, ROWS).astype(F32)
        left[pl.ds(start, 384), :] = piece[:, :128]
        right[pl.ds(start, 384), :] = piece[:, 128:]
    for j in range(16):
        at = pl.ds(j, 192, stride=16)
        mixed_ref[j * 192 : (j + 1) * 192, :128] = left[at, :].astype(BF16)
        mixed_ref[j * 192 : (j + 1) * 192, 128:] = right[at, :].astype(BF16)
    for pair in range(NB // 2):
        kept, sent = [], []
        for k in range(2):
            o = pair * 2 + k
            m = mixed_ref[o * 512 : (o + 1) * 512, :]
            g = dot(m, c_ref[:, o * 128 : (o + 1) * 128], 1, 0).reshape(32, 2, 8, 128)
            kept.append(jnp.where(first, g[:, 0], g[:, 1]))
            sent.append(jnp.where(first, g[:, 1], g[:, 0]))
        rows = slice(pair * 16, pair * 16 + 16)
        store_ordered(keep_ref, rows, jnp.concatenate(kept, axis=1).astype(BF16))
        store_ordered(send_ref, rows, jnp.concatenate(sent, axis=1).astype(BF16))


def call(kernel, name, args, outs, scratch):
    return pl.pallas_call(
        kernel,
        name=name,
        out_shape=[jax.ShapeDtypeStruct(shape, dtype) for shape, dtype in outs],
        in_specs=[SMEM] + [VMEM] * (len(args) - 1),
        out_specs=[VMEM] * len(outs),
        scratch_shapes=[pltpu.VMEM(shape, F32 if dtype is F32 else BF16) for shape, dtype in scratch],
        compiler_params=PARAMS,
        cost_estimate=pl.CostEstimate(
            flops=2 * 256 * 128 * 512 * 6, bytes_accessed=6_000_000, transcendentals=0
        ),
    )(*args)


def exchange(value, axis):
    return lax.all_to_all(value, axis, 0, 0, tiled=True)


def swap_cores(value):
    return lax.ppermute(value, "core", [(0, 1), (1, 0)])


def rotate(value, step):
    return lax.ppermute(value, MP, [(n, (n + step) % 8) for n in range(8)])


def add(first, second):
    return (first.astype(F32) + second.astype(F32)).astype(BF16)


def on_device(tokens, w_in, w_out, cotangent):
    scale = 1.0 / jnp.sqrt(F32(ROWS * 64))
    at = jnp.stack([lax.axis_index(MP), lax.axis_index("core")]).astype(jnp.int32)
    shard = jnp.concatenate(
        [w_in.transpose(1, 0, 2).reshape(48, 128), w_out.transpose(1, 0, 2).reshape(48, 128)]
    )
    along_z = lax.all_gather(shard, ("z_hi", "z_lo"), axis=0, tiled=False)
    mine = lax.all_gather(along_z, "x_hi", axis=0, tiled=False).reshape(32, 96, 128)
    other = swap_cores(mine)

    piece = (24, 16, ROWS)
    half = ((32, 48, 128), BF16)
    block = (NB, 512, ROWS)
    back_send, wout = call(
        back_kernel, "d_mixed", (at, mine, other, cotangent),
        [((8,) + piece, BF16), ((NB, 512, 128), BF16)],
        [((3072, 128), F32), ((3072, 128), F32)],
    )
    back = exchange(back_send, MP)
    *act, slope, win = call(
        forward_kernel, "act", (at, mine, other, tokens),
        [(piece, BF16)] * 8 + [(block, F32), ((NB, 128, 512), BF16)],
        [((1536, 128), F32), ((1536, 128), F32), ((4, 128, 128), F32), ((24, 8, 16, ROWS), BF16)],
    )
    moved = [act[0]] + [rotate(act[s], s) for s in range(1, 8)]
    d_pre, keep_in, send_in = call(
        first_grad_kernel, "first_grad", (at, back, slope, tokens),
        [(block, BF16), half, half],
        [((4, 128, 128), F32), ((2, 1536, 128), F32)],
    )
    half_in = add(keep_in, swap_cores(send_in))
    got_in = exchange(half_in.reshape(8, 192, 128), ("x_hi", "z_lo"))
    mixed, keep_out, send_out = call(
        second_grad_kernel, "second_grad", (at, *moved, cotangent),
        [((3072, ROWS), BF16), half, half],
        [((3072, 128), F32), ((3072, 128), F32)],
    )
    half_out = add(keep_out, swap_cores(send_out))
    got_out = exchange(half_out.reshape(8, 192, 128), ("x_hi", "z_lo"))
    both = jnp.concatenate(
        [g.astype(F32).sum(axis=0).astype(BF16).reshape(4, 48, 128) for g in (got_in, got_out)],
        axis=1,
    )
    total = exchange(both, "z_hi").astype(F32).sum(axis=0) * scale
    grad_in = total[:48].reshape(NB, 2, 512).transpose(1, 0, 2)
    grad_out = total[48:].reshape(NB, 8, 128).transpose(1, 0, 2)

    out = jnp.einsum("oet,oen->ton", mixed.reshape(block), wout, preferred_element_type=F32)
    output = out.astype(BF16).reshape(ROWS, 768)
    grad_x = jnp.einsum("iet,ire->tir", d_pre, win, preferred_element_type=F32)
    grad_tokens = grad_x.astype(BF16).reshape(ROWS, 768)
    return (output, grad_tokens, grad_in, grad_out)


def solution(mesh):
    fine = Mesh(mesh.devices.reshape(SIZES), DP + MP)
    placed = (P(DP, MP), P(DP, MP, None), P(DP, MP, None), P(DP, MP))
    return jax.shard_map(
        on_device,
        mesh=fine,
        in_specs=placed,
        out_specs=(P(DP, MP), P(DP, MP), P(DP, MP, None), P(DP, MP, None)),
        check_vma=False,
    )
```

time: 210 us -> 176 us (0.84)
  the two profiles are of different devices: /device:TPU:1 before, /device:TPU:8 now
where the time goes in v3:
time: 176 us; the launch traced here: 175 us
  starting transfers between devices  52.8 us (30%)
  blocking collectives  47.6 us (27%)
  waiting for transfers between devices  42.6 us (24%)
  local copies, waits for them, and re-layouts  11.6 us (7%)
  Pallas kernels  10.8 us (6%)
  other arithmetic  5.18 us (3%)
  matrix products  3.21 us (2%)
    all_gather x1, blocking collectives, on_device(): along_z = lax.all_gather(shard, ('z_hi', 'z_lo'), axis=0, tiled=False)  37.7 us
    ppermute x7, starting transfers between devices, rotate(): return lax.ppermute(value, MP, [(n, (n + step) % 8) for n in range(8)])  26.8 us
    all_to_all x4, waiting for transfers between devices, exchange(): return lax.all_to_all(value, axis, 0, 0, tiled=True)  26 us
    all_to_all x4, starting transfers between devices, exchange(): return lax.all_to_all(value, axis, 0, 0, tiled=True)  20.1 us
    ppermute x7, waiting for transfers between devices, rotate(): return lax.ppermute(value, MP, [(n, (n + step) % 8) for n in range(8)])  11.2 us
    pallas_call x4, Pallas kernels, call(): pl.pallas_call(kernel, name=name, out_shape=[jax.ShapeDtypeStruct(shape,...  10.8 us
    all_gather x1, blocking collectives, on_device(): lax.all_gather(along_z, 'x_hi', axis=0, tiled=False).reshape(32, 96, 128)  9.95 us
    unnamed x22, local copies, waits for them, and re-layouts  9.57 us
  transfers between devices with their start and end apart: 14, of which 10 were waited for; matrix products, arithmetic and copies ran while one was open for 5% of the time, Pallas kernels for 4%

profile of v3, /device:TPU:8, one launch (start us, length us, event | category | flops | bytes accessed | tf_op | source)
XLA Modules:
  0.0 174.8 jit_solution(6653120644320109355)
XLA Ops:
  0.6 0.0 copy-start.5
  0.6 0.8 reshape.44
  1.4 0.7 pad_maximum_fusion.1
  2.1 37.7 %all-gather = bf16[1536,128]{1,0:T(8,128)(2,1)S(1)} all-gather(bf16[96,128]{1,0:T(8,128)(2,1)S(1)} %pad_maximum_fusion.1), channel_id=2, replica_groups=mesh['x_hi'=2,'z_hi'=4,'z_lo'=4,'core'=2,'x_lo'=2,'y'=4] {'z_hi','z_lo'}, dimensions={0}, use_global_device_ids=true | all-gather | bytes 417792 | tf_op jit(solution)/shard_map/all_gather | solution.py:170
  39.8 9.9 %all-gather.1.mine_ref = bf16[32,96,128]{2,1,0:T(8,128)(2,1)S(1)} all-gather(bf16[16,96,128]{2,1,0:T(8,128)(2,1)S(1)} %bitcast.29), channel_id=3, replica_groups=mesh['x_hi'=2,'z_hi'=4,'z_lo'=4,'core'=2,'x_lo'=2,'y'=4] {'x_hi'}, dimensions={0}, use_global_device_ids=true | all-gather | bytes 1179648 | tf_op jit(solution)/shard_map/all_gather | solution.py:171
  49.8 1.9 %collective-permute-start = (bf16[32,96,128]{2,1,0:T(8,128)(2,1)S(1)}, bf16[32,96,128]{2,1,0:T(8,128)(2,1)S(1)}, u32[]{:S(2)}, u32[]{:S(2)}) collective-permute-start(bf16[32,96,128]{2,1,0:T(8,128)(2,1)S(1)} %all-gather.1.mine_ref), channel_id=1, source_target_pairs={{0,8},{8,0},{1,9},{9,1},{2,10},{10,2},{3,11},{11,3},{4,12},{12,4},... | collective-permute-start | bytes 2359304 | tf_op jit(solution)/shard_map/ppermute | solution.py:153
  51.7 0.1 pad_add_fusion.at_ref
  51.8 2.2 %collective-permute-done.other_ref = bf16[32,96,128]{2,1,0:T(8,128)(2,1)S(1)} collective-permute-done((bf16[32,96,128]{2,1,0:T(8,128)(2,1)S(1)}, bf16[32,96,128]{2,1,0:T(8,128)(2,1)S(1)}, u32[]{:S(2)}, u32[]{:S(2)}) %collective-permute-start) | collective-permute-done | bytes 786464 | tf_op jit(solution)/shard_map/ppermute | solution.py:153
  53.9 0.0 copy-done.5
  53.9 3.4 %d_mixed.1 = (bf16[8,24,16,256]{3,2,1,0:T(8,128)(2,1)S(1)}, bf16[6,512,128]{2,1,0:T(8,128)(2,1)S(1)}) custom-call(s32[2]{0:T(128)S(1)} %pad_add_fusion.at_ref, bf16[32,96,128]{2,1,0:T(8,128)(2,1)S(1)} %all-gather.1.mine_ref, bf16[32,96,128]{2,1,0:T(8,128)(2,1)S(1)} %collective-permute-done.other_ref, bf16[256,768]{1,0:T(8,128)(2,1)S(1)} %copy-done.5), custom_call_target="tpu_custom_call" | custom-call | flops 201326592 | bytes 6000000 | tf_op jit(solution)/shard_map/d_mixed/pallas_call | solution.py:134
  57.4 0.0 copy-start.2
  57.4 1.2 copy-done.2
  58.5 0.9 copy-done.8
  59.4 5.8 %all-to-all-start = ((bf16[8,24,16,256]{3,2,1,0:T(8,128)(2,1)}), bf16[8,24,16,256]{3,2,1,0:T(8,128)(2,1)S(1)}, u32[]{:S(2)}, u32[]{:S(2)}) async-start(bf16[8,24,16,256]{3,2,1,0:T(8,128)(2,1)} %copy-done.2), calls=%async_computation | async-start | bytes 3145728 | tf_op jit(solution)/shard_map/all_to_all | solution.py:149
  65.3 1.0 copy-done.6
  66.3 3.2 %act.1 = (bf16[24,16,256]{2,1,0:T(8,128)(2,1)S(1)}, bf16[24,16,256]{2,1,0:T(8,128)(2,1)S(1)}, bf16[24,16,256]{2,1,0:T(8,128)(2,1)S(1)}, bf16[24,16,256]{2,1,0:T(...) custom-call(s32[2]{0:T(128)S(1)} %pad_add_fusion.at_ref, ...), custom_call_target="tpu_custom_call" | custom-call | flops 201326592 | bytes 6000000 | tf_op jit(solution)/shard_map/act/pallas_call | solution.py:134
  69.5 0.0 copy-start
  69.5 1.6 copy-done
  71.1 3.4 %collective-permute-start.1 = (bf16[24,16,256]{2,1,0:T(8,128)(2,1)S(1)}, bf16[24,16,256]{2,1,0:T(8,128)(2,1)S(1)}, u32[]{:S(2)}, u32[]{:S(2)}) collective-permute-start(bf16[24,16,256]{2,1,0:T(8,128)(2,1)S(1)} %get-tuple-element.24), channel_id=1, source_target_pairs={{0,1},{1,2},{2,3},{3,4},{4,5},{5,6},{6,7},{7,0},{8,9},{9,10},{10,1... | collective-permute-start | bytes 589832 | tf_op jit(solution)/shard_map/ppermute | solution.py:157
  74.5 4.0 %collective-permute-start.2 = (bf16[24,16,256]{2,1,0:T(8,128)(2,1)S(1)}, bf16[24,16,256]{2,1,0:T(8,128)(2,1)S(1)}, u32[]{:S(2)}, u32[]{:S(2)}) collective-permute-start(bf16[24,16,256]{2,1,0:T(8,128)(2,1)S(1)} %get-tuple-element.25), channel_id=1, source_target_pairs={{0,2},{1,3},{2,4},{3,5},{4,6},{5,7},{6,0},{7,1},{8,10},{9,11},{10,... | collective-permute-start | bytes 589832 | tf_op jit(solution)/shard_map/ppermute | solution.py:157
  78.5 4.0 %collective-permute-start.3 = (bf16[24,16,256]{2,1,0:T(8,128)(2,1)S(1)}, bf16[24,16,256]{2,1,0:T(8,128)(2,1)S(1)}, u32[]{:S(2)}, u32[]{:S(2)}) collective-permute-start(bf16[24,16,256]{2,1,0:T(8,128)(2,1)S(1)} %get-tuple-element.26), channel_id=1, source_target_pairs={{0,3},{1,4},{2,5},{3,6},{4,7},{5,0},{6,1},{7,2},{8,11},{9,12},{10,... | collective-permute-start | bytes 589832 | tf_op jit(solution)/shard_map/ppermute | solution.py:157
  82.5 2.5 %collective-permute-start.4 = (bf16[24,16,256]{2,1,0:T(8,128)(2,1)S(1)}, bf16[24,16,256]{2,1,0:T(8,128)(2,1)S(1)}, u32[]{:S(2)}, u32[]{:S(2)}) collective-permute-start(bf16[24,16,256]{2,1,0:T(8,128)(2,1)S(1)} %get-tuple-element.27), channel_id=1, source_target_pairs={{0,4},{1,5},{2,6},{3,7},{4,0},{5,1},{6,2},{7,3},{8,12},{9,13},{10,... | collective-permute-start | bytes 589832 | tf_op jit(solution)/shard_map/ppermute | solution.py:157
  85.0 2.2 %collective-permute-start.5 = (bf16[24,16,256]{2,1,0:T(8,128)(2,1)S(1)}, bf16[24,16,256]{2,1,0:T(8,128)(2,1)S(1)}, u32[]{:S(2)}, u32[]{:S(2)}) collective-permute-start(bf16[24,16,256]{2,1,0:T(8,128)(2,1)S(1)} %get-tuple-element.28), channel_id=1, source_target_pairs={{0,5},{1,6},{2,7},{3,0},{4,1},{5,2},{6,3},{7,4},{8,13},{9,14},{10,... | collective-permute-start | bytes 589832 | tf_op jit(solution)/shard_map/ppermute | solution.py:157
  87.2 0.9 collective-permute-done.1.rest_1_
  88.1 8.9 %collective-permute-start.6 = (bf16[24,16,256]{2,1,0:T(8,128)(2,1)S(1)}, bf16[24,16,256]{2,1,0:T(8,128)(2,1)S(1)}, u32[]{:S(2)}, u32[]{:S(2)}) collective-permute-start(bf16[24,16,256]{2,1,0:T(8,128)(2,1)S(1)} %get-tuple-element.29), channel_id=1, source_target_pairs={{0,6},{1,7},{2,0},{3,1},{4,2},{5,3},{6,4},{7,5},{8,14},{9,15},{10,... | collective-permute-start | bytes 589832 | tf_op jit(solution)/shard_map/ppermute | solution.py:157
  97.0 1.6 collective-permute-done.2.rest_2_
  98.6 1.9 %collective-permute-start.7 = (bf16[24,16,256]{2,1,0:T(8,128)(2,1)S(1)}, bf16[24,16,256]{2,1,0:T(8,128)(2,1)S(1)}, u32[]{:S(2)}, u32[]{:S(2)}) collective-permute-start(bf16[24,16,256]{2,1,0:T(8,128)(2,1)S(1)} %get-tuple-element.30), channel_id=1, source_target_pairs={{0,7},{1,0},{2,1},{3,2},{4,3},{5,4},{6,5},{7,6},{8,15},{9,8},{10,9... | collective-permute-start | bytes 589832 | tf_op jit(solution)/shard_map/ppermute | solution.py:157
  100.5 0.0 collective-permute-done.3.rest_3_
  100.5 0.0 collective-permute-done.4.rest_4_
  100.5 0.0 collective-permute-done.5.rest_5_
  100.5 5.4 %collective-permute-done.6.rest_6_ = bf16[24,16,256]{2,1,0:T(8,128)(2,1)S(1)} collective-permute-done((bf16[24,16,256]{2,1,0:T(8,128)(2,1)S(1)}, bf16[24,16,256]{2,1,0:T(8,128)(2,1)S(1)}, u32[]{:S(2)}, u32[]{:S(2)}) %collective-permute-start.6) | collective-permute-done | bytes 196640 | tf_op jit(solution)/shard_map/ppermute | solution.py:157
  106.0 3.3 %collective-permute-done.7.rest_7_ = bf16[24,16,256]{2,1,0:T(8,128)(2,1)S(1)} collective-permute-done((bf16[24,16,256]{2,1,0:T(8,128)(2,1)S(1)}, bf16[24,16,256]{2,1,0:T(8,128)(2,1)S(1)}, u32[]{:S(2)}, u32[]{:S(2)}) %collective-permute-start.7) | collective-permute-done | bytes 196640 | tf_op jit(solution)/shard_map/ppermute | solution.py:157
  109.2 2.2 %second_grad.1 = (bf16[3072,256]{1,0:T(8,128)(2,1)S(1)}, bf16[32,48,128]{2,1,0:T(8,128)(2,1)S(1)}, bf16[32,48,128]{2,1,0:T(8,128)(2,1)S(1)}) custom-call(s32[2]{0:T(128)S(1)} %pad_add_fusion.at_ref, bf16[24,16,256]{2,1,0:T(8,128)(2,1)S(1)} %get-tuple-element.23.rest_0_, bf16[24,16,256]{2,1,0:T(8,128)(2,1)S(1)} %collective-permute-done.1.rest_1_, ...), custom_call_target="tpu_custom_call" | custom-call | flops 201326592 | bytes 6000000 | tf_op jit(solution)/shard_map/second_grad/pallas_call | solution.py:134
  111.5 0.0 copy-start.7
  111.5 2.1 %collective-permute-start.9 = (bf16[32,48,128]{2,1,0:T(8,128)(2,1)S(1)}, bf16[32,48,128]{2,1,0:T(8,128)(2,1)S(1)}, u32[]{:S(2)}, u32[]{:S(2)}) collective-permute-start(bf16[32,48,128]{2,1,0:T(8,128)(2,1)S(1)} %get-tuple-element.39), channel_id=1, source_target_pairs={{0,8},{8,0},{1,9},{9,1},{2,10},{10,2},{3,11},{11,3},{4,12},{12,4},... | collective-permute-start | bytes 1179656 | tf_op jit(solution)/shard_map/ppermute | solution.py:153
  113.5 1.7 collective-permute-done.9
  115.2 0.0 copy-done.9
  115.2 0.9 add_convert_fusion
  116.1 0.0 all-to-all-done.back_ref
  116.1 4.1 %all-to-all-start.2 = ((bf16[8,192,128]{2,1,0:T(8,128)(2,1)}), bf16[8,192,128]{2,1,0:T(8,128)(2,1)}, u32[]{:S(2)}, u32[]{:S(2)}) async-start(bf16[8,192,128]{2,1,0:T(8,128)(2,1)} %bitcast.28), calls=%async_computation.2 | async-start | bytes 786432 | tf_op jit(solution)/shard_map/all_to_all | solution.py:149
  120.2 0.0 copy-done.7
  120.2 0.0 copy-start.1
  120.2 1.9 %copy-done.1 = f32[6,512,256]{2,1,0:T(8,128)S(1)} copy-done((f32[6,512,256]{2,1,0:T(8,128)S(1)}, f32[6,512,256]{2,1,0:T(8,128)}, u32[]{:S(2)}) %copy-start.1) | copy-done | bytes 3145752
  122.1 1.9 %first_grad.1 = (bf16[6,512,256]{2,1,0:T(8,128)(2,1)S(1)}, bf16[32,48,128]{2,1,0:T(8,128)(2,1)S(1)}, bf16[32,48,128]{2,1,0:T(8,128)(2,1)S(1)}) custom-call(s32[2]{0:T(128)S(1)} %pad_add_fusion.at_ref, bf16[8,24,16,256]{3,2,1,0:T(8,128)(2,1)S(1)} %all-to-all-done.back_ref, f32[6,512,256]{2,1,0:T(8,128)S(1)} %copy-done.1, bf16[256,768]{1,0:T(8,128)(2,1)S(1)} %copy-done.7), custom_call_target="tpu_custom_call" | custom-call | flops 201326592 | bytes 6000000 | tf_op jit(solution)/shard_map/first_grad/pallas_call | solution.py:134
  124.0 1.1 copy-done.3
  125.2 2.0 %collective-permute-start.8 = (bf16[32,48,128]{2,1,0:T(8,128)(2,1)S(1)}, bf16[32,48,128]{2,1,0:T(8,128)(2,1)S(1)}, u32[]{:S(2)}, u32[]{:S(2)}) collective-permute-start(bf16[32,48,128]{2,1,0:T(8,128)(2,1)S(1)} %get-tuple-element.37), channel_id=1, source_target_pairs={{0,8},{8,0},{1,9},{9,1},{2,10},{10,2},{3,11},{11,3},{4,12},{12,4},... | collective-permute-start | bytes 1179656 | tf_op jit(solution)/shard_map/ppermute | solution.py:153
  127.2 1.6 collective-permute-done.8
  128.8 0.8 add_convert_fusion.1
  129.6 5.2 %all-to-all-done.2 = bf16[8,192,128]{2,1,0:T(8,128)(2,1)} async-done(((bf16[8,192,128]{2,1,0:T(8,128)(2,1)}), bf16[8,192,128]{2,1,0:T(8,128)(2,1)}, u32[]{:S(2)}, u32[]{:S(2)}) %all-to-all-start.2) | async-done | bytes 393248 | tf_op jit(solution)/shard_map/all_to_all | solution.py:149
  134.9 3.5 %all-to-all-start.1 = ((bf16[8,192,128]{2,1,0:T(8,128)(2,1)}), bf16[8,192,128]{2,1,0:T(8,128)(2,1)S(1)}, u32[]{:S(2)}, u32[]{:S(2)}) async-start(bf16[8,192,128]{2,1,0:T(8,128)(2,1)} %bitcast.11), calls=%async_computation.1 | async-start | bytes 786432 | tf_op jit(solution)/shard_map/all_to_all | solution.py:149
  138.3 1.1 reduce_sum.34
  139.4 12.4 %all-to-all-done.1 = bf16[8,192,128]{2,1,0:T(8,128)(2,1)S(1)} async-done(((bf16[8,192,128]{2,1,0:T(8,128)(2,1)}), bf16[8,192,128]{2,1,0:T(8,128)(2,1)S(1)}, u32[]{:S(2)}, u32[]{:S(2)}) %all-to-all-start.1) | async-done | bytes 393248 | tf_op jit(solution)/shard_map/all_to_all | solution.py:149
  151.8 0.1 reduce_sum.33
  151.9 0.7 pad_maximum_fusion
  152.5 6.7 %all-to-all-start.3 = ((bf16[4,96,128]{2,1,0:T(8,128)(2,1)}), bf16[4,96,128]{2,1,0:T(8,128)(2,1)}, u32[]{:S(2)}, u32[]{:S(2)}) async-start(bf16[4,96,128]{2,1,0:T(8,128)(2,1)} %pad_maximum_fusion), calls=%async_computation.3 | async-start | bytes 196608 | tf_op jit(solution)/shard_map/all_to_all | solution.py:149
  159.2 1.7 convolution_convert_fusion.1
  160.9 0.9 copy.15
  161.9 0.0 copy-done.4
  161.9 1.5 convolution_convert_fusion
  163.4 0.9 copy.16
  164.3 8.3 %all-to-all-done.3 = bf16[4,96,128]{2,1,0:T(8,128)(2,1)} async-done(((bf16[4,96,128]{2,1,0:T(8,128)(2,1)}), bf16[4,96,128]{2,1,0:T(8,128)(2,1)}, u32[]{:S(2)}, u32[]{:S(2)}) %all-to-all-start.3) | async-done | bytes 98336 | tf_op jit(solution)/shard_map/all_to_all | solution.py:149
  172.6 0.9 convert_reduce_fusion
  173.5 0.6 slice_bitcast_fusion
  174.1 0.6 reshape.54
  (6 shorter events, 0.0 us)
Async XLA Ops:
  0.6 53.3 %copy-start.5 = (bf16[256,768]{1,0:T(8,128)(2,1)S(1)}, bf16[256,768]{1,0:T(8,128)(2,1)}, u32[]{:S(2)}) copy-start(bf16[256,768]{1,0:T(8,128)(2,1)} %rest_8_.1) | copy-start | bytes 1179652
  49.8 4.2 %collective-permute-start = (bf16[32,96,128]{2,1,0:T(8,128)(2,1)S(1)}, bf16[32,96,128]{2,1,0:T(8,128)(2,1)S(1)}, u32[]{:S(2)}, u32[]{:S(2)}) collective-permute-start(bf16[32,96,128]{2,1,0:T(8,128)(2,1)S(1)} %all-gather.1.mine_ref), channel_id=1, source_target_pairs={{0,8},{8,0},{1,9},{9,1},{2,10},{10,2},{3,11},{11,3},{4,12},{12,4},... | collective-permute-start | bytes 2359304 | tf_op jit(solution)/shard_map/ppermute | solution.py:153
  57.4 1.2 copy-start.2
  58.5 0.9 copy-start.8
  59.4 56.7 %all-to-all-start = ((bf16[8,24,16,256]{3,2,1,0:T(8,128)(2,1)}), bf16[8,24,16,256]{3,2,1,0:T(8,128)(2,1)S(1)}, u32[]{:S(2)}, u32[]{:S(2)}) async-start(bf16[8,24,16,256]{3,2,1,0:T(8,128)(2,1)} %copy-done.2), calls=%async_computation | async-start | bytes 3145728 | tf_op jit(solution)/shard_map/all_to_all | solution.py:149
  65.3 1.0 copy-start.6
  69.5 1.6 copy-start
  71.1 44.1 %copy-start.9 = (bf16[6,128,512]{2,1,0:T(8,128)(2,1)}, bf16[6,128,512]{2,1,0:T(8,128)(2,1)S(1)}, u32[]{:S(2)}) copy-start(bf16[6,128,512]{2,1,0:T(8,128)(2,1)S(1)} %get-tuple-element.32) | copy-start | bytes 2359300
  71.1 17.0 %collective-permute-start.1 = (bf16[24,16,256]{2,1,0:T(8,128)(2,1)S(1)}, bf16[24,16,256]{2,1,0:T(8,128)(2,1)S(1)}, u32[]{:S(2)}, u32[]{:S(2)}) collective-permute-start(bf16[24,16,256]{2,1,0:T(8,128)(2,1)S(1)} %get-tuple-element.24), channel_id=1, source_target_pairs={{0,1},{1,2},{2,3},{3,4},{4,5},{5,6},{6,7},{7,0},{8,9},{9,10},{10,1... | collective-permute-start | bytes 589832 | tf_op jit(solution)/shard_map/ppermute | solution.py:157
  74.5 24.1 %collective-permute-start.2 = (bf16[24,16,256]{2,1,0:T(8,128)(2,1)S(1)}, bf16[24,16,256]{2,1,0:T(8,128)(2,1)S(1)}, u32[]{:S(2)}, u32[]{:S(2)}) collective-permute-start(bf16[24,16,256]{2,1,0:T(8,128)(2,1)S(1)} %get-tuple-element.25), channel_id=1, source_target_pairs={{0,2},{1,3},{2,4},{3,5},{4,6},{5,7},{6,0},{7,1},{8,10},{9,11},{10,... | collective-permute-start | bytes 589832 | tf_op jit(solution)/shard_map/ppermute | solution.py:157
  78.5 22.0 %collective-permute-start.3 = (bf16[24,16,256]{2,1,0:T(8,128)(2,1)S(1)}, bf16[24,16,256]{2,1,0:T(8,128)(2,1)S(1)}, u32[]{:S(2)}, u32[]{:S(2)}) collective-permute-start(bf16[24,16,256]{2,1,0:T(8,128)(2,1)S(1)} %get-tuple-element.26), channel_id=1, source_target_pairs={{0,3},{1,4},{2,5},{3,6},{4,7},{5,0},{6,1},{7,2},{8,11},{9,12},{10,... | collective-permute-start | bytes 589832 | tf_op jit(solution)/shard_map/ppermute | solution.py:157
  82.5 18.0 %collective-permute-start.4 = (bf16[24,16,256]{2,1,0:T(8,128)(2,1)S(1)}, bf16[24,16,256]{2,1,0:T(8,128)(2,1)S(1)}, u32[]{:S(2)}, u32[]{:S(2)}) collective-permute-start(bf16[24,16,256]{2,1,0:T(8,128)(2,1)S(1)} %get-tuple-element.27), channel_id=1, source_target_pairs={{0,4},{1,5},{2,6},{3,7},{4,0},{5,1},{6,2},{7,3},{8,12},{9,13},{10,... | collective-permute-start | bytes 589832 | tf_op jit(solution)/shard_map/ppermute | solution.py:157
  85.0 15.6 %collective-permute-start.5 = (bf16[24,16,256]{2,1,0:T(8,128)(2,1)S(1)}, bf16[24,16,256]{2,1,0:T(8,128)(2,1)S(1)}, u32[]{:S(2)}, u32[]{:S(2)}) collective-permute-start(bf16[24,16,256]{2,1,0:T(8,128)(2,1)S(1)} %get-tuple-element.28), channel_id=1, source_target_pairs={{0,5},{1,6},{2,7},{3,0},{4,1},{5,2},{6,3},{7,4},{8,13},{9,14},{10,... | collective-permute-start | bytes 589832 | tf_op jit(solution)/shard_map/ppermute | solution.py:157
  88.1 17.9 %collective-permute-start.6 = (bf16[24,16,256]{2,1,0:T(8,128)(2,1)S(1)}, bf16[24,16,256]{2,1,0:T(8,128)(2,1)S(1)}, u32[]{:S(2)}, u32[]{:S(2)}) collective-permute-start(bf16[24,16,256]{2,1,0:T(8,128)(2,1)S(1)} %get-tuple-element.29), channel_id=1, source_target_pairs={{0,6},{1,7},{2,0},{3,1},{4,2},{5,3},{6,4},{7,5},{8,14},{9,15},{10,... | collective-permute-start | bytes 589832 | tf_op jit(solution)/shard_map/ppermute | solution.py:157
  98.6 10.6 %collective-permute-start.7 = (bf16[24,16,256]{2,1,0:T(8,128)(2,1)S(1)}, bf16[24,16,256]{2,1,0:T(8,128)(2,1)S(1)}, u32[]{:S(2)}, u32[]{:S(2)}) collective-permute-start(bf16[24,16,256]{2,1,0:T(8,128)(2,1)S(1)} %get-tuple-element.30), channel_id=1, source_target_pairs={{0,7},{1,0},{2,1},{3,2},{4,3},{5,4},{6,5},{7,6},{8,15},{9,8},{10,9... | collective-permute-start | bytes 589832 | tf_op jit(solution)/shard_map/ppermute | solution.py:157
  111.5 8.7 %copy-start.7 = (bf16[256,768]{1,0:T(8,128)(2,1)S(1)}, bf16[256,768]{1,0:T(8,128)(2,1)}, u32[]{:S(2)}) copy-start(bf16[256,768]{1,0:T(8,128)(2,1)} %x_ref.3) | copy-start | bytes 1179652
  111.5 3.7 %collective-permute-start.9 = (bf16[32,48,128]{2,1,0:T(8,128)(2,1)S(1)}, bf16[32,48,128]{2,1,0:T(8,128)(2,1)S(1)}, u32[]{:S(2)}, u32[]{:S(2)}) collective-permute-start(bf16[32,48,128]{2,1,0:T(8,128)(2,1)S(1)} %get-tuple-element.39), channel_id=1, source_target_pairs={{0,8},{8,0},{1,9},{9,1},{2,10},{10,2},{3,11},{11,3},{4,12},{12,4},... | collective-permute-start | bytes 1179656 | tf_op jit(solution)/shard_map/ppermute | solution.py:153
  116.1 18.8 %all-to-all-start.2 = ((bf16[8,192,128]{2,1,0:T(8,128)(2,1)}), bf16[8,192,128]{2,1,0:T(8,128)(2,1)}, u32[]{:S(2)}, u32[]{:S(2)}) async-start(bf16[8,192,128]{2,1,0:T(8,128)(2,1)} %bitcast.28), calls=%async_computation.2 | async-start | bytes 786432 | tf_op jit(solution)/shard_map/all_to_all | solution.py:149
  120.2 1.9 %copy-start.1 = (f32[6,512,256]{2,1,0:T(8,128)S(1)}, f32[6,512,256]{2,1,0:T(8,128)}, u32[]{:S(2)}) copy-start(f32[6,512,256]{2,1,0:T(8,128)} %copy-done) | copy-start | bytes 9437188
  124.0 1.2 copy-start.3
  125.2 3.6 %collective-permute-start.8 = (bf16[32,48,128]{2,1,0:T(8,128)(2,1)S(1)}, bf16[32,48,128]{2,1,0:T(8,128)(2,1)S(1)}, u32[]{:S(2)}, u32[]{:S(2)}) collective-permute-start(bf16[32,48,128]{2,1,0:T(8,128)(2,1)S(1)} %get-tuple-element.37), channel_id=1, source_target_pairs={{0,8},{8,0},{1,9},{9,1},{2,10},{10,2},{3,11},{11,3},{4,12},{12,4},... | collective-permute-start | bytes 1179656 | tf_op jit(solution)/shard_map/ppermute | solution.py:153
  134.9 16.9 %all-to-all-start.1 = ((bf16[8,192,128]{2,1,0:T(8,128)(2,1)}), bf16[8,192,128]{2,1,0:T(8,128)(2,1)S(1)}, u32[]{:S(2)}, u32[]{:S(2)}) async-start(bf16[8,192,128]{2,1,0:T(8,128)(2,1)} %bitcast.11), calls=%async_computation.1 | async-start | bytes 786432 | tf_op jit(solution)/shard_map/all_to_all | solution.py:149
  152.5 20.1 %all-to-all-start.3 = ((bf16[4,96,128]{2,1,0:T(8,128)(2,1)}), bf16[4,96,128]{2,1,0:T(8,128)(2,1)}, u32[]{:S(2)}, u32[]{:S(2)}) async-start(bf16[4,96,128]{2,1,0:T(8,128)(2,1)} %pad_maximum_fusion), calls=%async_computation.3 | async-start | bytes 196608 | tf_op jit(solution)/shard_map/all_to_all | solution.py:149
  159.2 2.6 %copy-start.4 = (bf16[6,512,256]{2,1,0:T(8,128)(2,1)S(1)}, bf16[6,512,256]{2,1,0:T(8,128)(2,1)}, u32[]{:S(2)}) copy-start(bf16[6,512,256]{2,1,0:T(8,128)(2,1)} %copy-done.3) | copy-start | bytes 4718596

commit v4 on v3

--- a/solution.py
+++ b/solution.py
@@ -12,8 +12,9 @@
 SIZES = (2, 4, 4, 2, 2, 4)
 F32 = jnp.float32
 BF16 = jnp.bfloat16
-PARAMS = pltpu.CompilerParams(vmem_limit_bytes=40 * 1024 * 1024)
+PARAMS = pltpu.CompilerParams(vmem_limit_bytes=20 * 1024 * 1024)
 SMEM = pl.BlockSpec(memory_space=pltpu.SMEM)
+ANY = pl.BlockSpec(memory_space=pl.ANY)
 VMEM = pl.BlockSpec(memory_space=pltpu.VMEM)
 
 
@@ -51,12 +52,42 @@
             send_ref[p, g, :, 128:] = right[at, :].astype(BF16)
 
 
-def forward_kernel(at_ref, mine_ref, other_ref, x_ref, *rest):
-    sends, (slope_ref, win_ref, mine_f, other_f, w_f, act) = rest[:8], rest[8:]
-    place, first = at_ref[0], at_ref[1] == 0
+def spread_kernel(x_ref, out_ref, moved, sems):
+    row = lax.broadcasted_iota(jnp.int32, (256, 256), 0)
+    col = lax.broadcasted_iota(jnp.int32, (256, 256), 1)
+    source = (col // 64 % 2) * 128 + (col % 32) * 4 + (col // 128) * 2 + col // 32 % 2
+    pick = jnp.where(row == source, 1.0, 0.0).astype(BF16)
+    for pair in range(NB // 2):
+        cut = slice(pair * 256, pair * 256 + 256)
+        moved[:, cut] = dot(x_ref[:, cut], pick, 1, 0).astype(BF16)
+    copies = [pltpu.make_async_copy(moved, out_ref.at[q], sems.at[q]) for q in range(8)]
+    for copy in copies:
+        copy.start()
+    for copy in copies:
+        copy.wait()
+
+
+def columns_kernel(mine_ref, after_ref, send_ref, mine_f):
+    mine_f[...] = mine_ref[:, :48, :].astype(F32).reshape(32 * 48, 128)
+    for pair in range(NB // 2):
+        for c in range(4):
+            rows = [
+                mine_f[pl.ds((pair * 2 + i) * 8 + k * 4 + c, 32, stride=48), :]
+                for i in range(2)
+                for k in range(2)
+            ]
+            turned = jnp.concatenate(rows, axis=0).T.astype(BF16)
+            for q in range(8):
+                send_ref[q, pair, c * 16 : (c + 1) * 16, :] = turned[q * 16 : (q + 1) * 16]
+
+
+ROOT = 0.7978845608028654
+
+
+def slope_kernel(at_ref, mine_ref, other_ref, x_ref, slope_ref, win_ref, mine_f, other_f, w_f):
+    first = at_ref[1] == 0
     mine_f[...] = mine_ref[:, :48, :].astype(F32).reshape(32 * 48, 128)
     other_f[...] = other_ref[:, :48, :].astype(F32).reshape(32 * 48, 128)
-    root = 0.7978845608028654
     for i in range(NB):
         for k in range(2):
             for c in range(4):
@@ -69,15 +100,10 @@
             win_ref[i, :, c * 128 : (c + 1) * 128] = w
             v = dot(w, x_ref[:, i * 128 : (i + 1) * 128], 0, 1)
             square = v * v
-            th = jnp.tanh(root * (v + 0.044715 * (v * square)))
-            half = 0.5 * (1.0 + th)
-            act[i * 4 + c] = (v * half).astype(BF16).reshape(8, 16, ROWS)
-            slope_ref[i, c * 128 : (c + 1) * 128, :] = half + (0.5 * root) * v * (
+            th = jnp.tanh(ROOT * (v + 0.044715 * (v * square)))
+            slope_ref[i, c * 128 : (c + 1) * 128, :] = 0.5 * (1.0 + th) + (0.5 * ROOT) * v * (
                 1.0 - th * th
             ) * (1.0 + 0.134145 * square)
-    for s in range(8):
-        to = lax.rem(place + s, 8)
-        sends[s][...] = act[:, to]
 
 
 def store_ordered(ref, rows, value):
@@ -85,7 +111,7 @@
         ref[n // 16 * 16 + n % 4 * 4 + n // 4 % 4, rows, :] = value[n]
 
 
-def first_grad_kernel(at_ref, back_ref, slope_ref, x_ref, dpre_ref, keep_ref, send_ref, p_f, o_f):
+def first_grad_kernel(at_ref, back_ref, slope_ref, x_ref, after_ref, dpre_ref, keep_ref, send_ref, p_f, o_f):
     first = at_ref[1] == 0
     for i in range(NB):
         parts = [back_ref[:, i * 4 + a].reshape(128, ROWS) for a in range(4)]
@@ -105,14 +131,28 @@
     store_ordered(send_ref, slice(0, 48), jnp.where(first, one, zero).astype(BF16))
 
 
-def second_grad_kernel(at_ref, *rest):
-    pieces, (c_ref, mixed_ref, keep_ref, send_ref, left, right) = rest[:8], rest[8:]
-    place, first = at_ref[0], at_ref[1] == 0
-    for s in range(8):
-        start = pl.multiple_of(lax.rem(place + 8 - s, 8) * 384, 384)
-        piece = pieces[s][...].reshape(384, ROWS).astype(F32)
-        left[pl.ds(start, 384), :] = piece[:, :128]
-        right[pl.ds(start, 384), :] = piece[:, 128:]
+def second_grad_kernel(
+    at_ref, x_ref, mine_ref, other_ref, c_ref, mixed_ref, keep_ref, send_ref, left, right
+):
+    first = at_ref[1] == 0
+    lane = lax.broadcasted_iota(jnp.int32, (64, 128), 1) < 64
+    zero = jnp.zeros((64, 128), F32)
+    for p in range(8):
+        for pair in range(NB // 2):
+            mine = mine_ref[p, pair].astype(F32)
+            other = other_ref[p, pair].astype(F32)
+            v = None
+            for core in range(2):
+                w = jnp.where(first, mine, other) if core == 0 else jnp.where(first, other, mine)
+                w = jnp.concatenate([jnp.where(lane, w, zero), jnp.where(lane, zero, w)])
+                cut = slice(pair * 256 + core * 128, pair * 256 + core * 128 + 128)
+                part = dot(w.astype(BF16), x_ref[p, :, cut], 1, 1)
+                v = part if v is None else v + part
+            th = jnp.tanh(ROOT * (v + 0.044715 * (v * (v * v))))
+            act = (0.5 * v) * (1.0 + th)
+            start = (p * 3 + pair) * 128
+            left[start : start + 128, :] = act[:, :128]
+            right[start : start + 128, :] = act[:, 128:]
     for j in range(16):
         at = pl.ds(j, 192, stride=16)
         mixed_ref[j * 192 : (j + 1) * 192, :128] = left[at, :].astype(BF16)
@@ -130,12 +170,14 @@
         store_ordered(send_ref, rows, jnp.concatenate(sent, axis=1).astype(BF16))
 
 
-def call(kernel, name, args, outs, scratch):
+def call(kernel, name, args, outs, scratch=(), unread=()):
     return pl.pallas_call(
         kernel,
         name=name,
         out_shape=[jax.ShapeDtypeStruct(shape, dtype) for shape, dtype in outs],
-        in_specs=[SMEM] + [VMEM] * (len(args) - 1),
+        in_specs=[
+            ANY if n in unread else SMEM if arg.ndim == 1 else VMEM for n, arg in enumerate(args)
+        ],
         out_specs=[VMEM] * len(outs),
         scratch_shapes=[pltpu.VMEM(shape, F32 if dtype is F32 else BF16) for shape, dtype in scratch],
         compiler_params=PARAMS,
@@ -145,20 +187,17 @@
     )(*args)
 
 
+def join_kernel(keep_in, got_in, keep_out, got_out, both_ref):
+    both_ref[:, :48, :] = (keep_in[...].astype(F32) + got_in[...].astype(F32)).astype(BF16)
+    both_ref[:, 48:, :] = (keep_out[...].astype(F32) + got_out[...].astype(F32)).astype(BF16)
+
+
 def exchange(value, axis):
     return lax.all_to_all(value, axis, 0, 0, tiled=True)
 
 
 def swap_cores(value):
     return lax.ppermute(value, "core", [(0, 1), (1, 0)])
-
-
-def rotate(value, step):
-    return lax.ppermute(value, MP, [(n, (n + step) % 8) for n in range(8)])
-
-
-def add(first, second):
-    return (first.astype(F32) + second.astype(F32)).astype(BF16)
 
 
 def on_device(tokens, w_in, w_out, cotangent):
@@ -167,43 +206,56 @@
     shard = jnp.concatenate(
         [w_in.transpose(1, 0, 2).reshape(48, 128), w_out.transpose(1, 0, 2).reshape(48, 128)]
     )
+    copies = pl.pallas_call(
+        spread_kernel,
+        name="spread",
+        out_shape=jax.ShapeDtypeStruct((8, ROWS, 768), BF16),
+        in_specs=[VMEM],
+        out_specs=pl.BlockSpec(memory_space=pltpu.HBM),
+        scratch_shapes=[pltpu.VMEM((ROWS, 768), BF16), pltpu.SemaphoreType.DMA((8,))],
+        compiler_params=PARAMS,
+    )(tokens)
+    gathered = exchange(copies, MP)
     along_z = lax.all_gather(shard, ("z_hi", "z_lo"), axis=0, tiled=False)
     mine = lax.all_gather(along_z, "x_hi", axis=0, tiled=False).reshape(32, 96, 128)
     other = swap_cores(mine)
 
-    piece = (24, 16, ROWS)
     half = ((32, 48, 128), BF16)
     block = (NB, 512, ROWS)
+    (column_send,) = call(
+        columns_kernel, "columns", (mine, gathered), [((8, 3, 64, 128), BF16)], [((1536, 128), F32)], (1,)
+    )
+    columns = exchange(column_send, MP)
+    other_columns = swap_cores(columns)
     back_send, wout = call(
         back_kernel, "d_mixed", (at, mine, other, cotangent),
-        [((8,) + piece, BF16), ((NB, 512, 128), BF16)],
+        [((8, 24, 16, ROWS), BF16), ((NB, 512, 128), BF16)],
         [((3072, 128), F32), ((3072, 128), F32)],
     )
     back = exchange(back_send, MP)
-    *act, slope, win = call(
-        forward_kernel, "act", (at, mine, other, tokens),
-        [(piece, BF16)] * 8 + [(block, F32), ((NB, 128, 512), BF16)],
-        [((1536, 128), F32), ((1536, 128), F32), ((4, 128, 128), F32), ((24, 8, 16, ROWS), BF16)],
-    )
-    moved = [act[0]] + [rotate(act[s], s) for s in range(1, 8)]
+    mixed, keep_out, send_out = call(
+        second_grad_kernel, "second_grad", (at, gathered, columns, other_columns, cotangent),
+        [((3072, ROWS), BF16), half, half],
+        [((3072, 128), F32), ((3072, 128), F32)],
+    )
+    got_out = swap_cores(send_out)
+    slope, win = call(
+        slope_kernel, "slope", (at, mine, other, tokens),
+        [(block, F32), ((NB, 128, 512), BF16)],
+        [((1536, 128), F32), ((1536, 128), F32), ((4, 128, 128), F32)],
+    )
     d_pre, keep_in, send_in = call(
-        first_grad_kernel, "first_grad", (at, back, slope, tokens),
+        first_grad_kernel, "first_grad", (at, back, slope, tokens, got_out),
         [(block, BF16), half, half],
         [((4, 128, 128), F32), ((2, 1536, 128), F32)],
-    )
-    half_in = add(keep_in, swap_cores(send_in))
-    got_in = exchange(half_in.reshape(8, 192, 128), ("x_hi", "z_lo"))
-    mixed, keep_out, send_out = call(
-        second_grad_kernel, "second_grad", (at, *moved, cotangent),
-        [((3072, ROWS), BF16), half, half],
-        [((3072, 128), F32), ((3072, 128), F32)],
-    )
-    half_out = add(keep_out, swap_cores(send_out))
-    got_out = exchange(half_out.reshape(8, 192, 128), ("x_hi", "z_lo"))
-    both = jnp.concatenate(
-        [g.astype(F32).sum(axis=0).astype(BF16).reshape(4, 48, 128) for g in (got_in, got_out)],
-        axis=1,
-    )
+        (4,),
+    )
+    got_in = swap_cores(send_in)
+    (both,) = call(
+        join_kernel, "join", (keep_in, got_in, keep_out, got_out), [((32, 96, 128), BF16)]
+    )
+    got = exchange(both.reshape(8, 384, 128), ("x_hi", "z_lo"))
+    both = got.astype(F32).sum(axis=0).astype(BF16).reshape(4, 96, 128)
     total = exchange(both, "z_hi").astype(F32).sum(axis=0) * scale
     grad_in = total[:48].reshape(NB, 2, 512).transpose(1, 0, 2)
     grad_out = total[48:].reshape(NB, 8, 128).transpose(1, 0, 2)

time: 176 us -> 166 us (0.943)
  the two profiles are of different devices: /device:TPU:8 before, /device:TPU:1 now
where the time goes in v4:
time: 166 us; the launch traced here: 164 us
  blocking collectives  67.6 us (41%)
  starting transfers between devices  45.5 us (27%)
  Pallas kernels  20 us (12%)
  local copies, waits for them, and re-layouts  13.5 us (8%)
  waiting for transfers between devices  11.7 us (7%)
  matrix products  3.2 us (2%)
  other arithmetic  1.75 us (1%)
    all_gather x1, blocking collectives, on_device(): along_z = lax.all_gather(shard, ('z_hi', 'z_lo'), axis=0, tiled=False)  32.6 us
    all_to_all x4, starting transfers between devices, exchange(): return lax.all_to_all(value, axis, 0, 0, tiled=True)  27.9 us
    all_to_all x1, blocking collectives, exchange(): return lax.all_to_all(value, axis, 0, 0, tiled=True)  25.9 us
    pallas_call x6, Pallas kernels, call(): pl.pallas_call(kernel, name=name, out_shape=[jax.ShapeDtypeStruct(shape,...  18.1 us
    ppermute x4, starting transfers between devices, swap_cores(): return lax.ppermute(value, 'core', [(0, 1), (1, 0)])  17.6 us
    unnamed x36, local copies, waits for them, and re-layouts  12.2 us
    all_gather x1, blocking collectives, on_device(): lax.all_gather(along_z, 'x_hi', axis=0, tiled=False).reshape(32, 96, 128)  9.11 us
    all_to_all x4, waiting for transfers between devices, exchange(): return lax.all_to_all(value, axis, 0, 0, tiled=True)  8.85 us
  transfers between devices with their start and end apart: 8, of which 5 were waited for; matrix products, arithmetic and copies ran while one was open for 3% of the time, Pallas kernels for 9%

profile of v4, /device:TPU:1, one launch (start us, length us, event | category | flops | bytes accessed | tf_op | source)
XLA Modules:
  0.0 164.0 jit_solution(8518733133546051074)
XLA Ops:
  0.6 0.0 copy-start.1
  0.6 1.0 copy-done.1
  1.6 1.9 %spread.1 = bf16[8,256,768]{2,1,0:T(8,128)(2,1)S(1)} custom-call(bf16[256,768]{1,0:T(8,128)(2,1)S(1)} %copy-done.1), custom_call_target="tpu_custom_call" | custom-call | tf_op jit(solution)/shard_map/spread/pallas_call | solution.py:209
  3.5 0.0 copy-start
  3.5 1.6 copy-done
  5.1 0.0 copy-start.15
  5.1 0.0 copy-start.16
  5.1 6.1 %all-to-all-start = ((bf16[8,256,768]{2,1,0:T(8,128)(2,1)}), bf16[8,256,768]{2,1,0:T(8,128)(2,1)S(1)}, u32[]{:S(2)}, u32[]{:S(2)}) async-start(bf16[8,256,768]{2,1,0:T(8,128)(2,1)} %copy-done), calls=%async_computation | async-start | bytes 6291456 | tf_op jit(solution)/shard_map/all_to_all | solution.py:196
  11.2 0.0 copy-done.15
  11.2 0.0 copy-done.16
  11.3 32.6 %all-gather = bf16[1536,128]{1,0:T(8,128)(2,1)S(1)} all-gather(bf16[96,128]{1,0:T(8,128)(2,1)S(1)} %pad_maximum_fusion), channel_id=2, replica_groups=mesh['x_hi'=2,'z_hi'=4,'z_lo'=4,'core'=2,'x_lo'=2,'y'=4] {'z_hi','z_lo'}, dimensions={0}, use_global_device_ids=true | all-gather | bytes 417792 | tf_op jit(solution)/shard_map/all_gather | solution.py:219
  43.8 9.1 %all-gather.1.mine_ref = bf16[32,96,128]{2,1,0:T(8,128)(2,1)} all-gather(bf16[16,96,128]{2,1,0:T(8,128)(2,1)S(1)} %bitcast.27), channel_id=3, replica_groups=mesh['x_hi'=2,'z_hi'=4,'z_lo'=4,'core'=2,'x_lo'=2,'y'=4] {'x_hi'}, dimensions={0}, use_global_device_ids=true | all-gather | bytes 1179648 | tf_op jit(solution)/shard_map/all_gather | solution.py:220
  52.9 0.0 copy-start.4
  52.9 8.9 %collective-permute-start = (bf16[32,96,128]{2,1,0:T(8,128)(2,1)}, bf16[32,96,128]{2,1,0:T(8,128)(2,1)}, u32[]{:S(2)}, u32[]{:S(2)}) collective-permute-start(bf16[32,96,128]{2,1,0:T(8,128)(2,1)} %all-gather.1.mine_ref), channel_id=1, source_target_pairs={{0,8},{8,0},{1,9},{9,1},{2,10},{10,2},{3,11},{11,3},{4,12},{12,4},... | collective-permute-start | bytes 2359304 | tf_op jit(solution)/shard_map/ppermute | solution.py:200
  61.8 0.0 all-to-all-done.after_ref.x_ref
  61.8 1.5 columns.1
  63.3 0.0 copy-start.6
  63.3 0.7 copy-done.6
  64.0 5.4 %all-to-all-start.1 = ((bf16[8,3,64,128]{3,2,1,0:T(8,128)(2,1)}), bf16[8,3,64,128]{3,2,1,0:T(8,128)(2,1)}, u32[]{:S(2)}, u32[]{:S(2)}) async-start(bf16[8,3,64,128]{3,2,1,0:T(8,128)(2,1)} %copy-done.6), calls=%async_computation.1 | async-start | bytes 786432 | tf_op jit(solution)/shard_map/all_to_all | solution.py:196
  69.4 0.1 pad_add_fusion.at_ref
  69.5 0.0 collective-permute-done.other_ref
  69.5 0.0 copy-done.4
  69.5 4.2 %d_mixed.1 = (bf16[8,24,16,256]{3,2,1,0:T(8,128)(2,1)S(1)}, bf16[6,512,128]{2,1,0:T(8,128)(2,1)S(1)}) custom-call(s32[2]{0:T(128)S(1)} %pad_add_fusion.at_ref, bf16[32,96,128]{2,1,0:T(8,128)(2,1)} %all-gather.1.mine_ref, bf16[32,96,128]{2,1,0:T(8,128)(2,1)} %collective-permute-done.other_ref, bf16[256,768]{1,0:T(8,128)(2,1)S(1)} %copy-done.4), custom_call_target="tpu_custom_call" | custom-call | flops 201326592 | bytes 6000000 | tf_op jit(solution)/shard_map/d_mixed/pallas_call | solution.py:174
  73.8 0.0 copy-start.3
  73.8 1.1 copy-done.3
  74.9 0.0 copy-start.11
  74.9 0.9 copy-done.11
  75.8 1.2 all-to-all-done.1.mine_ref
  77.1 4.3 %all-to-all-start.2 = ((bf16[8,24,16,256]{3,2,1,0:T(8,128)(2,1)}), bf16[8,24,16,256]{3,2,1,0:T(8,128)(2,1)}, u32[]{:S(2)}, u32[]{:S(2)}) async-start(bf16[8,24,16,256]{3,2,1,0:T(8,128)(2,1)} %copy-done.3), calls=%async_computation.2 | async-start | bytes 3145728 | tf_op jit(solution)/shard_map/all_to_all | solution.py:196
  81.4 0.0 copy-start.2
  81.4 3.7 %collective-permute-start.1 = (bf16[8,3,64,128]{3,2,1,0:T(8,128)(2,1)}, bf16[8,3,64,128]{3,2,1,0:T(8,128)(2,1)S(1)}, u32[]{:S(2)}, u32[]{:S(2)}) collective-permute-start(bf16[8,3,64,128]{3,2,1,0:T(8,128)(2,1)} %all-to-all-done.1.mine_ref), channel_id=1, source_target_pairs={{0,8},{8,0},{1,9},{9,1},{2,10},{10,2},{3,11},{11,3},{4,12},{12,4},... | collective-permute-start | bytes 1179656 | tf_op jit(solution)/shard_map/ppermute | solution.py:200
  85.0 1.5 collective-permute-done.1.other_ref
  86.6 1.0 copy-done.5
  87.6 4.7 %second_grad.1 = (bf16[3072,256]{1,0:T(8,128)(2,1)S(1)}, bf16[32,48,128]{2,1,0:T(8,128)(2,1)S(1)}, bf16[32,48,128]{2,1,0:T(8,128)(2,1)}) custom-call(s32[2]{0:T(128)S(1)} %pad_add_fusion.at_ref, bf16[8,256,768]{2,1,0:T(8,128)(2,1)S(1)} %all-to-all-done.after_ref.x_ref, bf16[8,3,64,128]{3,2,1,0:T(8,128)(2,1)} %all-to-all-done.1.mine_ref, ...), custom_call_target="tpu_custom_call" | custom-call | flops 201326592 | bytes 6000000 | tf_op jit(solution)/shard_map/second_grad/pallas_call | solution.py:174
  92.2 1.2 copy-done.7
  93.4 0.7 copy-done.13
  94.2 2.3 %collective-permute-start.2 = (bf16[32,48,128]{2,1,0:T(8,128)(2,1)}, bf16[32,48,128]{2,1,0:T(8,128)(2,1)}, u32[]{:S(2)}, u32[]{:S(2)}) collective-permute-start(bf16[32,48,128]{2,1,0:T(8,128)(2,1)} %get-tuple-element.19), channel_id=1, source_target_pairs={{0,8},{8,0},{1,9},{9,1},{2,10},{10,2},{3,11},{11,3},{4,12},{12,4},... | collective-permute-start | bytes 1179656 | tf_op jit(solution)/shard_map/ppermute | solution.py:200
  96.4 0.0 copy-done.2
  96.5 3.8 %slope.1 = (f32[6,512,256]{2,1,0:T(8,128)S(1)}, bf16[6,128,512]{2,1,0:T(8,128)(2,1)S(1)}) custom-call(s32[2]{0:T(128)S(1)} %pad_add_fusion.at_ref, bf16[32,96,128]{2,1,0:T(8,128)(2,1)} %all-gather.1.mine_ref, bf16[32,96,128]{2,1,0:T(8,128)(2,1)} %collective-permute-done.other_ref, bf16[256,768]{1,0:T(8,128)(2,1)S(1)} %copy-done.2), custom_call_target="tpu_custom_call" | custom-call | flops 201326592 | bytes 6000000 | tf_op jit(solution)/shard_map/slope/pallas_call | solution.py:174
  100.3 0.0 copy-start.12
  100.3 0.9 copy-done.12
  101.2 0.7 all-to-all-done.2.back_ref
  101.9 0.0 collective-permute-done.2.after_ref.got_out
  101.9 2.8 %first_grad.1 = (bf16[6,512,256]{2,1,0:T(8,128)(2,1)S(1)}, bf16[32,48,128]{2,1,0:T(8,128)(2,1)S(1)}, bf16[32,48,128]{2,1,0:T(8,128)(2,1)S(1)}) custom-call(s32[2]{0:T(128)S(1)} %pad_add_fusion.at_ref, bf16[8,24,16,256]{3,2,1,0:T(8,128)(2,1)} %all-to-all-done.2.back_ref, f32[6,512,256]{2,1,0:T(8,128)S(1)} %get-tuple-element.18.slope_ref, ...), custom_call_target="tpu_custom_call" | custom-call | flops 201326592 | bytes 6000000 | tf_op jit(solution)/shard_map/first_grad/pallas_call | solution.py:174
  104.7 0.0 copy-start.9
  104.7 1.1 copy-done.9
  105.8 2.7 %collective-permute-start.3 = (bf16[32,48,128]{2,1,0:T(8,128)(2,1)S(1)}, bf16[32,48,128]{2,1,0:T(8,128)(2,1)S(1)}, u32[]{:S(2)}, u32[]{:S(2)}) collective-permute-start(bf16[32,48,128]{2,1,0:T(8,128)(2,1)S(1)} %get-tuple-element.22), channel_id=1, source_target_pairs={{0,8},{8,0},{1,9},{9,1},{2,10},{10,2},{3,11},{11,3},{4,12},{12,4},... | collective-permute-start | bytes 1179656 | tf_op jit(solution)/shard_map/ppermute | solution.py:200
  108.6 1.3 collective-permute-done.3.got_in
  109.9 0.0 copy-done.14
  109.9 1.2 join.1
  111.1 0.0 copy-start.8
  111.1 25.9 %all_to_all.25 = bf16[8,384,128]{2,1,0:T(8,128)(2,1)S(1)} all-to-all(bf16[8,384,128]{2,1,0:T(8,128)(2,1)S(1)} %bitcast.25), channel_id=1, replica_groups=mesh['x_hi'=2,'z_hi'=4,'z_lo'=4,'core'=2,'x_lo'=2,'y'=4] {'x_hi','z_lo'}, dimensions={0} | all-to-all | bytes 1572864 | tf_op jit(solution)/shard_map/all_to_all | solution.py:196
  137.0 0.8 reduce_sum.21
  137.7 12.1 %all-to-all-start.4 = ((bf16[4,96,128]{2,1,0:T(8,128)(2,1)}), bf16[4,96,128]{2,1,0:T(8,128)(2,1)}, u32[]{:S(2)}, u32[]{:S(2)}) async-start(bf16[4,96,128]{2,1,0:T(8,128)(2,1)} %bitcast.12), calls=%async_computation.4 | async-start | bytes 196608 | tf_op jit(solution)/shard_map/all_to_all | solution.py:196
  149.8 0.0 copy-done.8
  149.8 1.7 %convolution_convert_fusion.1 = bf16[6,128,256]{2,1,0:T(8,128)(2,1)S(1)} fusion(bf16[6,512,128]{2,1,0:T(8,128)(2,1)} %copy-done.11, bf16[6,512,256]{2,1,0:T(8,128)(2,1)S(1)} %bitcast.26), kind=kOutput, calls=%fused_computation.1 | convolution fusion | flops 201523200 | bytes 2752512 | tf_op jit(solution)/shard_map/oet,oen->ton/dot_general | solution.py:263
  151.5 0.9 copy.15
  152.5 0.0 copy-done.10
  152.5 1.5 convolution_convert_fusion
  154.0 0.9 copy.16
  154.9 6.9 %all-to-all-done.4 = bf16[4,96,128]{2,1,0:T(8,128)(2,1)} async-done(((bf16[4,96,128]{2,1,0:T(8,128)(2,1)}), bf16[4,96,128]{2,1,0:T(8,128)(2,1)}, u32[]{:S(2)}, u32[]{:S(2)}) %all-to-all-start.4) | async-done | bytes 98336 | tf_op jit(solution)/shard_map/all_to_all | solution.py:196
  161.8 0.9 convert_reduce_fusion
  162.8 0.6 slice_bitcast_fusion
  163.4 0.6 reshape.46
  (8 shorter events, 0.0 us)
Async XLA Ops:
  0.6 1.0 copy-start.1
  3.5 1.6 copy-start
  5.1 6.1 %copy-start.15 = (bf16[2,6,512]{2,0,1:T(2,128)(2,1)S(1)}, bf16[2,6,512]{2,0,1:T(2,128)(2,1)}, u32[]{:S(2)}) copy-start(bf16[2,6,512]{2,0,1:T(2,128)(2,1)} %param.5) | copy-start | bytes 36868
  5.1 6.1 %copy-start.16 = (bf16[8,6,128]{2,0,1:T(8,128)(2,1)S(1)}, bf16[8,6,128]{2,0,1:T(8,128)(2,1)}, u32[]{:S(2)}) copy-start(bf16[8,6,128]{2,0,1:T(8,128)(2,1)} %param.6) | copy-start | bytes 36868
  5.1 56.7 %all-to-all-start = ((bf16[8,256,768]{2,1,0:T(8,128)(2,1)}), bf16[8,256,768]{2,1,0:T(8,128)(2,1)S(1)}, u32[]{:S(2)}, u32[]{:S(2)}) async-start(bf16[8,256,768]{2,1,0:T(8,128)(2,1)} %copy-done), calls=%async_computation | async-start | bytes 6291456 | tf_op jit(solution)/shard_map/all_to_all | solution.py:196
  52.9 16.6 %copy-start.4 = (bf16[256,768]{1,0:T(8,128)(2,1)S(1)}, bf16[256,768]{1,0:T(8,128)(2,1)}, u32[]{:S(2)}) copy-start(bf16[256,768]{1,0:T(8,128)(2,1)} %c_ref.3) | copy-start | bytes 1179652
  52.9 16.6 %collective-permute-start = (bf16[32,96,128]{2,1,0:T(8,128)(2,1)}, bf16[32,96,128]{2,1,0:T(8,128)(2,1)}, u32[]{:S(2)}, u32[]{:S(2)}) collective-permute-start(bf16[32,96,128]{2,1,0:T(8,128)(2,1)} %all-gather.1.mine_ref), channel_id=1, source_target_pairs={{0,8},{8,0},{1,9},{9,1},{2,10},{10,2},{3,11},{11,3},{4,12},{12,4},... | collective-permute-start | bytes 2359304 | tf_op jit(solution)/shard_map/ppermute | solution.py:200
  63.3 0.7 copy-start.6
  64.0 13.0 %all-to-all-start.1 = ((bf16[8,3,64,128]{3,2,1,0:T(8,128)(2,1)}), bf16[8,3,64,128]{3,2,1,0:T(8,128)(2,1)}, u32[]{:S(2)}, u32[]{:S(2)}) async-start(bf16[8,3,64,128]{3,2,1,0:T(8,128)(2,1)} %copy-done.6), calls=%async_computation.1 | async-start | bytes 786432 | tf_op jit(solution)/shard_map/all_to_all | solution.py:196
  73.8 1.1 copy-start.3
  74.9 0.9 copy-start.11
  77.1 24.8 %all-to-all-start.2 = ((bf16[8,24,16,256]{3,2,1,0:T(8,128)(2,1)}), bf16[8,24,16,256]{3,2,1,0:T(8,128)(2,1)}, u32[]{:S(2)}, u32[]{:S(2)}) async-start(bf16[8,24,16,256]{3,2,1,0:T(8,128)(2,1)} %copy-done.3), calls=%async_computation.2 | async-start | bytes 3145728 | tf_op jit(solution)/shard_map/all_to_all | solution.py:196
  81.4 15.1 %copy-start.2 = (bf16[256,768]{1,0:T(8,128)(2,1)S(1)}, bf16[256,768]{1,0:T(8,128)(2,1)}, u32[]{:S(2)}) copy-start(bf16[256,768]{1,0:T(8,128)(2,1)} %x_ref.5) | copy-start | bytes 1179652
  81.4 5.2 %collective-permute-start.1 = (bf16[8,3,64,128]{3,2,1,0:T(8,128)(2,1)}, bf16[8,3,64,128]{3,2,1,0:T(8,128)(2,1)S(1)}, u32[]{:S(2)}, u32[]{:S(2)}) collective-permute-start(bf16[8,3,64,128]{3,2,1,0:T(8,128)(2,1)} %all-to-all-done.1.mine_ref), channel_id=1, source_target_pairs={{0,8},{8,0},{1,9},{9,1},{2,10},{10,2},{3,11},{11,3},{4,12},{12,4},... | collective-permute-start | bytes 1179656 | tf_op jit(solution)/shard_map/ppermute | solution.py:200
  86.6 1.0 copy-start.5
  92.2 1.2 copy-start.7
  93.4 0.7 copy-start.13
  94.2 7.7 %collective-permute-start.2 = (bf16[32,48,128]{2,1,0:T(8,128)(2,1)}, bf16[32,48,128]{2,1,0:T(8,128)(2,1)}, u32[]{:S(2)}, u32[]{:S(2)}) collective-permute-start(bf16[32,48,128]{2,1,0:T(8,128)(2,1)} %get-tuple-element.19), channel_id=1, source_target_pairs={{0,8},{8,0},{1,9},{9,1},{2,10},{10,2},{3,11},{11,3},{4,12},{12,4},... | collective-permute-start | bytes 1179656 | tf_op jit(solution)/shard_map/ppermute | solution.py:200
  100.3 0.9 copy-start.12
  101.9 8.0 %copy-start.14 = (bf16[32,48,128]{2,1,0:T(8,128)(2,1)S(1)}, bf16[32,48,128]{2,1,0:T(8,128)(2,1)}, u32[]{:S(2)}) copy-start(bf16[32,48,128]{2,1,0:T(8,128)(2,1)} %copy-done.13) | copy-start | bytes 1179652
  104.7 1.1 copy-start.9
  105.8 4.1 %collective-permute-start.3 = (bf16[32,48,128]{2,1,0:T(8,128)(2,1)S(1)}, bf16[32,48,128]{2,1,0:T(8,128)(2,1)S(1)}, u32[]{:S(2)}, u32[]{:S(2)}) collective-permute-start(bf16[32,48,128]{2,1,0:T(8,128)(2,1)S(1)} %get-tuple-element.22), channel_id=1, source_target_pairs={{0,8},{8,0},{1,9},{9,1},{2,10},{10,2},{3,11},{11,3},{4,12},{12,4},... | collective-permute-start | bytes 1179656 | tf_op jit(solution)/shard_map/ppermute | solution.py:200
  111.1 38.8 %copy-start.8 = (bf16[3072,256]{1,0:T(8,128)(2,1)S(1)}, bf16[3072,256]{1,0:T(8,128)(2,1)}, u32[]{:S(2)}) copy-start(bf16[3072,256]{1,0:T(8,128)(2,1)} %copy-done.7) | copy-start | bytes 4718596
  137.7 24.1 %all-to-all-start.4 = ((bf16[4,96,128]{2,1,0:T(8,128)(2,1)}), bf16[4,96,128]{2,1,0:T(8,128)(2,1)}, u32[]{:S(2)}, u32[]{:S(2)}) async-start(bf16[4,96,128]{2,1,0:T(8,128)(2,1)} %bitcast.12), calls=%async_computation.4 | async-start | bytes 196608 | tf_op jit(solution)/shard_map/all_to_all | solution.py:196
  149.8 2.6 %copy-start.10 = (bf16[6,512,256]{2,1,0:T(8,128)(2,1)S(1)}, bf16[6,512,256]{2,1,0:T(8,128)(2,1)}, u32[]{:S(2)}) copy-start(bf16[6,512,256]{2,1,0:T(8,128)(2,1)} %copy-done.9) | copy-start | bytes 4718596

commit v5 on v4

--- a/solution.py
+++ b/solution.py
@@ -52,23 +52,11 @@
             send_ref[p, g, :, 128:] = right[at, :].astype(BF16)
 
 
-def spread_kernel(x_ref, out_ref, moved, sems):
-    row = lax.broadcasted_iota(jnp.int32, (256, 256), 0)
-    col = lax.broadcasted_iota(jnp.int32, (256, 256), 1)
-    source = (col // 64 % 2) * 128 + (col % 32) * 4 + (col // 128) * 2 + col // 32 % 2
-    pick = jnp.where(row == source, 1.0, 0.0).astype(BF16)
-    for pair in range(NB // 2):
-        cut = slice(pair * 256, pair * 256 + 256)
-        moved[:, cut] = dot(x_ref[:, cut], pick, 1, 0).astype(BF16)
-    copies = [pltpu.make_async_copy(moved, out_ref.at[q], sems.at[q]) for q in range(8)]
-    for copy in copies:
-        copy.start()
-    for copy in copies:
-        copy.wait()
-
-
-def columns_kernel(mine_ref, after_ref, send_ref, mine_f):
-    mine_f[...] = mine_ref[:, :48, :].astype(F32).reshape(32 * 48, 128)
+def columns_kernel(mine_ref, after_ref, send_ref, relay_ref, mine_f):
+    for x in range(2):
+        rows = mine_ref[:, x]
+        relay_ref[x * 16 : (x + 1) * 16] = rows
+        mine_f[x * 768 : (x + 1) * 768, :] = rows[:, :48].astype(F32).reshape(768, 128)
     for pair in range(NB // 2):
         for c in range(4):
             rows = [
@@ -135,24 +123,27 @@
     at_ref, x_ref, mine_ref, other_ref, c_ref, mixed_ref, keep_ref, send_ref, left, right
 ):
     first = at_ref[1] == 0
-    lane = lax.broadcasted_iota(jnp.int32, (64, 128), 1) < 64
-    zero = jnp.zeros((64, 128), F32)
+    row = lax.broadcasted_iota(jnp.int32, (256, 256), 0)
+    col = lax.broadcasted_iota(jnp.int32, (256, 256), 1)
+    target = (row // 64 % 2) * 128 + (row % 32) * 4 + (row // 128) * 2 + row // 32 % 2
+    place = jnp.where(col == target, 1.0, 0.0).astype(BF16)
     for p in range(8):
-        for pair in range(NB // 2):
-            mine = mine_ref[p, pair].astype(F32)
-            other = other_ref[p, pair].astype(F32)
-            v = None
-            for core in range(2):
-                w = jnp.where(first, mine, other) if core == 0 else jnp.where(first, other, mine)
-                w = jnp.concatenate([jnp.where(lane, w, zero), jnp.where(lane, zero, w)])
-                cut = slice(pair * 256 + core * 128, pair * 256 + core * 128 + 128)
-                part = dot(w.astype(BF16), x_ref[p, :, cut], 1, 1)
-                v = part if v is None else v + part
+        mine = mine_ref[p].reshape(192, 128).astype(F32)
+        other = other_ref[p].reshape(192, 128).astype(F32)
+        w = jnp.concatenate(
+            [jnp.where(first, mine, other), jnp.where(first, other, mine)], axis=1
+        ).astype(BF16)
+        w = dot(w, place, 1, 0).astype(BF16)
+        for i in range(NB):
+            rows = slice(i // 2 * 64, i // 2 * 64 + 64)
+            v = dot(
+                w[rows, i % 2 * 128 : i % 2 * 128 + 128], x_ref[p, :, i * 128 : (i + 1) * 128], 1, 1
+            )
             th = jnp.tanh(ROOT * (v + 0.044715 * (v * (v * v))))
             act = (0.5 * v) * (1.0 + th)
-            start = (p * 3 + pair) * 128
-            left[start : start + 128, :] = act[:, :128]
-            right[start : start + 128, :] = act[:, 128:]
+            start = (p * NB + i) * 64
+            left[start : start + 64, :] = act[:, :128]
+            right[start : start + 64, :] = act[:, 128:]
     for j in range(16):
         at = pl.ds(j, 192, stride=16)
         mixed_ref[j * 192 : (j + 1) * 192, :128] = left[at, :].astype(BF16)
@@ -206,25 +197,18 @@
     shard = jnp.concatenate(
         [w_in.transpose(1, 0, 2).reshape(48, 128), w_out.transpose(1, 0, 2).reshape(48, 128)]
     )
-    copies = pl.pallas_call(
-        spread_kernel,
-        name="spread",
-        out_shape=jax.ShapeDtypeStruct((8, ROWS, 768), BF16),
-        in_specs=[VMEM],
-        out_specs=pl.BlockSpec(memory_space=pltpu.HBM),
-        scratch_shapes=[pltpu.VMEM((ROWS, 768), BF16), pltpu.SemaphoreType.DMA((8,))],
-        compiler_params=PARAMS,
-    )(tokens)
-    gathered = exchange(copies, MP)
-    along_z = lax.all_gather(shard, ("z_hi", "z_lo"), axis=0, tiled=False)
-    mine = lax.all_gather(along_z, "x_hi", axis=0, tiled=False).reshape(32, 96, 128)
-    other = swap_cores(mine)
+    sent, _ = lax.optimization_barrier((tokens, shard))
+    gathered = exchange(jnp.broadcast_to(sent[None], (8, ROWS, 768)), MP)
+    pair = lax.all_gather(shard, "x_hi", axis=0, tiled=False)
+    along_z = lax.all_gather(pair, ("z_hi", "z_lo"), axis=0, tiled=False)
 
     half = ((32, 48, 128), BF16)
     block = (NB, 512, ROWS)
-    (column_send,) = call(
-        columns_kernel, "columns", (mine, gathered), [((8, 3, 64, 128), BF16)], [((1536, 128), F32)], (1,)
-    )
+    column_send, mine = call(
+        columns_kernel, "columns", (along_z, gathered),
+        [((8, 3, 64, 128), BF16), ((32, 96, 128), BF16)], [((1536, 128), F32)], (1,)
+    )
+    other = swap_cores(mine)
     columns = exchange(column_send, MP)
     other_columns = swap_cores(columns)
     back_send, wout = call(

time: 166 us -> 190 us (1.14)
  blocking collectives: 67.6 us -> 97.1 us
  starting transfers between devices: 45.5 us -> 41.1 us
  Pallas kernels: 20 us -> 16.7 us
    all_gather x2, blocking collectives: 41.7 us -> 72.6 us  [the longest x1 36.8 us: on_device(): pair = lax.all_gather(shard, 'x_hi', axis=0, tiled=False)]
    all_to_all x4, starting transfers between devices: 27.9 us -> 21.9 us  [exchange(): return lax.all_to_all(value, axis, 0, 0, tiled=True)]
    broadcast_in_dim x0 -> x1, local copies, waits for them, and re-layouts: none -> 2.84 us  [on_device(): gathered = exchange(jnp.broadcast_to(sent[None], (8, ROWS, 768)), MP)]
    unnamed x36 -> x34, local copies, waits for them, and re-layouts: 12.2 us -> 9.86 us
  transfers between devices with their start and end apart: 8 -> 8, of which waited for: 5 -> 5; matrix products, arithmetic and copies ran while one was open for 3% -> 3% of each run, Pallas kernels for 9% -> 7%
where the time goes in v5:
time: 190 us; the launch traced here: 188 us
  blocking collectives  97.1 us (51%)
  starting transfers between devices  41.1 us (22%)
  Pallas kernels  16.7 us (9%)
  local copies, waits for them, and re-layouts  14.7 us (8%)
  waiting for transfers between devices  11.9 us (6%)
  matrix products  3.2 us (2%)
  other arithmetic  2.46 us (1%)
    all_gather x1, blocking collectives, on_device(): pair = lax.all_gather(shard, 'x_hi', axis=0, tiled=False)  36.8 us
    all_gather x1, blocking collectives, on_device(): along_z = lax.all_gather(pair, ('z_hi', 'z_lo'), axis=0, tiled=False)  35.8 us
    all_to_all x1, blocking collectives, exchange(): return lax.all_to_all(value, axis, 0, 0, tiled=True)  24.5 us
    all_to_all x4, starting transfers between devices, exchange(): return lax.all_to_all(value, axis, 0, 0, tiled=True)  21.9 us
    ppermute x4, starting transfers between devices, swap_cores(): return lax.ppermute(value, 'core', [(0, 1), (1, 0)])  19.2 us
    pallas_call x6, Pallas kernels, call(): pl.pallas_call(kernel, name=name, out_shape=[jax.ShapeDtypeStruct(shape,...  16.7 us
    unnamed x34, local copies, waits for them, and re-layouts  9.86 us
    all_to_all x4, waiting for transfers between devices, exchange(): return lax.all_to_all(value, axis, 0, 0, tiled=True)  9.03 us
  transfers between devices with their start and end apart: 8, of which 5 were waited for; matrix products, arithmetic and copies ran while one was open for 3% of the time, Pallas kernels for 7%

profile of v5, /device:TPU:1, one launch (start us, length us, event | category | flops | bytes accessed | tf_op | source)
XLA Modules:
  0.0 188.0 jit_solution(14097303987347445830)
XLA Ops:
  0.6 0.7 reshape.36
  1.4 0.7 pad_maximum_fusion
  2.1 2.8 %broadcast_in_dim.2 = bf16[8,256,768]{2,1,0:T(8,128)(2,1)} broadcast(bf16[256,768]{1,0:T(8,128)(2,1)} %x_ref.3), dimensions={1,2} | broadcast | bytes 3538944 | tf_op jit(solution)/shard_map/broadcast_in_dim | solution.py:201
  4.9 5.9 %all-to-all-start = ((bf16[8,256,768]{2,1,0:T(8,128)(2,1)}), bf16[8,256,768]{2,1,0:T(8,128)(2,1)S(1)}, u32[]{:S(2)}, u32[]{:S(2)}) async-start(bf16[8,256,768]{2,1,0:T(8,128)(2,1)} %broadcast_in_dim.2), calls=%async_computation | async-start | bytes 6291456 | tf_op jit(solution)/shard_map/all_to_all | solution.py:187
  10.9 36.8 %all-gather = bf16[192,128]{1,0:T(8,128)(2,1)S(1)} all-gather(bf16[96,128]{1,0:T(8,128)(2,1)S(1)} %pad_maximum_fusion), channel_id=2, replica_groups=mesh['x_hi'=2,'z_hi'=4,'z_lo'=4,'core'=2,'x_lo'=2,'y'=4] {'x_hi'}, dimensions={0}, use_global_device_ids=true | all-gather | bytes 73728 | tf_op jit(solution)/shard_map/all_gather | solution.py:202
  47.6 35.8 %all-gather.1 = bf16[32,96,128]{2,1,0:T(8,128)(2,1)} all-gather(bf16[2,96,128]{2,1,0:T(8,128)(2,1)S(1)} %bitcast.31), channel_id=3, replica_groups=mesh['x_hi'=2,'z_hi'=4,'z_lo'=4,'core'=2,'x_lo'=2,'y'=4] {'z_hi','z_lo'}, dimensions={0}, use_global_device_ids=true | all-gather | bytes 835584 | tf_op jit(solution)/shard_map/all_gather | solution.py:203
  83.5 0.0 all-to-all-done.after_ref.x_ref
  83.5 0.0 copy-start.1
  83.5 1.1 copy-done.1
  84.6 0.0 copy-start.5
  84.6 1.2 columns.1
  85.8 0.0 copy-start.15
  85.8 10.5 %collective-permute-start = (bf16[32,96,128]{2,1,0:T(8,128)(2,1)}, bf16[32,96,128]{2,1,0:T(8,128)(2,1)}, u32[]{:S(2)}, u32[]{:S(2)}) collective-permute-start(bf16[32,96,128]{2,1,0:T(8,128)(2,1)} %get-tuple-element.18.mine_ref), channel_id=1, source_target_pairs={{0,8},{8,0},{1,9},{9,1},{2,10},{10,2},{3,11},{11,3},{4,12},{12,4},... | collective-permute-start | bytes 2359304 | tf_op jit(solution)/shard_map/ppermute | solution.py:191
  96.3 0.0 copy-done.15
  96.3 4.9 %all-to-all-start.1 = ((bf16[8,3,64,128]{3,2,1,0:T(8,128)(2,1)}), bf16[8,3,64,128]{3,2,1,0:T(8,128)(2,1)}, u32[]{:S(2)}, u32[]{:S(2)}) async-start(bf16[8,3,64,128]{3,2,1,0:T(8,128)(2,1)} %copy-done.15), calls=%async_computation.1 | async-start | bytes 786432 | tf_op jit(solution)/shard_map/all_to_all | solution.py:187
  101.2 0.1 pad_add_fusion.at_ref
  101.3 0.0 collective-permute-done.other_ref
  101.3 0.0 copy-done.5
  101.3 4.3 %d_mixed.1 = (bf16[8,24,16,256]{3,2,1,0:T(8,128)(2,1)S(1)}, bf16[6,512,128]{2,1,0:T(8,128)(2,1)S(1)}) custom-call(s32[2]{0:T(128)S(1)} %pad_add_fusion.at_ref, bf16[32,96,128]{2,1,0:T(8,128)(2,1)} %get-tuple-element.18.mine_ref, bf16[32,96,128]{2,1,0:T(8,128)(2,1)} %collective-permute-done.other_ref, bf16[256,768]{1,0:T(8,128)(2,1)S(1)} %copy-done.5), custom_call_target="tpu_custom_call" | custom-call | flops 201326592 | bytes 6000000 | tf_op jit(solution)/shard_map/d_mixed/pallas_call | solution.py:165
  105.6 0.0 copy-start.4
  105.6 1.1 copy-done.4
  106.7 0.0 copy-start.11
  106.7 0.9 copy-done.11
  107.7 1.2 all-to-all-done.1.mine_ref
  108.9 4.3 %all-to-all-start.2 = ((bf16[8,24,16,256]{3,2,1,0:T(8,128)(2,1)}), bf16[8,24,16,256]{3,2,1,0:T(8,128)(2,1)}, u32[]{:S(2)}, u32[]{:S(2)}) async-start(bf16[8,24,16,256]{3,2,1,0:T(8,128)(2,1)} %copy-done.4), calls=%async_computation.2 | async-start | bytes 3145728 | tf_op jit(solution)/shard_map/all_to_all | solution.py:187
  113.2 0.0 copy-start
  113.2 3.7 %collective-permute-start.1 = (bf16[8,3,64,128]{3,2,1,0:T(8,128)(2,1)}, bf16[8,3,64,128]{3,2,1,0:T(8,128)(2,1)S(1)}, u32[]{:S(2)}, u32[]{:S(2)}) collective-permute-start(bf16[8,3,64,128]{3,2,1,0:T(8,128)(2,1)} %all-to-all-done.1.mine_ref), channel_id=1, source_target_pairs={{0,8},{8,0},{1,9},{9,1},{2,10},{10,2},{3,11},{11,3},{4,12},{12,4},... | collective-permute-start | bytes 1179656 | tf_op jit(solution)/shard_map/ppermute | solution.py:191
  116.9 1.5 collective-permute-done.1.other_ref
  118.4 0.0 copy-start.6
  118.4 1.0 copy-done.6
  119.4 4.4 %second_grad.1 = (bf16[3072,256]{1,0:T(8,128)(2,1)S(1)}, bf16[32,48,128]{2,1,0:T(8,128)(2,1)S(1)}, bf16[32,48,128]{2,1,0:T(8,128)(2,1)S(1)}) custom-call(s32[2]{0:T(128)S(1)} %pad_add_fusion.at_ref, bf16[8,256,768]{2,1,0:T(8,128)(2,1)S(1)} %all-to-all-done.after_ref.x_ref, bf16[8,3,64,128]{3,2,1,0:T(8,128)(2,1)} %all-to-all-done.1.mine_ref, ...), custom_call_target="tpu_custom_call" | custom-call | flops 201326592 | bytes 6000000 | tf_op jit(solution)/shard_map/second_grad/pallas_call | solution.py:165
  123.8 0.0 copy-start.7
  123.8 1.2 copy-done.7
  125.0 2.3 %collective-permute-start.2 = (bf16[32,48,128]{2,1,0:T(8,128)(2,1)S(1)}, bf16[32,48,128]{2,1,0:T(8,128)(2,1)S(1)}, u32[]{:S(2)}, u32[]{:S(2)}) collective-permute-start(bf16[32,48,128]{2,1,0:T(8,128)(2,1)S(1)} %get-tuple-element.25), channel_id=1, source_target_pairs={{0,8},{8,0},{1,9},{9,1},{2,10},{10,2},{3,11},{11,3},{4,12},{12,4},... | collective-permute-start | bytes 1179656 | tf_op jit(solution)/shard_map/ppermute | solution.py:191
  127.3 0.0 copy-done
  127.3 3.8 %slope.1 = (f32[6,512,256]{2,1,0:T(8,128)S(1)}, bf16[6,128,512]{2,1,0:T(8,128)(2,1)S(1)}) custom-call(s32[2]{0:T(128)S(1)} %pad_add_fusion.at_ref, bf16[32,96,128]{2,1,0:T(8,128)(2,1)} %get-tuple-element.18.mine_ref, bf16[32,96,128]{2,1,0:T(8,128)(2,1)} %collective-permute-done.other_ref, bf16[256,768]{1,0:T(8,128)(2,1)S(1)} %copy-done), custom_call_target="tpu_custom_call" | custom-call | flops 201326592 | bytes 6000000 | tf_op jit(solution)/shard_map/slope/pallas_call | solution.py:165
  131.1 0.0 copy-done.13
  131.2 0.0 copy-start.12
  131.2 0.9 copy-done.12
  132.0 0.0 collective-permute-done.2.after_ref.got_out
  132.1 0.7 copy-done.2
  132.8 0.9 all-to-all-done.2.back_ref
  133.7 1.0 copy-done.3
  134.7 2.8 %first_grad.1 = (bf16[6,512,256]{2,1,0:T(8,128)(2,1)S(1)}, bf16[32,48,128]{2,1,0:T(8,128)(2,1)S(1)}, bf16[32,48,128]{2,1,0:T(8,128)(2,1)S(1)}) custom-call(s32[2]{0:T(128)S(1)} %pad_add_fusion.at_ref, bf16[8,24,16,256]{3,2,1,0:T(8,128)(2,1)} %all-to-all-done.2.back_ref, f32[6,512,256]{2,1,0:T(8,128)S(1)} %get-tuple-element.24.slope_ref, ...), custom_call_target="tpu_custom_call" | custom-call | flops 201326592 | bytes 6000000 | tf_op jit(solution)/shard_map/first_grad/pallas_call | solution.py:165
  137.5 0.0 copy-start.9
  137.5 2.8 %collective-permute-start.3 = (bf16[32,48,128]{2,1,0:T(8,128)(2,1)S(1)}, bf16[32,48,128]{2,1,0:T(8,128)(2,1)S(1)}, u32[]{:S(2)}, u32[]{:S(2)}) collective-permute-start(bf16[32,48,128]{2,1,0:T(8,128)(2,1)S(1)} %get-tuple-element.28), channel_id=1, source_target_pairs={{0,8},{8,0},{1,9},{9,1},{2,10},{10,2},{3,11},{11,3},{4,12},{12,4},... | collective-permute-start | bytes 1179656 | tf_op jit(solution)/shard_map/ppermute | solution.py:191
  140.2 1.3 collective-permute-done.3.got_in
  141.6 0.0 copy-done.14
  141.6 0.2 join.1
  141.8 0.0 copy-done.9
  141.8 0.0 copy-start.8
  141.8 24.5 %all_to_all.25 = bf16[8,384,128]{2,1,0:T(8,128)(2,1)S(1)} all-to-all(bf16[8,384,128]{2,1,0:T(8,128)(2,1)S(1)} %bitcast.26), channel_id=1, replica_groups=mesh['x_hi'=2,'z_hi'=4,'z_lo'=4,'core'=2,'x_lo'=2,'y'=4] {'x_hi','z_lo'}, dimensions={0} | all-to-all | bytes 1572864 | tf_op jit(solution)/shard_map/all_to_all | solution.py:187
  166.3 0.8 reduce_sum.21
  167.1 6.8 %all-to-all-start.4 = ((bf16[4,96,128]{2,1,0:T(8,128)(2,1)}), bf16[4,96,128]{2,1,0:T(8,128)(2,1)}, u32[]{:S(2)}, u32[]{:S(2)}) async-start(bf16[4,96,128]{2,1,0:T(8,128)(2,1)} %bitcast.13), calls=%async_computation.4 | async-start | bytes 196608 | tf_op jit(solution)/shard_map/all_to_all | solution.py:187
  173.8 0.0 copy-done.8
  173.8 1.7 convolution_convert_fusion.1
  175.5 0.9 copy.15
  176.5 0.0 copy-done.10
  176.5 1.5 convolution_convert_fusion
  178.0 0.9 copy.16
  178.9 6.9 %all-to-all-done.4 = bf16[4,96,128]{2,1,0:T(8,128)(2,1)} async-done(((bf16[4,96,128]{2,1,0:T(8,128)(2,1)}), bf16[4,96,128]{2,1,0:T(8,128)(2,1)}, u32[]{:S(2)}, u32[]{:S(2)}) %all-to-all-start.4) | async-done | bytes 98336 | tf_op jit(solution)/shard_map/all_to_all | solution.py:187
  185.9 0.9 convert_reduce_fusion
  186.8 0.6 slice_bitcast_fusion
  187.4 0.6 reshape.43
  (6 shorter events, 0.0 us)
Async XLA Ops:
  4.9 78.6 %all-to-all-start = ((bf16[8,256,768]{2,1,0:T(8,128)(2,1)}), bf16[8,256,768]{2,1,0:T(8,128)(2,1)S(1)}, u32[]{:S(2)}, u32[]{:S(2)}) async-start(bf16[8,256,768]{2,1,0:T(8,128)(2,1)} %broadcast_in_dim.2), calls=%async_computation | async-start | bytes 6291456 | tf_op jit(solution)/shard_map/all_to_all | solution.py:187
  83.5 1.1 copy-start.1
  84.6 16.7 %copy-start.5 = (bf16[256,768]{1,0:T(8,128)(2,1)S(1)}, bf16[256,768]{1,0:T(8,128)(2,1)}, u32[]{:S(2)}) copy-start(bf16[256,768]{1,0:T(8,128)(2,1)} %c_ref.3) | copy-start | bytes 1179652
  85.8 10.5 %copy-start.15 = (bf16[8,3,64,128]{3,2,1,0:T(8,128)(2,1)}, bf16[8,3,64,128]{3,2,1,0:T(8,128)(2,1)S(1)}, u32[]{:S(2)}) copy-start(bf16[8,3,64,128]{3,2,1,0:T(8,128)(2,1)S(1)} %get-tuple-element.20) | copy-start | bytes 1179652
  85.8 15.5 %collective-permute-start = (bf16[32,96,128]{2,1,0:T(8,128)(2,1)}, bf16[32,96,128]{2,1,0:T(8,128)(2,1)}, u32[]{:S(2)}, u32[]{:S(2)}) collective-permute-start(bf16[32,96,128]{2,1,0:T(8,128)(2,1)} %get-tuple-element.18.mine_ref), channel_id=1, source_target_pairs={{0,8},{8,0},{1,9},{9,1},{2,10},{10,2},{3,11},{11,3},{4,12},{12,4},... | collective-permute-start | bytes 2359304 | tf_op jit(solution)/shard_map/ppermute | solution.py:191
  96.3 12.5 %all-to-all-start.1 = ((bf16[8,3,64,128]{3,2,1,0:T(8,128)(2,1)}), bf16[8,3,64,128]{3,2,1,0:T(8,128)(2,1)}, u32[]{:S(2)}, u32[]{:S(2)}) async-start(bf16[8,3,64,128]{3,2,1,0:T(8,128)(2,1)} %copy-done.15), calls=%async_computation.1 | async-start | bytes 786432 | tf_op jit(solution)/shard_map/all_to_all | solution.py:187
  105.6 1.1 copy-start.4
  106.7 0.9 copy-start.11
  108.9 24.8 %all-to-all-start.2 = ((bf16[8,24,16,256]{3,2,1,0:T(8,128)(2,1)}), bf16[8,24,16,256]{3,2,1,0:T(8,128)(2,1)}, u32[]{:S(2)}, u32[]{:S(2)}) async-start(bf16[8,24,16,256]{3,2,1,0:T(8,128)(2,1)} %copy-done.4), calls=%async_computation.2 | async-start | bytes 3145728 | tf_op jit(solution)/shard_map/all_to_all | solution.py:187
  113.2 14.2 %copy-start = (bf16[256,768]{1,0:T(8,128)(2,1)S(1)}, bf16[256,768]{1,0:T(8,128)(2,1)}, u32[]{:S(2)}) copy-start(bf16[256,768]{1,0:T(8,128)(2,1)} %x_ref.3) | copy-start | bytes 1179652
  113.2 5.2 %collective-permute-start.1 = (bf16[8,3,64,128]{3,2,1,0:T(8,128)(2,1)}, bf16[8,3,64,128]{3,2,1,0:T(8,128)(2,1)S(1)}, u32[]{:S(2)}, u32[]{:S(2)}) collective-permute-start(bf16[8,3,64,128]{3,2,1,0:T(8,128)(2,1)} %all-to-all-done.1.mine_ref), channel_id=1, source_target_pairs={{0,8},{8,0},{1,9},{9,1},{2,10},{10,2},{3,11},{11,3},{4,12},{12,4},... | collective-permute-start | bytes 1179656 | tf_op jit(solution)/shard_map/ppermute | solution.py:191
  118.4 1.0 copy-start.6
  123.8 1.2 copy-start.7
  125.0 6.1 %copy-start.13 = (bf16[32,48,128]{2,1,0:T(8,128)(2,1)}, bf16[32,48,128]{2,1,0:T(8,128)(2,1)S(1)}, u32[]{:S(2)}) copy-start(bf16[32,48,128]{2,1,0:T(8,128)(2,1)S(1)} %get-tuple-element.29.keep_out) | copy-start | bytes 1179652
  125.0 7.0 %collective-permute-start.2 = (bf16[32,48,128]{2,1,0:T(8,128)(2,1)S(1)}, bf16[32,48,128]{2,1,0:T(8,128)(2,1)S(1)}, u32[]{:S(2)}, u32[]{:S(2)}) collective-permute-start(bf16[32,48,128]{2,1,0:T(8,128)(2,1)S(1)} %get-tuple-element.25), channel_id=1, source_target_pairs={{0,8},{8,0},{1,9},{9,1},{2,10},{10,2},{3,11},{11,3},{4,12},{12,4},... | collective-permute-start | bytes 1179656 | tf_op jit(solution)/shard_map/ppermute | solution.py:191
  131.2 0.9 copy-start.12
  132.1 0.7 copy-start.2
  133.7 1.0 copy-start.3
  134.7 6.9 %copy-start.14 = (bf16[32,48,128]{2,1,0:T(8,128)(2,1)S(1)}, bf16[32,48,128]{2,1,0:T(8,128)(2,1)}, u32[]{:S(2)}) copy-start(bf16[32,48,128]{2,1,0:T(8,128)(2,1)} %copy-done.13) | copy-start | bytes 1179652
  137.5 4.3 %copy-start.9 = (bf16[6,512,256]{2,1,0:T(8,128)(2,1)}, bf16[6,512,256]{2,1,0:T(8,128)(2,1)S(1)}, u32[]{:S(2)}) copy-start(bf16[6,512,256]{2,1,0:T(8,128)(2,1)S(1)} %get-tuple-element.26) | copy-start | bytes 4718596
  137.5 4.1 %collective-permute-start.3 = (bf16[32,48,128]{2,1,0:T(8,128)(2,1)S(1)}, bf16[32,48,128]{2,1,0:T(8,128)(2,1)S(1)}, u32[]{:S(2)}, u32[]{:S(2)}) collective-permute-start(bf16[32,48,128]{2,1,0:T(8,128)(2,1)S(1)} %get-tuple-element.28), channel_id=1, source_target_pairs={{0,8},{8,0},{1,9},{9,1},{2,10},{10,2},{3,11},{11,3},{4,12},{12,4},... | collective-permute-start | bytes 1179656 | tf_op jit(solution)/shard_map/ppermute | solution.py:191
  141.8 32.1 %copy-start.8 = (bf16[3072,256]{1,0:T(8,128)(2,1)S(1)}, bf16[3072,256]{1,0:T(8,128)(2,1)}, u32[]{:S(2)}) copy-start(bf16[3072,256]{1,0:T(8,128)(2,1)} %copy-done.7) | copy-start | bytes 4718596
  167.1 18.8 %all-to-all-start.4 = ((bf16[4,96,128]{2,1,0:T(8,128)(2,1)}), bf16[4,96,128]{2,1,0:T(8,128)(2,1)}, u32[]{:S(2)}, u32[]{:S(2)}) async-start(bf16[4,96,128]{2,1,0:T(8,128)(2,1)} %bitcast.13), calls=%async_computation.4 | async-start | bytes 196608 | tf_op jit(solution)/shard_map/all_to_all | solution.py:187
  173.8 2.6 %copy-start.10 = (bf16[6,512,256]{2,1,0:T(8,128)(2,1)S(1)}, bf16[6,512,256]{2,1,0:T(8,128)(2,1)}, u32[]{:S(2)}) copy-start(bf16[6,512,256]{2,1,0:T(8,128)(2,1)} %copy-done.9) | copy-start | bytes 4718596

commit v6 on v5

v6 whole, which is shorter than its diff:
```python
import jax
import jax.numpy as jnp
from jax import lax
from jax.experimental import pallas as pl
from jax.experimental.pallas import tpu as pltpu
from jax.sharding import Mesh, PartitionSpec as P

NB = 6
ROWS = 256
DP = ("x_hi", "z", "core")
MP = ("x_lo", "y")
SIZES = (2, 16, 2, 2, 4)
F32 = jnp.float32
BF16 = jnp.bfloat16
PARAMS = pltpu.CompilerParams(vmem_limit_bytes=20 * 1024 * 1024)
SMEM = pl.BlockSpec(memory_space=pltpu.SMEM)
ANY = pl.BlockSpec(memory_space=pl.ANY)
VMEM = pl.BlockSpec(memory_space=pltpu.VMEM)


def dot(lhs, rhs, lhs_dim, rhs_dim):
    return lax.dot_general(
        lhs, rhs, (((lhs_dim,), (rhs_dim,)), ((), ())), preferred_element_type=F32
    )


def halves(value, step):
    return value[:, step * 128 : (step + 1) * 128]


def shard_rows(ref, rows):
    return jnp.concatenate([ref[:, 0, rows], ref[:, 1, rows]], axis=0).astype(F32)


def second_factor(first, mine_ref, other_ref, pair):
    rows = slice(48 + pair * 16, 48 + pair * 16 + 16)
    mine, other = shard_rows(mine_ref, rows), shard_rows(other_ref, rows)
    zero = jnp.where(first, mine, other)
    one = jnp.where(first, other, mine)
    return [
        jnp.stack([zero[:, cut], one[:, cut]], axis=1).reshape(512, 128).astype(BF16)
        for cut in (slice(0, 8), slice(8, 16))
    ]


def back_kernel(at_ref, mine_ref, other_ref, c_ref, send_ref, left, right):
    first = at_ref[1] == 0
    for pair in range(NB // 2):
        for k, w in enumerate(second_factor(first, mine_ref, other_ref, pair)):
            o = pair * 2 + k
            d = dot(w, c_ref[:, o * 128 : (o + 1) * 128], 1, 1)
            left[o * 512 : (o + 1) * 512, :] = d[:, :128]
            right[o * 512 : (o + 1) * 512, :] = d[:, 128:]
    for p in range(8):
        for g in range(24):
            at = pl.ds(p * 24 + g, 16, stride=192)
            send_ref[p, g, :, :128] = left[at, :].astype(BF16)
            send_ref[p, g, :, 128:] = right[at, :].astype(BF16)


def columns_kernel(mine_ref, send_ref, mine_f):
    mine_f[...] = shard_rows(mine_ref, slice(0, 48)).reshape(32 * 48, 128)
    for pair in range(NB // 2):
        for c in range(4):
            rows = [
                mine_f[pl.ds((pair * 2 + i) * 8 + k * 4 + c, 32, stride=48), :]
                for i in range(2)
                for k in range(2)
            ]
            turned = jnp.concatenate(rows, axis=0).T.astype(BF16)
            for q in range(8):
                send_ref[q, pair, c * 16 : (c + 1) * 16, :] = turned[q * 16 : (q + 1) * 16]


ROOT = 0.7978845608028654


def first_grad_kernel(
    at_ref, mine_ref, other_ref, x_ref, back_ref, after_ref, gx_ref, keep_ref, send_ref,
    mine_f, other_f, w_f, p_f, o_f,
):
    first = at_ref[1] == 0
    mine_f[...] = shard_rows(mine_ref, slice(0, 48)).reshape(32 * 48, 128)
    other_f[...] = shard_rows(other_ref, slice(0, 48)).reshape(32 * 48, 128)
    for i in range(NB):
        for k in range(2):
            for c in range(4):
                at = pl.ds(i * 8 + k * 4 + c, 32, stride=48)
                mine, other = mine_f[at, :], other_f[at, :]
                w_f[c, pl.ds(k, 32, stride=4), :] = jnp.where(first, mine, other)
                w_f[c, pl.ds(2 + k, 32, stride=4), :] = jnp.where(first, other, mine)
        x = x_ref[:, i * 128 : (i + 1) * 128].T
        gx = None
        for c in range(4):
            w = w_f[c].astype(BF16)
            v = dot(w, x, 0, 0)
            square = v * v
            th = jnp.tanh(ROOT * (v + 0.044715 * (v * square)))
            slope = 0.5 * (1.0 + th) + (0.5 * ROOT) * v * (1.0 - th * th) * (1.0 + 0.134145 * square)
            d = (back_ref[:, i * 4 + c].reshape(128, ROWS).astype(F32) * slope).astype(BF16)
            part = dot(w, d, 1, 0)
            gx = part if gx is None else gx + part
            p_f[c] = dot(x, d, 1, 1)
            for core in range(2):
                for k in range(2):
                    o_f[core, pl.ds(i * 8 + k * 4 + c, 32, stride=48), :] = p_f[
                        c, pl.ds(core * 2 + k, 32, stride=4), :
                    ]
        gx_ref[:, i * 128 : (i + 1) * 128] = gx.T.astype(BF16)
    zero = o_f[0].reshape(32, 48, 128)
    one = o_f[1].reshape(32, 48, 128)
    keep_ref[...] = jnp.where(first, zero, one).astype(BF16)
    send_ref[...] = jnp.where(first, one, zero).astype(BF16)


def second_grad_kernel(
    at_ref, x_ref, mine_ref, other_ref, c_ref, wmine_ref, wother_ref, out_ref, keep_ref,
    send_ref, mixed_ref, left, right,
):
    first = at_ref[1] == 0
    row = lax.broadcasted_iota(jnp.int32, (256, 256), 0)
    col = lax.broadcasted_iota(jnp.int32, (256, 256), 1)
    target = (row // 64 % 2) * 128 + (row % 32) * 4 + (row // 128) * 2 + row // 32 % 2
    place = jnp.where(col == target, 1.0, 0.0).astype(BF16)
    for p in range(8):
        mine = mine_ref[p].reshape(192, 128).astype(F32)
        other = other_ref[p].reshape(192, 128).astype(F32)
        w = jnp.concatenate(
            [jnp.where(first, mine, other), jnp.where(first, other, mine)], axis=1
        ).astype(BF16)
        w = dot(w, place, 1, 0).astype(BF16)
        for i in range(NB):
            rows = slice(i // 2 * 64, i // 2 * 64 + 64)
            v = dot(
                w[rows, i % 2 * 128 : i % 2 * 128 + 128], x_ref[p, :, i * 128 : (i + 1) * 128], 1, 1
            )
            th = jnp.tanh(ROOT * (v + 0.044715 * (v * (v * v))))
            act = (0.5 * v) * (1.0 + th)
            start = (p * NB + i) * 64
            left[start : start + 64, :] = act[:, :128]
            right[start : start + 64, :] = act[:, 128:]
    for j in range(16):
        at = pl.ds(j, 192, stride=16)
        mixed_ref[j * 192 : (j + 1) * 192, :128] = left[at, :].astype(BF16)
        mixed_ref[j * 192 : (j + 1) * 192, 128:] = right[at, :].astype(BF16)
    for pair in range(NB // 2):
        kept, sent = [], []
        wout = second_factor(first, wmine_ref, wother_ref, pair)
        for k in range(2):
            o = pair * 2 + k
            m = mixed_ref[o * 512 : (o + 1) * 512, :]
            out_ref[:, o * 128 : (o + 1) * 128] = dot(m, wout[k], 0, 0).astype(BF16)
            g = dot(m, c_ref[:, o * 128 : (o + 1) * 128], 1, 0).reshape(32, 2, 8, 128)
            kept.append(jnp.where(first, g[:, 0], g[:, 1]))
            sent.append(jnp.where(first, g[:, 1], g[:, 0]))
        rows = slice(pair * 16, pair * 16 + 16)
        keep_ref[:, rows, :] = jnp.concatenate(kept, axis=1).astype(BF16)
        send_ref[:, rows, :] = jnp.concatenate(sent, axis=1).astype(BF16)


def call(kernel, name, args, outs, scratch=(), unread=()):
    return pl.pallas_call(
        kernel,
        name=name,
        out_shape=[jax.ShapeDtypeStruct(shape, dtype) for shape, dtype in outs],
        in_specs=[
            ANY if n in unread else SMEM if arg.ndim == 1 else VMEM for n, arg in enumerate(args)
        ],
        out_specs=[VMEM] * len(outs),
        scratch_shapes=[pltpu.VMEM(shape, F32 if dtype is F32 else BF16) for shape, dtype in scratch],
        compiler_params=PARAMS,
        cost_estimate=pl.CostEstimate(
            flops=2 * 256 * 128 * 512 * 6, bytes_accessed=6_000_000, transcendentals=0
        ),
    )(*args)


def join_kernel(at_ref, keep_in, got_in, keep_out, got_out, both_ref):
    for n in range(32):
        place = lax.rem(n % 4 + 2 * at_ref[1], 4)
        to = n // 16 * 16 + place * 4 + n // 4 % 4
        both_ref[to, :48, :] = (keep_in[n].astype(F32) + got_in[n].astype(F32)).astype(BF16)
        both_ref[to, 48:, :] = (keep_out[n].astype(F32) + got_out[n].astype(F32)).astype(BF16)


def part_kernel(got_ref, part_ref):
    total = got_ref[0].astype(F32)
    for n in range(1, 8):
        total = total + got_ref[n].astype(F32)
    part_ref[...] = total.astype(BF16)


def total_kernel(got_ref, in_ref, out_ref):
    total = got_ref[0].astype(F32)
    for n in range(1, 4):
        total = total + got_ref[n].astype(F32)
    total = total * (1.0 / 128.0)
    out_ref[...] = total[48:].reshape(NB, 8, 128)
    for i in range(NB):
        for k in range(2):
            for c in range(4):
                row = i * 8 + k * 4 + c
                in_ref[i, k : k + 1, c * 128 : (c + 1) * 128] = total[row : row + 1]


NEAR = [
    [x * 32 + (run * 4 + 2 * core + n) % 16 * 2 + core for x in range(2) for n in range(4)]
    for core in range(2)
    for run in range(4)
]
FAR = [
    [x * 32 + (run * 4 + n) * 2 + core for run in range(4)]
    for x in range(2)
    for n in range(4)
    for core in range(2)
]


def exchange(value, axis, groups=None):
    return lax.all_to_all(value, axis, 0, 0, axis_index_groups=groups, tiled=True)


def swap_cores(value):
    return lax.ppermute(value, "core", [(0, 1), (1, 0)])


def on_device(tokens, w_in, w_out, cotangent):
    at = jnp.stack([lax.axis_index(MP), lax.axis_index("core")]).astype(jnp.int32)
    shard = jnp.concatenate(
        [w_in.transpose(1, 0, 2).reshape(48, 128), w_out.transpose(1, 0, 2).reshape(48, 128)]
    )
    pair = lax.all_gather(shard, "x_hi", axis=0, tiled=False)
    sent, pair = lax.optimization_barrier((tokens, pair))
    gathered = exchange(jnp.broadcast_to(sent[None], (8, ROWS, 768)), MP)
    mine = lax.all_gather(pair, "z", axis=0, tiled=False)
    other = swap_cores(mine)

    half = ((32, 48, 128), BF16)
    (column_send,) = call(
        columns_kernel, "columns", (mine,), [((8, 3, 64, 128), BF16)], [((1536, 128), F32)]
    )
    column_send, gathered = lax.optimization_barrier((column_send, gathered))
    columns = exchange(column_send, MP)
    other_columns = swap_cores(columns)
    (back_send,) = call(
        back_kernel, "d_mixed", (at, mine, other, cotangent),
        [((8, 24, 16, ROWS), BF16)],
        [((3072, 128), F32), ((3072, 128), F32)],
    )
    back = exchange(back_send, MP)
    output, keep_out, send_out = call(
        second_grad_kernel, "second_grad",
        (at, gathered, columns, other_columns, cotangent, mine, other),
        [((ROWS, 768), BF16), half, half],
        [((3072, ROWS), BF16), ((3072, 128), F32), ((3072, 128), F32)],
    )
    got_out = swap_cores(send_out)
    grad_tokens, keep_in, send_in = call(
        first_grad_kernel, "first_grad", (at, mine, other, tokens, back, got_out),
        [((ROWS, 768), BF16), half, half],
        [((1536, 128), F32)] * 2 + [((4, 128, 128), F32)] * 2 + [((2, 1536, 128), F32)],
        (5,),
    )
    got_in = swap_cores(send_in)
    (both,) = call(
        join_kernel, "join", (at, keep_in, got_in, keep_out, got_out), [((32, 96, 128), BF16)]
    )
    near = exchange(both.reshape(8, 4, 96, 128), DP, NEAR)
    (part,) = call(part_kernel, "part", (near,), [((4, 96, 128), BF16)])
    grad_in, grad_out = call(
        total_kernel, "total", (exchange(part, DP, FAR),),
        [((NB, 2, 512), F32), ((NB, 8, 128), F32)],
    )
    grad_in, grad_out = grad_in.transpose(1, 0, 2), grad_out.transpose(1, 0, 2)
    return (output, grad_tokens, grad_in, grad_out)


def solution(mesh):
    fine = Mesh(mesh.devices.reshape(SIZES), DP + MP)
    placed = (P(DP, MP), P(DP, MP, None), P(DP, MP, None), P(DP, MP))
    return jax.shard_map(
        on_device,
        mesh=fine,
        in_specs=placed,
        out_specs=(P(DP, MP), P(DP, MP), P(DP, MP, None), P(DP, MP, None)),
        check_vma=False,
    )
```

time: 190 us -> 155 us (0.82)
  blocking collectives: 97.1 us -> 81.3 us
  starting transfers between devices: 41.1 us -> 31.5 us
  local copies, waits for them, and re-layouts: 14.7 us -> 8.25 us
  Pallas kernels: 16.7 us -> 20.2 us
  matrix products: 3.2 us -> 0 us
  waiting for transfers between devices: 11.9 us -> 9.54 us
    all_gather x1, blocking collectives: 36.8 us -> 5.43 us  [on_device(): pair = lax.all_gather(shard, 'x_hi', axis=0, tiled=False)]
    all_to_all x1 -> x2, blocking collectives: 24.5 us -> 40.2 us  [exchange(): lax.all_to_all(value, axis, 0, 0, axis_index_groups=groups, tiled=True)]
    all_to_all x4 -> x3, starting transfers between devices: 21.9 us -> 14.8 us  [exchange(): lax.all_to_all(value, axis, 0, 0, axis_index_groups=groups, tiled=True)]
    unnamed x34 -> x16, local copies, waits for them, and re-layouts: 9.86 us -> 4.64 us
    pallas_call x6 -> x7, Pallas kernels: 16.7 us -> 20.2 us  [call(): pl.pallas_call(kernel, name=name, out_shape=[jax.ShapeDtypeStruct(shape,...]
    dot_general x2 -> x0, matrix products: 3.2 us -> none  [the longest x1 1.7 us: on_device(): jnp.einsum('oet,oen->ton', mixed.reshape(block), wout, preferred_element_...]
    ppermute x4, starting transfers between devices: 19.2 us -> 16.7 us  [swap_cores(): return lax.ppermute(value, 'core', [(0, 1), (1, 0)])]
    all_to_all x4 -> x3, waiting for transfers between devices: 9.03 us -> 6.67 us  [exchange(): lax.all_to_all(value, axis, 0, 0, axis_index_groups=groups, tiled=True)]
  transfers between devices with their start and end apart: 8 -> 7, of which waited for: 5 -> 4; matrix products, arithmetic and copies ran while one was open for 3% -> 0% of each run, Pallas kernels for 7% -> 7%
where the time goes in v6:
time: 155 us; the launch traced here: 152 us
  blocking collectives  81.3 us (52%)
  starting transfers between devices  31.5 us (20%)
  Pallas kernels  20.2 us (13%)
  waiting for transfers between devices  9.54 us (6%)
  local copies, waits for them, and re-layouts  8.25 us (5%)
    all_to_all x2, blocking collectives, exchange(): lax.all_to_all(value, axis, 0, 0, axis_index_groups=groups, tiled=True)  40.2 us
    all_gather x1, blocking collectives, on_device(): mine = lax.all_gather(pair, 'z', axis=0, tiled=False)  35.6 us
    pallas_call x7, Pallas kernels, call(): pl.pallas_call(kernel, name=name, out_shape=[jax.ShapeDtypeStruct(shape,...  20.2 us
    ppermute x4, starting transfers between devices, swap_cores(): return lax.ppermute(value, 'core', [(0, 1), (1, 0)])  16.7 us
    all_to_all x3, starting transfers between devices, exchange(): lax.all_to_all(value, axis, 0, 0, axis_index_groups=groups, tiled=True)  14.8 us
    all_to_all x3, waiting for transfers between devices, exchange(): lax.all_to_all(value, axis, 0, 0, axis_index_groups=groups, tiled=True)  6.67 us
    all_gather x1, blocking collectives, on_device(): pair = lax.all_gather(shard, 'x_hi', axis=0, tiled=False)  5.43 us
    unnamed x16, local copies, waits for them, and re-layouts  4.64 us
  transfers between devices with their start and end apart: 7, of which 4 were waited for; matrix products, arithmetic and copies ran while one was open for 0% of the time, Pallas kernels for 7%

profile of v6, /device:TPU:1, one launch (start us, length us, event | category | flops | bytes accessed | tf_op | source)
XLA Modules:
  0.0 152.3 jit_solution(2675570379047252862)
XLA Ops:
  0.6 0.7 reshape.18
  1.4 0.7 pad_maximum_fusion
  2.1 5.4 %all-gather = bf16[192,128]{1,0:T(8,128)(2,1)S(1)} all-gather(bf16[96,128]{1,0:T(8,128)(2,1)S(1)} %pad_maximum_fusion), channel_id=2, replica_groups=mesh['x_hi'=2,'z'=16,'core'=2,'x_lo'=2,'y'=4] {'x_hi'}, dimensions={0}, use_global_device_ids=true | all-gather | bytes 73728 | tf_op jit(solution)/shard_map/all_gather | solution.py:232
  7.5 2.9 %broadcast_in_dim.2 = bf16[8,256,768]{2,1,0:T(8,128)(2,1)} broadcast(bf16[256,768]{1,0:T(8,128)(2,1)} %x_ref.1), dimensions={1,2} | broadcast | bytes 3538944 | tf_op jit(solution)/shard_map/broadcast_in_dim | solution.py:234
  10.4 0.0 copy-start.4
  10.4 5.5 %all-to-all-start = ((bf16[8,256,768]{2,1,0:T(8,128)(2,1)}), bf16[8,256,768]{2,1,0:T(8,128)(2,1)}, u32[]{:S(2)}, u32[]{:S(2)}) async-start(bf16[8,256,768]{2,1,0:T(8,128)(2,1)} %broadcast_in_dim.2), calls=%async_computation | async-start | bytes 6291456 | tf_op jit(solution)/shard_map/all_to_all | solution.py:220
  15.9 35.6 %all-gather.1 = bf16[32,96,128]{2,1,0:T(8,128)(2,1)S(1)} all-gather(bf16[2,96,128]{2,1,0:T(8,128)(2,1)S(1)} %bitcast.17), channel_id=3, replica_groups=mesh['x_hi'=2,'z'=16,'core'=2,'x_lo'=2,'y'=4] {'z'}, dimensions={0}, use_global_device_ids=true | all-gather | bytes 835584 | tf_op jit(solution)/shard_map/all_gather | solution.py:235
  51.5 8.4 %collective-permute-start.1 = (bf16[16,2,96,128]{3,2,1,0:T(8,128)(2,1)S(1)}, bf16[16,2,96,128]{3,2,1,0:T(8,128)(2,1)S(1)}, u32[]{:S(2)}, u32[]{:S(2)}) collective-permute-start(bf16[16,2,96,128]{3,2,1,0:T(8,128)(2,1)S(1)} %bitcast.11), channel_id=1, source_target_pairs={{0,8},{8,0},{1,9},{9,1},{2,10},{10,2},{3,11},{11,3},{4,12},{12,4},... | collective-permute-start | bytes 2359304 | tf_op jit(solution)/shard_map/ppermute | solution.py:224
  59.9 1.1 columns.1
  61.0 0.0 all-to-all-done.x_ref
  61.0 5.1 %all-to-all-start.1 = ((bf16[8,3,64,128]{3,2,1,0:T(8,128)(2,1)}), bf16[8,3,64,128]{3,2,1,0:T(8,128)(2,1)S(1)}, u32[]{:S(2)}, u32[]{:S(2)}) async-start(bf16[8,3,64,128]{3,2,1,0:T(8,128)(2,1)} %columns.1), calls=%async_computation.1 | async-start | bytes 786432 | tf_op jit(solution)/shard_map/all_to_all | solution.py:220
  66.1 0.1 pad_add_fusion.at_ref
  66.2 0.0 collective-permute-done.1.wother_ref.other_ref
  66.2 0.0 copy-done.4
  66.2 3.4 %d_mixed.1 = bf16[8,24,16,256]{3,2,1,0:T(8,128)(2,1)S(1)} custom-call(s32[2]{0:T(128)S(1)} %pad_add_fusion.at_ref, bf16[16,2,96,128]{3,2,1,0:T(8,128)(2,1)S(1)} %bitcast.13, bf16[16,2,96,128]{3,2,1,0:T(8,128)(2,1)S(1)} %collective-permute-done.1.wother_ref.other_ref, bf16[256,768]{1,0:T(8,128)(2,1)S(1)} %copy-done.4), custom_call_target="tpu_custom_call" | custom-call | flops 201326592 | bytes 6000000 | tf_op jit(solution)/shard_map/d_mixed/pallas_call | solution.py:162
  69.6 0.0 copy-start
  69.6 1.1 copy-done
  70.8 2.9 %all-to-all-done.1.mine_ref = bf16[8,3,64,128]{3,2,1,0:T(8,128)(2,1)S(1)} async-done(((bf16[8,3,64,128]{3,2,1,0:T(8,128)(2,1)}), bf16[8,3,64,128]{3,2,1,0:T(8,128)(2,1)S(1)}, u32[]{:S(2)}, u32[]{:S(2)}) %all-to-all-start.1) | async-done | bytes 393248 | tf_op jit(solution)/shard_map/all_to_all | solution.py:220
  73.6 0.0 copy-start.2
  73.6 0.7 copy-done.2
  74.4 4.1 %all-to-all-start.2 = ((bf16[8,24,16,256]{3,2,1,0:T(8,128)(2,1)}), bf16[8,24,16,256]{3,2,1,0:T(8,128)(2,1)S(1)}, u32[]{:S(2)}, u32[]{:S(2)}) async-start(bf16[8,24,16,256]{3,2,1,0:T(8,128)(2,1)} %copy-done), calls=%async_computation.2 | async-start | bytes 3145728 | tf_op jit(solution)/shard_map/all_to_all | solution.py:220
  78.5 0.0 copy-start.1
  78.5 3.2 %collective-permute-start = (bf16[8,3,64,128]{3,2,1,0:T(8,128)(2,1)}, bf16[8,3,64,128]{3,2,1,0:T(8,128)(2,1)S(1)}, u32[]{:S(2)}, u32[]{:S(2)}) collective-permute-start(bf16[8,3,64,128]{3,2,1,0:T(8,128)(2,1)} %copy-done.2), channel_id=1, source_target_pairs={{0,8},{8,0},{1,9},{9,1},{2,10},{10,2},{3,11},{11,3},{4,12},{12,4},... | collective-permute-start | bytes 1179656 | tf_op jit(solution)/shard_map/ppermute | solution.py:224
  81.7 1.5 %collective-permute-done.other_ref = bf16[8,3,64,128]{3,2,1,0:T(8,128)(2,1)S(1)} collective-permute-done((bf16[8,3,64,128]{3,2,1,0:T(8,128)(2,1)}, bf16[8,3,64,128]{3,2,1,0:T(8,128)(2,1)S(1)}, u32[]{:S(2)}, u32[]{:S(2)}) %collective-permute-start) | collective-permute-done | bytes 393248 | tf_op jit(solution)/shard_map/ppermute | solution.py:224
  83.2 0.0 copy-start.3
  83.2 1.0 copy-done.3
  84.2 0.0 copy-start.5
  84.2 1.0 copy-done.5
  85.2 6.8 %second_grad.1 = (bf16[256,768]{1,0:T(8,128)(2,1)}, bf16[32,48,128]{2,1,0:T(8,128)(2,1)S(1)}, bf16[32,48,128]{2,1,0:T(8,128)(2,1)}) custom-call(s32[2]{0:T(128)S(1)} %pad_add_fusion.at_ref, bf16[8,256,768]{2,1,0:T(8,128)(2,1)} %all-to-all-done.x_ref, bf16[8,3,64,128]{3,2,1,0:T(8,128)(2,1)S(1)} %copy-done.3, ...), custom_call_target="tpu_custom_call" | custom-call | flops 201326592 | bytes 6000000 | tf_op jit(solution)/shard_map/second_grad/pallas_call | solution.py:162
  92.0 0.0 copy-start.6
  92.0 0.7 copy-done.6
  92.7 2.4 %collective-permute-start.2 = (bf16[32,48,128]{2,1,0:T(8,128)(2,1)}, bf16[32,48,128]{2,1,0:T(8,128)(2,1)}, u32[]{:S(2)}, u32[]{:S(2)}) collective-permute-start(bf16[32,48,128]{2,1,0:T(8,128)(2,1)} %get-tuple-element.21), channel_id=1, source_target_pairs={{0,8},{8,0},{1,9},{9,1},{2,10},{10,2},{3,11},{11,3},{4,12},{12,4},... | collective-permute-start | bytes 1179656 | tf_op jit(solution)/shard_map/ppermute | solution.py:224
  95.2 3.8 %all-to-all-done.2.back_ref = bf16[8,24,16,256]{3,2,1,0:T(8,128)(2,1)S(1)} async-done(((bf16[8,24,16,256]{3,2,1,0:T(8,128)(2,1)}), bf16[8,24,16,256]{3,2,1,0:T(8,128)(2,1)S(1)}, u32[]{:S(2)}, u32[]{:S(2)}) %all-to-all-start.2) | async-done | bytes 1572896 | tf_op jit(solution)/shard_map/all_to_all | solution.py:220
  99.0 0.0 copy-start.7
  99.0 0.0 collective-permute-done.2.after_ref.got_out
  99.0 0.0 copy-done.1
  99.0 7.0 %first_grad.1 = (bf16[256,768]{1,0:T(8,128)(2,1)}, bf16[32,48,128]{2,1,0:T(8,128)(2,1)S(1)}, bf16[32,48,128]{2,1,0:T(8,128)(2,1)S(1)}) custom-call(s32[2]{0:T(128)S(1)} %pad_add_fusion.at_ref, bf16[16,2,96,128]{3,2,1,0:T(8,128)(2,1)S(1)} %bitcast.15, bf16[16,2,96,128]{3,2,1,0:T(8,128)(2,1)S(1)} %collective-permute-done.1.wother_ref.other_ref, ...), custom_call_target="tpu_custom_call" | custom-call | flops 201326592 | bytes 6000000 | tf_op jit(solution)/shard_map/first_grad/pallas_call | solution.py:162
  106.0 2.8 %collective-permute-start.3 = (bf16[32,48,128]{2,1,0:T(8,128)(2,1)S(1)}, bf16[32,48,128]{2,1,0:T(8,128)(2,1)S(1)}, u32[]{:S(2)}, u32[]{:S(2)}) collective-permute-start(bf16[32,48,128]{2,1,0:T(8,128)(2,1)S(1)} %get-tuple-element.24), channel_id=1, source_target_pairs={{0,8},{8,0},{1,9},{9,1},{2,10},{10,2},{3,11},{11,3},{4,12},{12,4},... | collective-permute-start | bytes 1179656 | tf_op jit(solution)/shard_map/ppermute | solution.py:224
  108.8 1.3 collective-permute-done.3.got_in
  110.1 0.0 copy-done.7
  110.1 1.2 join.1
  111.3 22.1 %all_to_all.25.got_ref = bf16[8,4,96,128]{3,2,1,0:T(8,128)(2,1)S(1)} all-to-all(bf16[8,4,96,128]{3,2,1,0:T(8,128)(2,1)S(1)} %bitcast.16), channel_id=1, replica_groups={{0,16,32,48,256,272,288,304},{64,80,96,112,320,336,352,368},{128,144,16..., dimensions={0} | all-to-all | bytes 1572864 | tf_op jit(solution)/shard_map/all_to_all | solution.py:220
  133.5 0.1 part.1
  133.6 18.1 %all_to_all.26.got_ref = bf16[4,96,128]{2,1,0:T(8,128)(2,1)S(1)} all-to-all(bf16[4,96,128]{2,1,0:T(8,128)(2,1)S(1)} %part.1), channel_id=1, replica_groups={{0,64,128,192},{8,72,136,200},{16,80,144,208},{24,88,152,216},{32,96,16..., dimensions={0} | all-to-all | bytes 196608 | tf_op jit(solution)/shard_map/all_to_all | solution.py:220
  151.6 0.6 total.1
Async XLA Ops:
  10.4 55.8 %copy-start.4 = (bf16[256,768]{1,0:T(8,128)(2,1)S(1)}, bf16[256,768]{1,0:T(8,128)(2,1)}, u32[]{:S(2)}) copy-start(bf16[256,768]{1,0:T(8,128)(2,1)} %c_ref.3) | copy-start | bytes 1179652
  10.4 50.6 %all-to-all-start = ((bf16[8,256,768]{2,1,0:T(8,128)(2,1)}), bf16[8,256,768]{2,1,0:T(8,128)(2,1)}, u32[]{:S(2)}, u32[]{:S(2)}) async-start(bf16[8,256,768]{2,1,0:T(8,128)(2,1)} %broadcast_in_dim.2), calls=%async_computation | async-start | bytes 6291456 | tf_op jit(solution)/shard_map/all_to_all | solution.py:220
  51.5 14.7 %collective-permute-start.1 = (bf16[16,2,96,128]{3,2,1,0:T(8,128)(2,1)S(1)}, bf16[16,2,96,128]{3,2,1,0:T(8,128)(2,1)S(1)}, u32[]{:S(2)}, u32[]{:S(2)}) collective-permute-start(bf16[16,2,96,128]{3,2,1,0:T(8,128)(2,1)S(1)} %bitcast.11), channel_id=1, source_target_pairs={{0,8},{8,0},{1,9},{9,1},{2,10},{10,2},{3,11},{11,3},{4,12},{12,4},... | collective-permute-start | bytes 2359304 | tf_op jit(solution)/shard_map/ppermute | solution.py:224
  61.0 12.7 %all-to-all-start.1 = ((bf16[8,3,64,128]{3,2,1,0:T(8,128)(2,1)}), bf16[8,3,64,128]{3,2,1,0:T(8,128)(2,1)S(1)}, u32[]{:S(2)}, u32[]{:S(2)}) async-start(bf16[8,3,64,128]{3,2,1,0:T(8,128)(2,1)} %columns.1), calls=%async_computation.1 | async-start | bytes 786432 | tf_op jit(solution)/shard_map/all_to_all | solution.py:220
  69.6 1.2 copy-start
  73.6 0.7 copy-start.2
  74.4 24.6 %all-to-all-start.2 = ((bf16[8,24,16,256]{3,2,1,0:T(8,128)(2,1)}), bf16[8,24,16,256]{3,2,1,0:T(8,128)(2,1)S(1)}, u32[]{:S(2)}, u32[]{:S(2)}) async-start(bf16[8,24,16,256]{3,2,1,0:T(8,128)(2,1)} %copy-done), calls=%async_computation.2 | async-start | bytes 3145728 | tf_op jit(solution)/shard_map/all_to_all | solution.py:220
  78.5 20.5 %copy-start.1 = (bf16[256,768]{1,0:T(8,128)(2,1)S(1)}, bf16[256,768]{1,0:T(8,128)(2,1)}, u32[]{:S(2)}) copy-start(bf16[256,768]{1,0:T(8,128)(2,1)} %x_ref.1) | copy-start | bytes 1179652
  78.5 4.7 %collective-permute-start = (bf16[8,3,64,128]{3,2,1,0:T(8,128)(2,1)}, bf16[8,3,64,128]{3,2,1,0:T(8,128)(2,1)S(1)}, u32[]{:S(2)}, u32[]{:S(2)}) collective-permute-start(bf16[8,3,64,128]{3,2,1,0:T(8,128)(2,1)} %copy-done.2), channel_id=1, source_target_pairs={{0,8},{8,0},{1,9},{9,1},{2,10},{10,2},{3,11},{11,3},{4,12},{12,4},... | collective-permute-start | bytes 1179656 | tf_op jit(solution)/shard_map/ppermute | solution.py:224
  83.2 1.0 copy-start.3
  84.2 1.0 copy-start.5
  92.0 0.7 copy-start.6
  92.7 6.3 %collective-permute-start.2 = (bf16[32,48,128]{2,1,0:T(8,128)(2,1)}, bf16[32,48,128]{2,1,0:T(8,128)(2,1)}, u32[]{:S(2)}, u32[]{:S(2)}) collective-permute-start(bf16[32,48,128]{2,1,0:T(8,128)(2,1)} %get-tuple-element.21), channel_id=1, source_target_pairs={{0,8},{8,0},{1,9},{9,1},{2,10},{10,2},{3,11},{11,3},{4,12},{12,4},... | collective-permute-start | bytes 1179656 | tf_op jit(solution)/shard_map/ppermute | solution.py:224
  99.0 11.1 %copy-start.7 = (bf16[32,48,128]{2,1,0:T(8,128)(2,1)S(1)}, bf16[32,48,128]{2,1,0:T(8,128)(2,1)}, u32[]{:S(2)}) copy-start(bf16[32,48,128]{2,1,0:T(8,128)(2,1)} %copy-done.6) | copy-start | bytes 1179652
  106.0 4.1 %collective-permute-start.3 = (bf16[32,48,128]{2,1,0:T(8,128)(2,1)S(1)}, bf16[32,48,128]{2,1,0:T(8,128)(2,1)S(1)}, u32[]{:S(2)}, u32[]{:S(2)}) collective-permute-start(bf16[32,48,128]{2,1,0:T(8,128)(2,1)S(1)} %get-tuple-element.24), channel_id=1, source_target_pairs={{0,8},{8,0},{1,9},{9,1},{2,10},{10,2},{3,11},{11,3},{4,12},{12,4},... | collective-permute-start | bytes 1179656 | tf_op jit(solution)/shard_map/ppermute | solution.py:224

commit v7 on v6

v7 whole, which is shorter than its diff:
```python
import jax
import jax.numpy as jnp
from jax import lax
from jax.experimental import pallas as pl
from jax.experimental.pallas import tpu as pltpu
from jax.sharding import Mesh, PartitionSpec as P

NB = 6
ROWS = 256
DP = ("x_hi", "z", "core")
MP = ("x_lo", "y")
SIZES = (2, 16, 2, 2, 4)
F32 = jnp.float32
BF16 = jnp.bfloat16
PARAMS = pltpu.CompilerParams(vmem_limit_bytes=20 * 1024 * 1024)
SMEM = pl.BlockSpec(memory_space=pltpu.SMEM)
ANY = pl.BlockSpec(memory_space=pl.ANY)
VMEM = pl.BlockSpec(memory_space=pltpu.VMEM)


def dot(lhs, rhs, lhs_dim, rhs_dim):
    return lax.dot_general(
        lhs, rhs, (((lhs_dim,), (rhs_dim,)), ((), ())), preferred_element_type=F32
    )


def halves(value, step):
    return value[:, step * 128 : (step + 1) * 128]


def start_kernel(win_ref, wout_ref, x_ref, shard_ref, copies_ref, sems):
    copies = [pltpu.make_async_copy(x_ref, copies_ref.at[q], sems.at[q]) for q in range(8)]
    for copy in copies:
        copy.start()
    rows = []
    for i in range(NB):
        w = win_ref[i].astype(F32)
        rows += [w[k : k + 1, c * 128 : (c + 1) * 128] for k in range(2) for c in range(4)]
    shard_ref[:48, :] = jnp.concatenate(rows).astype(BF16)
    shard_ref[48:, :] = wout_ref[...].astype(F32).reshape(48, 128).astype(BF16)
    for copy in copies:
        copy.wait()


def shard_rows(ref, rows):
    return jnp.concatenate([ref[:, 0, rows], ref[:, 1, rows]], axis=0).astype(F32)


def second_factor(first, mine_ref, other_ref, pair):
    rows = slice(48 + pair * 16, 48 + pair * 16 + 16)
    mine, other = shard_rows(mine_ref, rows), shard_rows(other_ref, rows)
    zero = jnp.where(first, mine, other)
    one = jnp.where(first, other, mine)
    return [
        jnp.stack([zero[:, cut], one[:, cut]], axis=1).reshape(512, 128).astype(BF16)
        for cut in (slice(0, 8), slice(8, 16))
    ]


def back_kernel(at_ref, mine_ref, other_ref, c_ref, send_ref, wide):
    first = at_ref[1] == 0
    for pair in range(NB // 2):
        for k, w in enumerate(second_factor(first, mine_ref, other_ref, pair)):
            o = pair * 2 + k
            d = dot(w, c_ref[:, o * 128 : (o + 1) * 128], 1, 1).reshape(8, 64, ROWS)
            for n in range(8):
                at = o * 512 + n * 64
                wide[at // 192, at % 192 : at % 192 + 64, :] = d[n]
    for p in range(8):
        for n in range(2):
            cut = slice(n * 128, n * 128 + 128)
            part = jnp.swapaxes(wide[:, p * 24 : (p + 1) * 24, cut], 0, 1)
            send_ref[p, :, :, cut] = part.astype(BF16)


def first_rows(ref, i):
    return jnp.swapaxes(shard_rows(ref, slice(i * 8, i * 8 + 8)), 0, 1)


def columns_kernel(mine_ref, send_ref):
    for pair in range(NB // 2):
        blocks = [first_rows(mine_ref, pair * 2), first_rows(mine_ref, pair * 2 + 1)]
        for c in range(4):
            rows = [blocks[i][k * 4 + c] for i in range(2) for k in range(2)]
            turned = jnp.concatenate(rows, axis=0).T.astype(BF16)
            for q in range(8):
                send_ref[q, pair, c * 16 : (c + 1) * 16, :] = turned[q * 16 : (q + 1) * 16]


ROOT = 0.7978845608028654


def first_grad_kernel(
    at_ref, mine_ref, other_ref, x_ref, back_ref, after_ref, gx_ref, keep_ref, send_ref
):
    first = at_ref[1] == 0
    row = lax.broadcasted_iota(jnp.int32, (128, 128), 0)
    col = lax.broadcasted_iota(jnp.int32, (128, 128), 1)
    pick = jnp.where(col == row % 32 * 4 + row // 32, 1.0, 0.0).astype(BF16)
    kept, sent = [], []
    for i in range(NB):
        mine, other = first_rows(mine_ref, i), first_rows(other_ref, i)
        zero, one = jnp.where(first, mine, other), jnp.where(first, other, mine)
        x = dot(pick, x_ref[:, i * 128 : (i + 1) * 128], 1, 1).astype(BF16)
        w = jnp.concatenate(
            [jnp.concatenate([zero[c], zero[4 + c], one[c], one[4 + c]]) for c in range(4)], axis=1
        ).astype(BF16)
        v = dot(w, x, 0, 0)
        square = v * v
        th = jnp.tanh(ROOT * (v + 0.044715 * (v * square)))
        slope = 0.5 * (1.0 + th) + (0.5 * ROOT) * v * (1.0 - th * th) * (1.0 + 0.134145 * square)
        back = jnp.concatenate([back_ref[:, i * 4 + c].reshape(128, ROWS) for c in range(4)])
        d = (back.astype(F32) * slope).astype(BF16)
        gx = dot(w, d, 1, 0)
        grad = dot(x, d, 1, 1).reshape(4, 32, 512)
        grads = [grad[:, :, c * 128 : (c + 1) * 128] for c in range(4)]
        gx_ref[:, i * 128 : (i + 1) * 128] = dot(gx.astype(BF16), pick, 0, 0).astype(BF16)
        by_core = [
            jnp.swapaxes(jnp.stack([grads[c][core * 2 + k] for k in range(2) for c in range(4)]), 0, 1)
            for core in range(2)
        ]
        kept.append(jnp.where(first, by_core[0], by_core[1]))
        sent.append(jnp.where(first, by_core[1], by_core[0]))
        if i % 2:
            rows = slice(i * 8 - 8, i * 8 + 8)
            keep_ref[:, rows, :] = jnp.concatenate(kept, axis=1).astype(BF16)
            send_ref[:, rows, :] = jnp.concatenate(sent, axis=1).astype(BF16)
            kept, sent = [], []


def second_grad_kernel(
    at_ref, x_ref, mine_ref, other_ref, c_ref, wmine_ref, wother_ref, out_ref, keep_ref,
    send_ref, mixed_ref, wide,
):
    first = at_ref[1] == 0
    row = lax.broadcasted_iota(jnp.int32, (256, 256), 0)
    col = lax.broadcasted_iota(jnp.int32, (256, 256), 1)
    target = (row // 64 % 2) * 128 + (row % 32) * 4 + (row // 128) * 2 + row // 32 % 2
    place = jnp.where(col == target, 1.0, 0.0).astype(BF16)
    for p in range(8):
        mine = mine_ref[p].reshape(192, 128).astype(F32)
        other = other_ref[p].reshape(192, 128).astype(F32)
        w = jnp.concatenate(
            [jnp.where(first, mine, other), jnp.where(first, other, mine)], axis=1
        ).astype(BF16)
        w = dot(w, place, 1, 0).astype(BF16)
        for i in range(NB):
            rows = slice(i // 2 * 64, i // 2 * 64 + 64)
            v = dot(
                w[rows, i % 2 * 128 : i % 2 * 128 + 128], x_ref[p, :, i * 128 : (i + 1) * 128], 1, 1
            )
            th = jnp.tanh(ROOT * (v + 0.044715 * (v * (v * v))))
            act = (0.5 * v) * (1.0 + th)
            start = (p * NB + i) * 4
            wide[start : start + 4] = act.reshape(4, 16, ROWS)
    for g in range(0, 192, 16):
        for n in range(2):
            cut = slice(n * 128, n * 128 + 128)
            part = jnp.swapaxes(wide[g : g + 16, :, cut], 0, 1).astype(BF16)
            for j in range(16):
                mixed_ref[j * 192 + g : j * 192 + g + 16, cut] = part[j]
    for pair in range(NB // 2):
        kept, sent = [], []
        wout = second_factor(first, wmine_ref, wother_ref, pair)
        for k in range(2):
            o = pair * 2 + k
            m = mixed_ref[o * 512 : (o + 1) * 512, :]
            out_ref[:, o * 128 : (o + 1) * 128] = dot(m, wout[k], 0, 0).astype(BF16)
            g = dot(m, c_ref[:, o * 128 : (o + 1) * 128], 1, 0).reshape(32, 2, 8, 128)
            kept.append(jnp.where(first, g[:, 0], g[:, 1]))
            sent.append(jnp.where(first, g[:, 1], g[:, 0]))
        rows = slice(pair * 16, pair * 16 + 16)
        keep_ref[:, rows, :] = jnp.concatenate(kept, axis=1).astype(BF16)
        send_ref[:, rows, :] = jnp.concatenate(sent, axis=1).astype(BF16)


def call(kernel, name, args, outs, scratch=(), unread=()):
    return pl.pallas_call(
        kernel,
        name=name,
        out_shape=[jax.ShapeDtypeStruct(shape, dtype) for shape, dtype in outs],
        in_specs=[
            ANY if n in unread else SMEM if arg.ndim == 1 else VMEM for n, arg in enumerate(args)
        ],
        out_specs=[VMEM] * len(outs),
        scratch_shapes=[pltpu.VMEM(shape, F32 if dtype is F32 else BF16) for shape, dtype in scratch],
        compiler_params=PARAMS,
        cost_estimate=pl.CostEstimate(
            flops=2 * 256 * 128 * 512 * 6, bytes_accessed=6_000_000, transcendentals=0
        ),
    )(*args)


def join_kernel(at_ref, keep_in, got_in, keep_out, got_out, both_ref):
    for n in range(32):
        place = lax.rem(n % RUN + RUN // 2 * at_ref[1], RUN)
        to = n // 16 * 16 + place * RUNS + n % 16 // RUN
        both_ref[to, :48, :] = (keep_in[n].astype(F32) + got_in[n].astype(F32)).astype(BF16)
        both_ref[to, 48:, :] = (keep_out[n].astype(F32) + got_out[n].astype(F32)).astype(BF16)


def part_kernel(got_ref, part_ref):
    total = got_ref[0].astype(F32)
    for n in range(1, 2 * RUN):
        total = total + got_ref[n].astype(F32)
    part_ref[...] = total.astype(BF16)


def total_kernel(got_ref, in_ref, out_ref):
    total = got_ref[0].astype(F32)
    for n in range(1, RUNS):
        total = total + got_ref[n].astype(F32)
    total = total * (1.0 / 128.0)
    out_ref[...] = total[48:].reshape(NB, 8, 128)
    for i in range(NB):
        for k in range(2):
            for c in range(4):
                row = i * 8 + k * 4 + c
                in_ref[i, k : k + 1, c * 128 : (c + 1) * 128] = total[row : row + 1]


RUN = 2
RUNS = 16 // RUN
NEAR = [
    [x * 32 + (run * RUN + RUN // 2 * core + n) % 16 * 2 + core for x in range(2) for n in range(RUN)]
    for core in range(2)
    for run in range(RUNS)
]
FAR = [
    [x * 32 + (run * RUN + n) * 2 + core for run in range(RUNS)]
    for x in range(2)
    for n in range(RUN)
    for core in range(2)
]


def exchange(value, axis, groups=None):
    return lax.all_to_all(value, axis, 0, 0, axis_index_groups=groups, tiled=True)


def swap_cores(value):
    return lax.ppermute(value, "core", [(0, 1), (1, 0)])


def on_device(tokens, w_in, w_out, cotangent):
    at = jnp.stack([lax.axis_index(MP), lax.axis_index("core")]).astype(jnp.int32)
    shard, copies = pl.pallas_call(
        start_kernel,
        name="start",
        out_shape=[
            jax.ShapeDtypeStruct((96, 128), BF16),
            jax.ShapeDtypeStruct((8, ROWS, 768), BF16),
        ],
        in_specs=[VMEM, VMEM, VMEM],
        out_specs=[VMEM, ANY],
        scratch_shapes=[pltpu.SemaphoreType.DMA((8,))],
        compiler_params=pltpu.CompilerParams(vmem_limit_bytes=62 * 1024 * 1024),
    )(w_in.transpose(1, 0, 2), w_out.transpose(1, 0, 2), tokens)
    pair = lax.all_gather(shard, "x_hi", axis=0, tiled=False)
    copies, pair = lax.optimization_barrier((copies, pair))
    gathered = exchange(copies, MP)
    mine = lax.all_gather(pair, "z", axis=0, tiled=False)
    other = swap_cores(mine)

    half = ((32, 48, 128), BF16)
    (column_send,) = call(
        columns_kernel, "columns", (mine,), [((8, 3, 64, 128), BF16)]
    )
    column_send, gathered = lax.optimization_barrier((column_send, gathered))
    columns = exchange(column_send, MP)
    other_columns = swap_cores(columns)
    (back_send,) = call(
        back_kernel, "d_mixed", (at, mine, other, cotangent),
        [((8, 24, 16, ROWS), BF16)], [((16, 192, ROWS), F32)],
    )
    back = exchange(back_send, MP)
    output, keep_out, send_out = call(
        second_grad_kernel, "second_grad",
        (at, gathered, columns, other_columns, cotangent, mine, other),
        [((ROWS, 768), BF16), half, half],
        [((3072, ROWS), BF16), ((192, 16, ROWS), F32)],
    )
    got_out = swap_cores(send_out)
    grad_tokens, keep_in, send_in = call(
        first_grad_kernel, "first_grad", (at, mine, other, tokens, back, got_out),
        [((ROWS, 768), BF16), half, half], (), (5,),
    )
    got_in = swap_cores(send_in)
    (both,) = call(
        join_kernel, "join", (at, keep_in, got_in, keep_out, got_out), [((32, 96, 128), BF16)]
    )
    near = exchange(both.reshape(2 * RUN, RUNS, 96, 128), DP, NEAR)
    (part,) = call(part_kernel, "part", (near,), [((RUNS, 96, 128), BF16)])
    grad_in, grad_out = call(
        total_kernel, "total", (exchange(part, DP, FAR),),
        [((NB, 2, 512), F32), ((NB, 8, 128), F32)],
    )
    grad_in, grad_out = grad_in.transpose(1, 0, 2), grad_out.transpose(1, 0, 2)
    return (output, grad_tokens, grad_in, grad_out)


def solution(mesh):
    fine = Mesh(mesh.devices.reshape(SIZES), DP + MP)
    placed = (P(DP, MP), P(DP, MP, None), P(DP, MP, None), P(DP, MP))
    return jax.shard_map(
        on_device,
        mesh=fine,
        in_specs=placed,
        out_specs=(P(DP, MP), P(DP, MP), P(DP, MP, None), P(DP, MP, None)),
        check_vma=False,
    )
```

time: 155 us -> 152 us (0.981); the launches traced: 152 us -> 152 us
  local copies, waits for them, and re-layouts: 8.25 us -> 3.89 us
  waiting for transfers between devices: 9.54 us -> 12.9 us
  blocking collectives: 81.3 us -> 83.3 us
    pallas_call x7, Pallas kernels: 20.2 us -> 16.4 us  [call(): pl.pallas_call(kernel, name=name, out_shape=[jax.ShapeDtypeStruct(shape,...]
    all_to_all x3, waiting for transfers between devices: 6.67 us -> 10.2 us  [exchange(): lax.all_to_all(value, axis, 0, 0, axis_index_groups=groups, tiled=True)]
    pallas_call x0 -> x1, Pallas kernels: none -> 3.4 us  [on_device(): pl.pallas_call(start_kernel, name='start', out_shape=[jax.ShapeDtypeStruc...]
    broadcast_in_dim x1 -> x0, local copies, waits for them, and re-layouts: 2.89 us -> none  [on_device(): gathered = exchange(jnp.broadcast_to(sent[None], (8, ROWS, 768)), MP)]
    all_to_all x2, blocking collectives: 40.2 us -> 41.9 us  [exchange(): lax.all_to_all(value, axis, 0, 0, axis_index_groups=groups, tiled=True)]
    unnamed x16 -> x12, local copies, waits for them, and re-layouts: 4.64 us -> 3.89 us
  transfers between devices with their start and end apart: 7 -> 7, of which waited for: 4 -> 4; matrix products, arithmetic and copies ran while one was open for 0% -> 0% of each run, Pallas kernels for 7% -> 6%
where the time goes in v7:
time: 152 us
  blocking collectives  83.3 us (55%)
  starting transfers between devices  31.1 us (20%)
  Pallas kernels  19.8 us (13%)
  waiting for transfers between devices  12.9 us (8%)
  local copies, waits for them, and re-layouts  3.89 us (3%)
    all_to_all x2, blocking collectives, exchange(): lax.all_to_all(value, axis, 0, 0, axis_index_groups=groups, tiled=True)  41.9 us
    all_gather x1, blocking collectives, on_device(): mine = lax.all_gather(pair, 'z', axis=0, tiled=False)  35.6 us
    ppermute x4, starting transfers between devices, swap_cores(): return lax.ppermute(value, 'core', [(0, 1), (1, 0)])  16.4 us
    pallas_call x7, Pallas kernels, call(): pl.pallas_call(kernel, name=name, out_shape=[jax.ShapeDtypeStruct(shape,...  16.4 us
    all_to_all x3, starting transfers between devices, exchange(): lax.all_to_all(value, axis, 0, 0, axis_index_groups=groups, tiled=True)  14.7 us
    all_to_all x3, waiting for transfers between devices, exchange(): lax.all_to_all(value, axis, 0, 0, axis_index_groups=groups, tiled=True)  10.2 us
    all_gather x1, blocking collectives, on_device(): pair = lax.all_gather(shard, 'x_hi', axis=0, tiled=False)  5.72 us
    unnamed x12, local copies, waits for them, and re-layouts  3.89 us
  transfers between devices with their start and end apart: 7, of which 4 were waited for; matrix products, arithmetic and copies ran while one was open for 0% of the time, Pallas kernels for 6%

profile of v7, /device:TPU:1, one launch (start us, length us, event | category | flops | bytes accessed | tf_op | source)
XLA Modules:
  0.0 151.7 jit_solution(13697679509698371220)
XLA Ops:
  0.6 3.4 %start.1 = (bf16[96,128]{1,0:T(8,128)(2,1)}, bf16[8,256,768]{2,1,0:T(8,128)(2,1)}) custom-call(bf16[6,2,512]{2,1,0:T(2,128)(2,1)} %bitcast.16, bf16[6,8,128]{2,1,0:T(8,128)(2,1)} %bitcast.17, bf16[256,768]{1,0:T(8,128)(2,1)} %x_ref.3), custom_call_target="tpu_custom_call" | custom-call | tf_op jit(solution)/shard_map/start/pallas_call | solution.py:247
  4.0 5.7 %all-gather = bf16[192,128]{1,0:T(8,128)(2,1)S(1)} all-gather(bf16[96,128]{1,0:T(8,128)(2,1)} %get-tuple-element.19), channel_id=2, replica_groups=mesh['x_hi'=2,'z'=16,'core'=2,'x_lo'=2,'y'=4] {'x_hi'}, dimensions={0}, use_global_device_ids=true | all-gather | bytes 73728 | tf_op jit(solution)/shard_map/all_gather | solution.py:259
  9.8 0.0 copy-start.2
  9.8 5.4 %all-to-all-start = ((bf16[8,256,768]{2,1,0:T(8,128)(2,1)}), bf16[8,256,768]{2,1,0:T(8,128)(2,1)}, u32[]{:S(2)}, u32[]{:S(2)}) async-start(bf16[8,256,768]{2,1,0:T(8,128)(2,1)} %get-tuple-element.21), calls=%async_computation | async-start | bytes 6291456 | tf_op jit(solution)/shard_map/all_to_all | solution.py:238
  15.2 35.6 %all-gather.1 = bf16[32,96,128]{2,1,0:T(8,128)(2,1)S(1)} all-gather(bf16[2,96,128]{2,1,0:T(8,128)(2,1)S(1)} %bitcast.15), channel_id=3, replica_groups=mesh['x_hi'=2,'z'=16,'core'=2,'x_lo'=2,'y'=4] {'z'}, dimensions={0}, use_global_device_ids=true | all-gather | bytes 835584 | tf_op jit(solution)/shard_map/all_gather | solution.py:262
  50.8 8.4 %collective-permute-start.1 = (bf16[16,2,96,128]{3,2,1,0:T(8,128)(2,1)S(1)}, bf16[16,2,96,128]{3,2,1,0:T(8,128)(2,1)S(1)}, u32[]{:S(2)}, u32[]{:S(2)}) collective-permute-start(bf16[16,2,96,128]{3,2,1,0:T(8,128)(2,1)S(1)} %bitcast.9), channel_id=1, source_target_pairs={{0,8},{8,0},{1,9},{9,1},{2,10},{10,2},{3,11},{11,3},{4,12},{12,4},... | collective-permute-start | bytes 2359304 | tf_op jit(solution)/shard_map/ppermute | solution.py:242
  59.2 1.0 columns.1
  60.2 0.0 all-to-all-done.x_ref
  60.2 5.1 %all-to-all-start.1 = ((bf16[8,3,64,128]{3,2,1,0:T(8,128)(2,1)}), bf16[8,3,64,128]{3,2,1,0:T(8,128)(2,1)S(1)}, u32[]{:S(2)}, u32[]{:S(2)}) async-start(bf16[8,3,64,128]{3,2,1,0:T(8,128)(2,1)} %columns.1), calls=%async_computation.1 | async-start | bytes 786432 | tf_op jit(solution)/shard_map/all_to_all | solution.py:238
  65.4 0.1 pad_add_fusion.at_ref
  65.4 0.0 collective-permute-done.1.wother_ref.other_ref
  65.4 0.0 copy-done.2
  65.4 1.6 %d_mixed.1 = bf16[8,24,16,256]{3,2,1,0:T(8,128)(2,1)S(1)} custom-call(s32[2]{0:T(128)S(1)} %pad_add_fusion.at_ref, bf16[16,2,96,128]{3,2,1,0:T(8,128)(2,1)S(1)} %bitcast.11, bf16[16,2,96,128]{3,2,1,0:T(8,128)(2,1)S(1)} %collective-permute-done.1.wother_ref.other_ref, bf16[256,768]{1,0:T(8,128)(2,1)S(1)} %copy-done.2), custom_call_target="tpu_custom_call" | custom-call | flops 201326592 | bytes 6000000 | tf_op jit(solution)/shard_map/d_mixed/pallas_call | solution.py:178
  67.1 0.0 copy-start
  67.1 1.1 copy-done
  68.2 4.6 %all-to-all-done.1.mine_ref = bf16[8,3,64,128]{3,2,1,0:T(8,128)(2,1)S(1)} async-done(((bf16[8,3,64,128]{3,2,1,0:T(8,128)(2,1)}), bf16[8,3,64,128]{3,2,1,0:T(8,128)(2,1)S(1)}, u32[]{:S(2)}, u32[]{:S(2)}) %all-to-all-start.1) | async-done | bytes 393248 | tf_op jit(solution)/shard_map/all_to_all | solution.py:238
  72.9 4.1 %all-to-all-start.2 = ((bf16[8,24,16,256]{3,2,1,0:T(8,128)(2,1)}), bf16[8,24,16,256]{3,2,1,0:T(8,128)(2,1)S(1)}, u32[]{:S(2)}, u32[]{:S(2)}) async-start(bf16[8,24,16,256]{3,2,1,0:T(8,128)(2,1)} %copy-done), calls=%async_computation.2 | async-start | bytes 3145728 | tf_op jit(solution)/shard_map/all_to_all | solution.py:238
  77.0 3.0 %collective-permute-start = (bf16[8,3,64,128]{3,2,1,0:T(8,128)(2,1)S(1)}, bf16[8,3,64,128]{3,2,1,0:T(8,128)(2,1)S(1)}, u32[]{:S(2)}, u32[]{:S(2)}) collective-permute-start(bf16[8,3,64,128]{3,2,1,0:T(8,128)(2,1)S(1)} %all-to-all-done.1.mine_ref), channel_id=1, source_target_pairs={{0,8},{8,0},{1,9},{9,1},{2,10},{10,2},{3,11},{11,3},{4,12},{12,4},... | collective-permute-start | bytes 1179656 | tf_op jit(solution)/shard_map/ppermute | solution.py:242
  80.0 1.3 collective-permute-done.other_ref
  81.3 0.0 copy-start.3
  81.4 1.0 copy-done.3
  82.3 6.5 %second_grad.1 = (bf16[256,768]{1,0:T(8,128)(2,1)}, bf16[32,48,128]{2,1,0:T(8,128)(2,1)S(1)}, bf16[32,48,128]{2,1,0:T(8,128)(2,1)}) custom-call(s32[2]{0:T(128)S(1)} %pad_add_fusion.at_ref, bf16[8,256,768]{2,1,0:T(8,128)(2,1)} %all-to-all-done.x_ref, bf16[8,3,64,128]{3,2,1,0:T(8,128)(2,1)S(1)} %all-to-all-done.1.mine_ref, ...), custom_call_target="tpu_custom_call" | custom-call | flops 201326592 | bytes 6000000 | tf_op jit(solution)/shard_map/second_grad/pallas_call | solution.py:178
  88.9 0.0 copy-start.4
  88.9 0.7 copy-done.4
  89.6 2.3 %collective-permute-start.2 = (bf16[32,48,128]{2,1,0:T(8,128)(2,1)}, bf16[32,48,128]{2,1,0:T(8,128)(2,1)S(1)}, u32[]{:S(2)}, u32[]{:S(2)}) collective-permute-start(bf16[32,48,128]{2,1,0:T(8,128)(2,1)} %get-tuple-element.25), channel_id=1, source_target_pairs={{0,8},{8,0},{1,9},{9,1},{2,10},{10,2},{3,11},{11,3},{4,12},{12,4},... | collective-permute-start | bytes 1179656 | tf_op jit(solution)/shard_map/ppermute | solution.py:242
  91.9 5.6 %all-to-all-done.2.back_ref = bf16[8,24,16,256]{3,2,1,0:T(8,128)(2,1)S(1)} async-done(((bf16[8,24,16,256]{3,2,1,0:T(8,128)(2,1)}), bf16[8,24,16,256]{3,2,1,0:T(8,128)(2,1)S(1)}, u32[]{:S(2)}, u32[]{:S(2)}) %all-to-all-start.2) | async-done | bytes 1572896 | tf_op jit(solution)/shard_map/all_to_all | solution.py:238
  97.5 0.0 collective-permute-done.2.after_ref.got_out
  97.5 0.0 copy-start.1
  97.5 1.0 copy-done.1
  98.5 0.0 copy-start.5
  98.5 5.7 %first_grad.1 = (bf16[256,768]{1,0:T(8,128)(2,1)}, bf16[32,48,128]{2,1,0:T(8,128)(2,1)S(1)}, bf16[32,48,128]{2,1,0:T(8,128)(2,1)S(1)}) custom-call(s32[2]{0:T(128)S(1)} %pad_add_fusion.at_ref, bf16[16,2,96,128]{3,2,1,0:T(8,128)(2,1)S(1)} %bitcast.13, bf16[16,2,96,128]{3,2,1,0:T(8,128)(2,1)S(1)} %collective-permute-done.1.wother_ref.other_ref, ...), custom_call_target="tpu_custom_call" | custom-call | flops 201326592 | bytes 6000000 | tf_op jit(solution)/shard_map/first_grad/pallas_call | solution.py:178
  104.2 2.8 %collective-permute-start.3 = (bf16[32,48,128]{2,1,0:T(8,128)(2,1)S(1)}, bf16[32,48,128]{2,1,0:T(8,128)(2,1)S(1)}, u32[]{:S(2)}, u32[]{:S(2)}) collective-permute-start(bf16[32,48,128]{2,1,0:T(8,128)(2,1)S(1)} %get-tuple-element.28), channel_id=1, source_target_pairs={{0,8},{8,0},{1,9},{9,1},{2,10},{10,2},{3,11},{11,3},{4,12},{12,4},... | collective-permute-start | bytes 1179656 | tf_op jit(solution)/shard_map/ppermute | solution.py:242
  107.0 1.3 collective-permute-done.3.got_in
  108.3 0.0 copy-done.5
  108.3 0.7 join.1
  109.1 17.2 %all_to_all.25.got_ref = bf16[4,8,96,128]{3,2,1,0:T(8,128)(2,1)S(1)} all-to-all(bf16[4,8,96,128]{3,2,1,0:T(8,128)(2,1)S(1)} %bitcast.14), channel_id=1, replica_groups={{0,16,256,272},{32,48,288,304},{64,80,320,336},{96,112,352,368},{128,14..., dimensions={0} | all-to-all | bytes 1572864 | tf_op jit(solution)/shard_map/all_to_all | solution.py:238
  126.3 0.1 part.1
  126.4 24.7 %all_to_all.26.got_ref = bf16[8,96,128]{2,1,0:T(8,128)(2,1)S(1)} all-to-all(bf16[8,96,128]{2,1,0:T(8,128)(2,1)S(1)} %part.1), channel_id=1, replica_groups={{0,32,64,96,128,160,192,224},{8,40,72,104,136,168,200,232},{16,48,80,11..., dimensions={0} | all-to-all | bytes 393216 | tf_op jit(solution)/shard_map/all_to_all | solution.py:238
  151.1 0.6 total.1
Async XLA Ops:
  9.8 55.7 %copy-start.2 = (bf16[256,768]{1,0:T(8,128)(2,1)S(1)}, bf16[256,768]{1,0:T(8,128)(2,1)}, u32[]{:S(2)}) copy-start(bf16[256,768]{1,0:T(8,128)(2,1)} %c_ref.3) | copy-start | bytes 1179652
  9.8 50.5 %all-to-all-start = ((bf16[8,256,768]{2,1,0:T(8,128)(2,1)}), bf16[8,256,768]{2,1,0:T(8,128)(2,1)}, u32[]{:S(2)}, u32[]{:S(2)}) async-start(bf16[8,256,768]{2,1,0:T(8,128)(2,1)} %get-tuple-element.21), calls=%async_computation | async-start | bytes 6291456 | tf_op jit(solution)/shard_map/all_to_all | solution.py:238
  50.8 14.6 %collective-permute-start.1 = (bf16[16,2,96,128]{3,2,1,0:T(8,128)(2,1)S(1)}, bf16[16,2,96,128]{3,2,1,0:T(8,128)(2,1)S(1)}, u32[]{:S(2)}, u32[]{:S(2)}) collective-permute-start(bf16[16,2,96,128]{3,2,1,0:T(8,128)(2,1)S(1)} %bitcast.9), channel_id=1, source_target_pairs={{0,8},{8,0},{1,9},{9,1},{2,10},{10,2},{3,11},{11,3},{4,12},{12,4},... | collective-permute-start | bytes 2359304 | tf_op jit(solution)/shard_map/ppermute | solution.py:242
  60.2 12.7 %all-to-all-start.1 = ((bf16[8,3,64,128]{3,2,1,0:T(8,128)(2,1)}), bf16[8,3,64,128]{3,2,1,0:T(8,128)(2,1)S(1)}, u32[]{:S(2)}, u32[]{:S(2)}) async-start(bf16[8,3,64,128]{3,2,1,0:T(8,128)(2,1)} %columns.1), calls=%async_computation.1 | async-start | bytes 786432 | tf_op jit(solution)/shard_map/all_to_all | solution.py:238
  67.1 1.2 copy-start
  72.9 24.6 %all-to-all-start.2 = ((bf16[8,24,16,256]{3,2,1,0:T(8,128)(2,1)}), bf16[8,24,16,256]{3,2,1,0:T(8,128)(2,1)S(1)}, u32[]{:S(2)}, u32[]{:S(2)}) async-start(bf16[8,24,16,256]{3,2,1,0:T(8,128)(2,1)} %copy-done), calls=%async_computation.2 | async-start | bytes 3145728 | tf_op jit(solution)/shard_map/all_to_all | solution.py:238
  77.0 4.4 %collective-permute-start = (bf16[8,3,64,128]{3,2,1,0:T(8,128)(2,1)S(1)}, bf16[8,3,64,128]{3,2,1,0:T(8,128)(2,1)S(1)}, u32[]{:S(2)}, u32[]{:S(2)}) collective-permute-start(bf16[8,3,64,128]{3,2,1,0:T(8,128)(2,1)S(1)} %all-to-all-done.1.mine_ref), channel_id=1, source_target_pairs={{0,8},{8,0},{1,9},{9,1},{2,10},{10,2},{3,11},{11,3},{4,12},{12,4},... | collective-permute-start | bytes 1179656 | tf_op jit(solution)/shard_map/ppermute | solution.py:242
  81.3 1.0 copy-start.3
  88.9 0.7 copy-start.4
  89.6 7.9 %collective-permute-start.2 = (bf16[32,48,128]{2,1,0:T(8,128)(2,1)}, bf16[32,48,128]{2,1,0:T(8,128)(2,1)S(1)}, u32[]{:S(2)}, u32[]{:S(2)}) collective-permute-start(bf16[32,48,128]{2,1,0:T(8,128)(2,1)} %get-tuple-element.25), channel_id=1, source_target_pairs={{0,8},{8,0},{1,9},{9,1},{2,10},{10,2},{3,11},{11,3},{4,12},{12,4},... | collective-permute-start | bytes 1179656 | tf_op jit(solution)/shard_map/ppermute | solution.py:242
  97.5 1.0 copy-start.1
  98.5 9.8 %copy-start.5 = (bf16[32,48,128]{2,1,0:T(8,128)(2,1)S(1)}, bf16[32,48,128]{2,1,0:T(8,128)(2,1)}, u32[]{:S(2)}) copy-start(bf16[32,48,128]{2,1,0:T(8,128)(2,1)} %copy-done.4) | copy-start | bytes 1179652
  104.2 4.1 %collective-permute-start.3 = (bf16[32,48,128]{2,1,0:T(8,128)(2,1)S(1)}, bf16[32,48,128]{2,1,0:T(8,128)(2,1)S(1)}, u32[]{:S(2)}, u32[]{:S(2)}) collective-permute-start(bf16[32,48,128]{2,1,0:T(8,128)(2,1)S(1)} %get-tuple-element.28), channel_id=1, source_target_pairs={{0,8},{8,0},{1,9},{9,1},{2,10},{10,2},{3,11},{11,3},{4,12},{12,4},... | collective-permute-start | bytes 1179656 | tf_op jit(solution)/shard_map/ppermute | solution.py:242

commit v8 on v7

--- a/solution.py
+++ b/solution.py
@@ -74,7 +74,8 @@
 
 
 def first_rows(ref, i):
-    return jnp.swapaxes(shard_rows(ref, slice(i * 8, i * 8 + 8)), 0, 1)
+    both = shard_rows(ref, slice(i // 2 * 16, i // 2 * 16 + 16))
+    return jnp.swapaxes(both[:, i % 2 * 8 : i % 2 * 8 + 8], 0, 1)
 
 
 def columns_kernel(mine_ref, send_ref):

time: 152 us -> 152 us (level)
  no operation moved by 1% of the time
where the time goes in v8:
time: 152 us
  blocking collectives  83.3 us (55%)
  starting transfers between devices  31.1 us (20%)
  Pallas kernels  19.8 us (13%)
  waiting for transfers between devices  12.9 us (8%)
  local copies, waits for them, and re-layouts  3.89 us (3%)
    all_to_all x2, blocking collectives, exchange(): lax.all_to_all(value, axis, 0, 0, axis_index_groups=groups, tiled=True)  41.9 us
    all_gather x1, blocking collectives, on_device(): mine = lax.all_gather(pair, 'z', axis=0, tiled=False)  35.6 us
    pallas_call x7, Pallas kernels, call(): pl.pallas_call(kernel, name=name, out_shape=[jax.ShapeDtypeStruct(shape,...  16.4 us
    ppermute x4, starting transfers between devices, swap_cores(): return lax.ppermute(value, 'core', [(0, 1), (1, 0)])  16.4 us
    all_to_all x3, starting transfers between devices, exchange(): lax.all_to_all(value, axis, 0, 0, axis_index_groups=groups, tiled=True)  14.7 us
    all_to_all x3, waiting for transfers between devices, exchange(): lax.all_to_all(value, axis, 0, 0, axis_index_groups=groups, tiled=True)  10.2 us
    all_gather x1, blocking collectives, on_device(): pair = lax.all_gather(shard, 'x_hi', axis=0, tiled=False)  5.72 us
    unnamed x12, local copies, waits for them, and re-layouts  3.89 us
  transfers between devices with their start and end apart: 7, of which 4 were waited for; matrix products, arithmetic and copies ran while one was open for 0% of the time, Pallas kernels for 6%

profile of v8, /device:TPU:1, one launch (start us, length us, event | category | flops | bytes accessed | tf_op | source)
XLA Modules:
  0.0 151.7 jit_solution(3944795443699395515)
XLA Ops:
  0.6 3.4 %start.1 = (bf16[96,128]{1,0:T(8,128)(2,1)}, bf16[8,256,768]{2,1,0:T(8,128)(2,1)}) custom-call(bf16[6,2,512]{2,1,0:T(2,128)(2,1)} %bitcast.16, bf16[6,8,128]{2,1,0:T(8,128)(2,1)} %bitcast.17, bf16[256,768]{1,0:T(8,128)(2,1)} %x_ref.3), custom_call_target="tpu_custom_call" | custom-call | tf_op jit(solution)/shard_map/start/pallas_call | solution.py:248
  4.0 5.7 %all-gather = bf16[192,128]{1,0:T(8,128)(2,1)S(1)} all-gather(bf16[96,128]{1,0:T(8,128)(2,1)} %get-tuple-element.19), channel_id=2, replica_groups=mesh['x_hi'=2,'z'=16,'core'=2,'x_lo'=2,'y'=4] {'x_hi'}, dimensions={0}, use_global_device_ids=true | all-gather | bytes 73728 | tf_op jit(solution)/shard_map/all_gather | solution.py:260
  9.8 0.0 copy-start.2
  9.8 5.4 %all-to-all-start = ((bf16[8,256,768]{2,1,0:T(8,128)(2,1)}), bf16[8,256,768]{2,1,0:T(8,128)(2,1)}, u32[]{:S(2)}, u32[]{:S(2)}) async-start(bf16[8,256,768]{2,1,0:T(8,128)(2,1)} %get-tuple-element.21), calls=%async_computation | async-start | bytes 6291456 | tf_op jit(solution)/shard_map/all_to_all | solution.py:239
  15.2 35.6 %all-gather.1 = bf16[32,96,128]{2,1,0:T(8,128)(2,1)S(1)} all-gather(bf16[2,96,128]{2,1,0:T(8,128)(2,1)S(1)} %bitcast.15), channel_id=3, replica_groups=mesh['x_hi'=2,'z'=16,'core'=2,'x_lo'=2,'y'=4] {'z'}, dimensions={0}, use_global_device_ids=true | all-gather | bytes 835584 | tf_op jit(solution)/shard_map/all_gather | solution.py:263
  50.8 8.4 %collective-permute-start.1 = (bf16[16,2,96,128]{3,2,1,0:T(8,128)(2,1)S(1)}, bf16[16,2,96,128]{3,2,1,0:T(8,128)(2,1)S(1)}, u32[]{:S(2)}, u32[]{:S(2)}) collective-permute-start(bf16[16,2,96,128]{3,2,1,0:T(8,128)(2,1)S(1)} %bitcast.9), channel_id=1, source_target_pairs={{0,8},{8,0},{1,9},{9,1},{2,10},{10,2},{3,11},{11,3},{4,12},{12,4},... | collective-permute-start | bytes 2359304 | tf_op jit(solution)/shard_map/ppermute | solution.py:243
  59.2 1.0 columns.1
  60.2 0.0 all-to-all-done.x_ref
  60.2 5.1 %all-to-all-start.1 = ((bf16[8,3,64,128]{3,2,1,0:T(8,128)(2,1)}), bf16[8,3,64,128]{3,2,1,0:T(8,128)(2,1)S(1)}, u32[]{:S(2)}, u32[]{:S(2)}) async-start(bf16[8,3,64,128]{3,2,1,0:T(8,128)(2,1)} %columns.1), calls=%async_computation.1 | async-start | bytes 786432 | tf_op jit(solution)/shard_map/all_to_all | solution.py:239
  65.4 0.1 pad_add_fusion.at_ref
  65.4 0.0 collective-permute-done.1.wother_ref.other_ref
  65.4 0.0 copy-done.2
  65.4 1.6 %d_mixed.1 = bf16[8,24,16,256]{3,2,1,0:T(8,128)(2,1)S(1)} custom-call(s32[2]{0:T(128)S(1)} %pad_add_fusion.at_ref, bf16[16,2,96,128]{3,2,1,0:T(8,128)(2,1)S(1)} %bitcast.11, bf16[16,2,96,128]{3,2,1,0:T(8,128)(2,1)S(1)} %collective-permute-done.1.wother_ref.other_ref, bf16[256,768]{1,0:T(8,128)(2,1)S(1)} %copy-done.2), custom_call_target="tpu_custom_call" | custom-call | flops 201326592 | bytes 6000000 | tf_op jit(solution)/shard_map/d_mixed/pallas_call | solution.py:179
  67.1 0.0 copy-start
  67.1 1.1 copy-done
  68.3 4.6 %all-to-all-done.1.mine_ref = bf16[8,3,64,128]{3,2,1,0:T(8,128)(2,1)S(1)} async-done(((bf16[8,3,64,128]{3,2,1,0:T(8,128)(2,1)}), bf16[8,3,64,128]{3,2,1,0:T(8,128)(2,1)S(1)}, u32[]{:S(2)}, u32[]{:S(2)}) %all-to-all-start.1) | async-done | bytes 393248 | tf_op jit(solution)/shard_map/all_to_all | solution.py:239
  72.9 4.1 %all-to-all-start.2 = ((bf16[8,24,16,256]{3,2,1,0:T(8,128)(2,1)}), bf16[8,24,16,256]{3,2,1,0:T(8,128)(2,1)S(1)}, u32[]{:S(2)}, u32[]{:S(2)}) async-start(bf16[8,24,16,256]{3,2,1,0:T(8,128)(2,1)} %copy-done), calls=%async_computation.2 | async-start | bytes 3145728 | tf_op jit(solution)/shard_map/all_to_all | solution.py:239
  77.0 3.0 %collective-permute-start = (bf16[8,3,64,128]{3,2,1,0:T(8,128)(2,1)S(1)}, bf16[8,3,64,128]{3,2,1,0:T(8,128)(2,1)S(1)}, u32[]{:S(2)}, u32[]{:S(2)}) collective-permute-start(bf16[8,3,64,128]{3,2,1,0:T(8,128)(2,1)S(1)} %all-to-all-done.1.mine_ref), channel_id=1, source_target_pairs={{0,8},{8,0},{1,9},{9,1},{2,10},{10,2},{3,11},{11,3},{4,12},{12,4},... | collective-permute-start | bytes 1179656 | tf_op jit(solution)/shard_map/ppermute | solution.py:243
  80.0 1.3 collective-permute-done.other_ref
  81.4 0.0 copy-start.3
  81.4 1.0 copy-done.3
  82.3 6.5 %second_grad.1 = (bf16[256,768]{1,0:T(8,128)(2,1)}, bf16[32,48,128]{2,1,0:T(8,128)(2,1)S(1)}, bf16[32,48,128]{2,1,0:T(8,128)(2,1)}) custom-call(s32[2]{0:T(128)S(1)} %pad_add_fusion.at_ref, bf16[8,256,768]{2,1,0:T(8,128)(2,1)} %all-to-all-done.x_ref, bf16[8,3,64,128]{3,2,1,0:T(8,128)(2,1)S(1)} %all-to-all-done.1.mine_ref, ...), custom_call_target="tpu_custom_call" | custom-call | flops 201326592 | bytes 6000000 | tf_op jit(solution)/shard_map/second_grad/pallas_call | solution.py:179
  88.9 0.0 copy-start.4
  88.9 0.7 copy-done.4
  89.6 2.3 %collective-permute-start.2 = (bf16[32,48,128]{2,1,0:T(8,128)(2,1)}, bf16[32,48,128]{2,1,0:T(8,128)(2,1)S(1)}, u32[]{:S(2)}, u32[]{:S(2)}) collective-permute-start(bf16[32,48,128]{2,1,0:T(8,128)(2,1)} %get-tuple-element.25), channel_id=1, source_target_pairs={{0,8},{8,0},{1,9},{9,1},{2,10},{10,2},{3,11},{11,3},{4,12},{12,4},... | collective-permute-start | bytes 1179656 | tf_op jit(solution)/shard_map/ppermute | solution.py:243
  91.9 5.6 %all-to-all-done.2.back_ref = bf16[8,24,16,256]{3,2,1,0:T(8,128)(2,1)S(1)} async-done(((bf16[8,24,16,256]{3,2,1,0:T(8,128)(2,1)}), bf16[8,24,16,256]{3,2,1,0:T(8,128)(2,1)S(1)}, u32[]{:S(2)}, u32[]{:S(2)}) %all-to-all-start.2) | async-done | bytes 1572896 | tf_op jit(solution)/shard_map/all_to_all | solution.py:239
  97.5 0.0 collective-permute-done.2.after_ref.got_out
  97.5 0.0 copy-start.1
  97.5 1.0 copy-done.1
  98.5 0.0 copy-start.5
  98.5 5.7 %first_grad.1 = (bf16[256,768]{1,0:T(8,128)(2,1)}, bf16[32,48,128]{2,1,0:T(8,128)(2,1)S(1)}, bf16[32,48,128]{2,1,0:T(8,128)(2,1)S(1)}) custom-call(s32[2]{0:T(128)S(1)} %pad_add_fusion.at_ref, bf16[16,2,96,128]{3,2,1,0:T(8,128)(2,1)S(1)} %bitcast.13, bf16[16,2,96,128]{3,2,1,0:T(8,128)(2,1)S(1)} %collective-permute-done.1.wother_ref.other_ref, ...), custom_call_target="tpu_custom_call" | custom-call | flops 201326592 | bytes 6000000 | tf_op jit(solution)/shard_map/first_grad/pallas_call | solution.py:179
  104.3 2.7 %collective-permute-start.3 = (bf16[32,48,128]{2,1,0:T(8,128)(2,1)S(1)}, bf16[32,48,128]{2,1,0:T(8,128)(2,1)S(1)}, u32[]{:S(2)}, u32[]{:S(2)}) collective-permute-start(bf16[32,48,128]{2,1,0:T(8,128)(2,1)S(1)} %get-tuple-element.28), channel_id=1, source_target_pairs={{0,8},{8,0},{1,9},{9,1},{2,10},{10,2},{3,11},{11,3},{4,12},{12,4},... | collective-permute-start | bytes 1179656 | tf_op jit(solution)/shard_map/ppermute | solution.py:243
  107.0 1.3 collective-permute-done.3.got_in
  108.3 0.0 copy-done.5
  108.3 0.7 join.1
  109.1 17.2 %all_to_all.25.got_ref = bf16[4,8,96,128]{3,2,1,0:T(8,128)(2,1)S(1)} all-to-all(bf16[4,8,96,128]{3,2,1,0:T(8,128)(2,1)S(1)} %bitcast.14), channel_id=1, replica_groups={{0,16,256,272},{32,48,288,304},{64,80,320,336},{96,112,352,368},{128,14..., dimensions={0} | all-to-all | bytes 1572864 | tf_op jit(solution)/shard_map/all_to_all | solution.py:239
  126.3 0.1 part.1
  126.4 24.7 %all_to_all.26.got_ref = bf16[8,96,128]{2,1,0:T(8,128)(2,1)S(1)} all-to-all(bf16[8,96,128]{2,1,0:T(8,128)(2,1)S(1)} %part.1), channel_id=1, replica_groups={{0,32,64,96,128,160,192,224},{8,40,72,104,136,168,200,232},{16,48,80,11..., dimensions={0} | all-to-all | bytes 393216 | tf_op jit(solution)/shard_map/all_to_all | solution.py:239
  151.1 0.6 total.1
Async XLA Ops:
  9.8 55.7 %copy-start.2 = (bf16[256,768]{1,0:T(8,128)(2,1)S(1)}, bf16[256,768]{1,0:T(8,128)(2,1)}, u32[]{:S(2)}) copy-start(bf16[256,768]{1,0:T(8,128)(2,1)} %c_ref.3) | copy-start | bytes 1179652
  9.8 50.5 %all-to-all-start = ((bf16[8,256,768]{2,1,0:T(8,128)(2,1)}), bf16[8,256,768]{2,1,0:T(8,128)(2,1)}, u32[]{:S(2)}, u32[]{:S(2)}) async-start(bf16[8,256,768]{2,1,0:T(8,128)(2,1)} %get-tuple-element.21), calls=%async_computation | async-start | bytes 6291456 | tf_op jit(solution)/shard_map/all_to_all | solution.py:239
  50.8 14.6 %collective-permute-start.1 = (bf16[16,2,96,128]{3,2,1,0:T(8,128)(2,1)S(1)}, bf16[16,2,96,128]{3,2,1,0:T(8,128)(2,1)S(1)}, u32[]{:S(2)}, u32[]{:S(2)}) collective-permute-start(bf16[16,2,96,128]{3,2,1,0:T(8,128)(2,1)S(1)} %bitcast.9), channel_id=1, source_target_pairs={{0,8},{8,0},{1,9},{9,1},{2,10},{10,2},{3,11},{11,3},{4,12},{12,4},... | collective-permute-start | bytes 2359304 | tf_op jit(solution)/shard_map/ppermute | solution.py:243
  60.2 12.7 %all-to-all-start.1 = ((bf16[8,3,64,128]{3,2,1,0:T(8,128)(2,1)}), bf16[8,3,64,128]{3,2,1,0:T(8,128)(2,1)S(1)}, u32[]{:S(2)}, u32[]{:S(2)}) async-start(bf16[8,3,64,128]{3,2,1,0:T(8,128)(2,1)} %columns.1), calls=%async_computation.1 | async-start | bytes 786432 | tf_op jit(solution)/shard_map/all_to_all | solution.py:239
  67.1 1.2 copy-start
  72.9 24.6 %all-to-all-start.2 = ((bf16[8,24,16,256]{3,2,1,0:T(8,128)(2,1)}), bf16[8,24,16,256]{3,2,1,0:T(8,128)(2,1)S(1)}, u32[]{:S(2)}, u32[]{:S(2)}) async-start(bf16[8,24,16,256]{3,2,1,0:T(8,128)(2,1)} %copy-done), calls=%async_computation.2 | async-start | bytes 3145728 | tf_op jit(solution)/shard_map/all_to_all | solution.py:239
  77.0 4.4 %collective-permute-start = (bf16[8,3,64,128]{3,2,1,0:T(8,128)(2,1)S(1)}, bf16[8,3,64,128]{3,2,1,0:T(8,128)(2,1)S(1)}, u32[]{:S(2)}, u32[]{:S(2)}) collective-permute-start(bf16[8,3,64,128]{3,2,1,0:T(8,128)(2,1)S(1)} %all-to-all-done.1.mine_ref), channel_id=1, source_target_pairs={{0,8},{8,0},{1,9},{9,1},{2,10},{10,2},{3,11},{11,3},{4,12},{12,4},... | collective-permute-start | bytes 1179656 | tf_op jit(solution)/shard_map/ppermute | solution.py:243
  81.4 1.0 copy-start.3
  88.9 0.7 copy-start.4
  89.6 7.9 %collective-permute-start.2 = (bf16[32,48,128]{2,1,0:T(8,128)(2,1)}, bf16[32,48,128]{2,1,0:T(8,128)(2,1)S(1)}, u32[]{:S(2)}, u32[]{:S(2)}) collective-permute-start(bf16[32,48,128]{2,1,0:T(8,128)(2,1)} %get-tuple-element.25), channel_id=1, source_target_pairs={{0,8},{8,0},{1,9},{9,1},{2,10},{10,2},{3,11},{11,3},{4,12},{12,4},... | collective-permute-start | bytes 1179656 | tf_op jit(solution)/shard_map/ppermute | solution.py:243
  97.5 1.0 copy-start.1
  98.5 9.8 %copy-start.5 = (bf16[32,48,128]{2,1,0:T(8,128)(2,1)S(1)}, bf16[32,48,128]{2,1,0:T(8,128)(2,1)}, u32[]{:S(2)}) copy-start(bf16[32,48,128]{2,1,0:T(8,128)(2,1)} %copy-done.4) | copy-start | bytes 1179652
  104.3 4.1 %collective-permute-start.3 = (bf16[32,48,128]{2,1,0:T(8,128)(2,1)S(1)}, bf16[32,48,128]{2,1,0:T(8,128)(2,1)S(1)}, u32[]{:S(2)}, u32[]{:S(2)}) collective-permute-start(bf16[32,48,128]{2,1,0:T(8,128)(2,1)S(1)} %get-tuple-element.28), channel_id=1, source_target_pairs={{0,8},{8,0},{1,9},{9,1},{2,10},{10,2},{3,11},{11,3},{4,12},{12,4},... | collective-permute-start | bytes 1179656 | tf_op jit(solution)/shard_map/ppermute | solution.py:243

commit v9 on v8

--- a/solution.py
+++ b/solution.py
@@ -195,7 +195,9 @@
 def join_kernel(at_ref, keep_in, got_in, keep_out, got_out, both_ref):
     for n in range(32):
         place = lax.rem(n % RUN + RUN // 2 * at_ref[1], RUN)
-        to = n // 16 * 16 + place * RUNS + n % 16 // RUN
+        turn = RUNS // 2 * at_ref[1] + RUNS // 4 * (n % RUN)
+        run = lax.rem(n % 16 // RUN + 2 * RUNS - turn, RUNS)
+        to = lax.rem(n // 16 + at_ref[1], 2) * 16 + place * RUNS + run
         both_ref[to, :48, :] = (keep_in[n].astype(F32) + got_in[n].astype(F32)).astype(BF16)
         both_ref[to, 48:, :] = (keep_out[n].astype(F32) + got_out[n].astype(F32)).astype(BF16)
 
@@ -223,12 +225,15 @@
 RUN = 2
 RUNS = 16 // RUN
 NEAR = [
-    [x * 32 + (run * RUN + RUN // 2 * core + n) % 16 * 2 + core for x in range(2) for n in range(RUN)]
+    [x * 32 + (run * RUN + RUN // 2 * core + n) % 16 * 2 + core for x in (core, 1 - core) for n in range(RUN)]
     for core in range(2)
     for run in range(RUNS)
 ]
 FAR = [
-    [x * 32 + (run * RUN + n) * 2 + core for run in range(RUNS)]
+    [
+        x * 32 + ((run + RUNS // 2 * core + RUNS // 4 * n) % RUNS * RUN + n) * 2 + core
+        for run in range(RUNS)
+    ]
     for x in range(2)
     for n in range(RUN)
     for core in range(2)

time: 152 us -> 147 us (0.967)
  blocking collectives: 83.3 us -> 77.1 us
    all_to_all x2, blocking collectives: 41.9 us -> 35.8 us  [exchange(): lax.all_to_all(value, axis, 0, 0, axis_index_groups=groups, tiled=True)]
where the time goes in v9:
time: 147 us; the launch traced here: 146 us
  blocking collectives  77.1 us (52%)
  starting transfers between devices  31.1 us (21%)
  Pallas kernels  19.8 us (13%)
  waiting for transfers between devices  12.9 us (9%)
  local copies, waits for them, and re-layouts  3.89 us (3%)
    all_to_all x2, blocking collectives, exchange(): lax.all_to_all(value, axis, 0, 0, axis_index_groups=groups, tiled=True)  35.8 us
    all_gather x1, blocking collectives, on_device(): mine = lax.all_gather(pair, 'z', axis=0, tiled=False)  35.6 us
    pallas_call x7, Pallas kernels, call(): pl.pallas_call(kernel, name=name, out_shape=[jax.ShapeDtypeStruct(shape,...  16.4 us
    ppermute x4, starting transfers between devices, swap_cores(): return lax.ppermute(value, 'core', [(0, 1), (1, 0)])  16.4 us
    all_to_all x3, starting transfers between devices, exchange(): lax.all_to_all(value, axis, 0, 0, axis_index_groups=groups, tiled=True)  14.7 us
    all_to_all x3, waiting for transfers between devices, exchange(): lax.all_to_all(value, axis, 0, 0, axis_index_groups=groups, tiled=True)  10.2 us
    all_gather x1, blocking collectives, on_device(): pair = lax.all_gather(shard, 'x_hi', axis=0, tiled=False)  5.72 us
    unnamed x12, local copies, waits for them, and re-layouts  3.89 us
  transfers between devices with their start and end apart: 7, of which 4 were waited for; matrix products, arithmetic and copies ran while one was open for 0% of the time, Pallas kernels for 6%

profile of v9, /device:TPU:1, one launch (start us, length us, event | category | flops | bytes accessed | tf_op | source)
XLA Modules:
  0.0 145.6 jit_solution(4926378164915758300)
XLA Ops:
  0.6 3.4 %start.1 = (bf16[96,128]{1,0:T(8,128)(2,1)}, bf16[8,256,768]{2,1,0:T(8,128)(2,1)}) custom-call(bf16[6,2,512]{2,1,0:T(2,128)(2,1)} %bitcast.16, bf16[6,8,128]{2,1,0:T(8,128)(2,1)} %bitcast.17, bf16[256,768]{1,0:T(8,128)(2,1)} %x_ref.3), custom_call_target="tpu_custom_call" | custom-call | tf_op jit(solution)/shard_map/start/pallas_call | solution.py:253
  4.0 5.7 %all-gather = bf16[192,128]{1,0:T(8,128)(2,1)S(1)} all-gather(bf16[96,128]{1,0:T(8,128)(2,1)} %get-tuple-element.19), channel_id=2, replica_groups=mesh['x_hi'=2,'z'=16,'core'=2,'x_lo'=2,'y'=4] {'x_hi'}, dimensions={0}, use_global_device_ids=true | all-gather | bytes 73728 | tf_op jit(solution)/shard_map/all_gather | solution.py:265
  9.8 0.0 copy-start.2
  9.8 5.4 %all-to-all-start = ((bf16[8,256,768]{2,1,0:T(8,128)(2,1)}), bf16[8,256,768]{2,1,0:T(8,128)(2,1)}, u32[]{:S(2)}, u32[]{:S(2)}) async-start(bf16[8,256,768]{2,1,0:T(8,128)(2,1)} %get-tuple-element.21), calls=%async_computation | async-start | bytes 6291456 | tf_op jit(solution)/shard_map/all_to_all | solution.py:244
  15.2 35.6 %all-gather.1 = bf16[32,96,128]{2,1,0:T(8,128)(2,1)S(1)} all-gather(bf16[2,96,128]{2,1,0:T(8,128)(2,1)S(1)} %bitcast.15), channel_id=3, replica_groups=mesh['x_hi'=2,'z'=16,'core'=2,'x_lo'=2,'y'=4] {'z'}, dimensions={0}, use_global_device_ids=true | all-gather | bytes 835584 | tf_op jit(solution)/shard_map/all_gather | solution.py:268
  50.8 8.4 %collective-permute-start.1 = (bf16[16,2,96,128]{3,2,1,0:T(8,128)(2,1)S(1)}, bf16[16,2,96,128]{3,2,1,0:T(8,128)(2,1)S(1)}, u32[]{:S(2)}, u32[]{:S(2)}) collective-permute-start(bf16[16,2,96,128]{3,2,1,0:T(8,128)(2,1)S(1)} %bitcast.9), channel_id=1, source_target_pairs={{0,8},{8,0},{1,9},{9,1},{2,10},{10,2},{3,11},{11,3},{4,12},{12,4},... | collective-permute-start | bytes 2359304 | tf_op jit(solution)/shard_map/ppermute | solution.py:248
  59.2 1.0 columns.1
  60.2 0.0 all-to-all-done.x_ref
  60.2 5.1 %all-to-all-start.1 = ((bf16[8,3,64,128]{3,2,1,0:T(8,128)(2,1)}), bf16[8,3,64,128]{3,2,1,0:T(8,128)(2,1)S(1)}, u32[]{:S(2)}, u32[]{:S(2)}) async-start(bf16[8,3,64,128]{3,2,1,0:T(8,128)(2,1)} %columns.1), calls=%async_computation.1 | async-start | bytes 786432 | tf_op jit(solution)/shard_map/all_to_all | solution.py:244
  65.4 0.1 pad_add_fusion.at_ref
  65.4 0.0 collective-permute-done.1.wother_ref.other_ref
  65.4 0.0 copy-done.2
  65.4 1.6 %d_mixed.1 = bf16[8,24,16,256]{3,2,1,0:T(8,128)(2,1)S(1)} custom-call(s32[2]{0:T(128)S(1)} %pad_add_fusion.at_ref, bf16[16,2,96,128]{3,2,1,0:T(8,128)(2,1)S(1)} %bitcast.11, bf16[16,2,96,128]{3,2,1,0:T(8,128)(2,1)S(1)} %collective-permute-done.1.wother_ref.other_ref, bf16[256,768]{1,0:T(8,128)(2,1)S(1)} %copy-done.2), custom_call_target="tpu_custom_call" | custom-call | flops 201326592 | bytes 6000000 | tf_op jit(solution)/shard_map/d_mixed/pallas_call | solution.py:179
  67.1 0.0 copy-start
  67.1 1.1 copy-done
  68.3 4.6 %all-to-all-done.1.mine_ref = bf16[8,3,64,128]{3,2,1,0:T(8,128)(2,1)S(1)} async-done(((bf16[8,3,64,128]{3,2,1,0:T(8,128)(2,1)}), bf16[8,3,64,128]{3,2,1,0:T(8,128)(2,1)S(1)}, u32[]{:S(2)}, u32[]{:S(2)}) %all-to-all-start.1) | async-done | bytes 393248 | tf_op jit(solution)/shard_map/all_to_all | solution.py:244
  72.9 4.1 %all-to-all-start.2 = ((bf16[8,24,16,256]{3,2,1,0:T(8,128)(2,1)}), bf16[8,24,16,256]{3,2,1,0:T(8,128)(2,1)S(1)}, u32[]{:S(2)}, u32[]{:S(2)}) async-start(bf16[8,24,16,256]{3,2,1,0:T(8,128)(2,1)} %copy-done), calls=%async_computation.2 | async-start | bytes 3145728 | tf_op jit(solution)/shard_map/all_to_all | solution.py:244
  77.0 3.0 %collective-permute-start = (bf16[8,3,64,128]{3,2,1,0:T(8,128)(2,1)S(1)}, bf16[8,3,64,128]{3,2,1,0:T(8,128)(2,1)S(1)}, u32[]{:S(2)}, u32[]{:S(2)}) collective-permute-start(bf16[8,3,64,128]{3,2,1,0:T(8,128)(2,1)S(1)} %all-to-all-done.1.mine_ref), channel_id=1, source_target_pairs={{0,8},{8,0},{1,9},{9,1},{2,10},{10,2},{3,11},{11,3},{4,12},{12,4},... | collective-permute-start | bytes 1179656 | tf_op jit(solution)/shard_map/ppermute | solution.py:248
  80.0 1.3 collective-permute-done.other_ref
  81.4 0.0 copy-start.3
  81.4 1.0 copy-done.3
  82.3 6.5 %second_grad.1 = (bf16[256,768]{1,0:T(8,128)(2,1)}, bf16[32,48,128]{2,1,0:T(8,128)(2,1)S(1)}, bf16[32,48,128]{2,1,0:T(8,128)(2,1)}) custom-call(s32[2]{0:T(128)S(1)} %pad_add_fusion.at_ref, bf16[8,256,768]{2,1,0:T(8,128)(2,1)} %all-to-all-done.x_ref, bf16[8,3,64,128]{3,2,1,0:T(8,128)(2,1)S(1)} %all-to-all-done.1.mine_ref, ...), custom_call_target="tpu_custom_call" | custom-call | flops 201326592 | bytes 6000000 | tf_op jit(solution)/shard_map/second_grad/pallas_call | solution.py:179
  88.9 0.0 copy-start.4
  88.9 0.7 copy-done.4
  89.6 2.3 %collective-permute-start.2 = (bf16[32,48,128]{2,1,0:T(8,128)(2,1)}, bf16[32,48,128]{2,1,0:T(8,128)(2,1)S(1)}, u32[]{:S(2)}, u32[]{:S(2)}) collective-permute-start(bf16[32,48,128]{2,1,0:T(8,128)(2,1)} %get-tuple-element.25), channel_id=1, source_target_pairs={{0,8},{8,0},{1,9},{9,1},{2,10},{10,2},{3,11},{11,3},{4,12},{12,4},... | collective-permute-start | bytes 1179656 | tf_op jit(solution)/shard_map/ppermute | solution.py:248
  91.9 5.6 %all-to-all-done.2.back_ref = bf16[8,24,16,256]{3,2,1,0:T(8,128)(2,1)S(1)} async-done(((bf16[8,24,16,256]{3,2,1,0:T(8,128)(2,1)}), bf16[8,24,16,256]{3,2,1,0:T(8,128)(2,1)S(1)}, u32[]{:S(2)}, u32[]{:S(2)}) %all-to-all-start.2) | async-done | bytes 1572896 | tf_op jit(solution)/shard_map/all_to_all | solution.py:244
  97.5 0.0 collective-permute-done.2.after_ref.got_out
  97.5 0.0 copy-start.1
  97.5 1.0 copy-done.1
  98.5 0.0 copy-start.5
  98.5 5.7 %first_grad.1 = (bf16[256,768]{1,0:T(8,128)(2,1)}, bf16[32,48,128]{2,1,0:T(8,128)(2,1)S(1)}, bf16[32,48,128]{2,1,0:T(8,128)(2,1)S(1)}) custom-call(s32[2]{0:T(128)S(1)} %pad_add_fusion.at_ref, bf16[16,2,96,128]{3,2,1,0:T(8,128)(2,1)S(1)} %bitcast.13, bf16[16,2,96,128]{3,2,1,0:T(8,128)(2,1)S(1)} %collective-permute-done.1.wother_ref.other_ref, ...), custom_call_target="tpu_custom_call" | custom-call | flops 201326592 | bytes 6000000 | tf_op jit(solution)/shard_map/first_grad/pallas_call | solution.py:179
  104.3 2.7 %collective-permute-start.3 = (bf16[32,48,128]{2,1,0:T(8,128)(2,1)S(1)}, bf16[32,48,128]{2,1,0:T(8,128)(2,1)S(1)}, u32[]{:S(2)}, u32[]{:S(2)}) collective-permute-start(bf16[32,48,128]{2,1,0:T(8,128)(2,1)S(1)} %get-tuple-element.28), channel_id=1, source_target_pairs={{0,8},{8,0},{1,9},{9,1},{2,10},{10,2},{3,11},{11,3},{4,12},{12,4},... | collective-permute-start | bytes 1179656 | tf_op jit(solution)/shard_map/ppermute | solution.py:248
  107.0 1.3 collective-permute-done.3.got_in
  108.3 0.0 copy-done.5
  108.3 0.7 join.1
  109.1 15.8 %all_to_all.25.got_ref = bf16[4,8,96,128]{3,2,1,0:T(8,128)(2,1)S(1)} all-to-all(bf16[4,8,96,128]{3,2,1,0:T(8,128)(2,1)S(1)} %bitcast.14), channel_id=1, replica_groups={{0,16,256,272},{32,48,288,304},{64,80,320,336},{96,112,352,368},{128,14..., dimensions={0} | all-to-all | bytes 1572864 | tf_op jit(solution)/shard_map/all_to_all | solution.py:244
  124.9 0.1 part.1
  125.0 19.9 %all_to_all.26.got_ref = bf16[8,96,128]{2,1,0:T(8,128)(2,1)S(1)} all-to-all(bf16[8,96,128]{2,1,0:T(8,128)(2,1)S(1)} %part.1), channel_id=1, replica_groups={{0,32,64,96,128,160,192,224},{136,168,200,232,8,40,72,104},{80,112,144,..., dimensions={0} | all-to-all | bytes 393216 | tf_op jit(solution)/shard_map/all_to_all | solution.py:244
  144.9 0.6 total.1
Async XLA Ops:
  9.8 55.7 %copy-start.2 = (bf16[256,768]{1,0:T(8,128)(2,1)S(1)}, bf16[256,768]{1,0:T(8,128)(2,1)}, u32[]{:S(2)}) copy-start(bf16[256,768]{1,0:T(8,128)(2,1)} %c_ref.3) | copy-start | bytes 1179652
  9.8 50.5 %all-to-all-start = ((bf16[8,256,768]{2,1,0:T(8,128)(2,1)}), bf16[8,256,768]{2,1,0:T(8,128)(2,1)}, u32[]{:S(2)}, u32[]{:S(2)}) async-start(bf16[8,256,768]{2,1,0:T(8,128)(2,1)} %get-tuple-element.21), calls=%async_computation | async-start | bytes 6291456 | tf_op jit(solution)/shard_map/all_to_all | solution.py:244
  50.8 14.6 %collective-permute-start.1 = (bf16[16,2,96,128]{3,2,1,0:T(8,128)(2,1)S(1)}, bf16[16,2,96,128]{3,2,1,0:T(8,128)(2,1)S(1)}, u32[]{:S(2)}, u32[]{:S(2)}) collective-permute-start(bf16[16,2,96,128]{3,2,1,0:T(8,128)(2,1)S(1)} %bitcast.9), channel_id=1, source_target_pairs={{0,8},{8,0},{1,9},{9,1},{2,10},{10,2},{3,11},{11,3},{4,12},{12,4},... | collective-permute-start | bytes 2359304 | tf_op jit(solution)/shard_map/ppermute | solution.py:248
  60.2 12.7 %all-to-all-start.1 = ((bf16[8,3,64,128]{3,2,1,0:T(8,128)(2,1)}), bf16[8,3,64,128]{3,2,1,0:T(8,128)(2,1)S(1)}, u32[]{:S(2)}, u32[]{:S(2)}) async-start(bf16[8,3,64,128]{3,2,1,0:T(8,128)(2,1)} %columns.1), calls=%async_computation.1 | async-start | bytes 786432 | tf_op jit(solution)/shard_map/all_to_all | solution.py:244
  67.1 1.2 copy-start
  72.9 24.6 %all-to-all-start.2 = ((bf16[8,24,16,256]{3,2,1,0:T(8,128)(2,1)}), bf16[8,24,16,256]{3,2,1,0:T(8,128)(2,1)S(1)}, u32[]{:S(2)}, u32[]{:S(2)}) async-start(bf16[8,24,16,256]{3,2,1,0:T(8,128)(2,1)} %copy-done), calls=%async_computation.2 | async-start | bytes 3145728 | tf_op jit(solution)/shard_map/all_to_all | solution.py:244
  77.0 4.4 %collective-permute-start = (bf16[8,3,64,128]{3,2,1,0:T(8,128)(2,1)S(1)}, bf16[8,3,64,128]{3,2,1,0:T(8,128)(2,1)S(1)}, u32[]{:S(2)}, u32[]{:S(2)}) collective-permute-start(bf16[8,3,64,128]{3,2,1,0:T(8,128)(2,1)S(1)} %all-to-all-done.1.mine_ref), channel_id=1, source_target_pairs={{0,8},{8,0},{1,9},{9,1},{2,10},{10,2},{3,11},{11,3},{4,12},{12,4},... | collective-permute-start | bytes 1179656 | tf_op jit(solution)/shard_map/ppermute | solution.py:248
  81.4 1.0 copy-start.3
  88.9 0.7 copy-start.4
  89.6 7.9 %collective-permute-start.2 = (bf16[32,48,128]{2,1,0:T(8,128)(2,1)}, bf16[32,48,128]{2,1,0:T(8,128)(2,1)S(1)}, u32[]{:S(2)}, u32[]{:S(2)}) collective-permute-start(bf16[32,48,128]{2,1,0:T(8,128)(2,1)} %get-tuple-element.25), channel_id=1, source_target_pairs={{0,8},{8,0},{1,9},{9,1},{2,10},{10,2},{3,11},{11,3},{4,12},{12,4},... | collective-permute-start | bytes 1179656 | tf_op jit(solution)/shard_map/ppermute | solution.py:248
  97.5 1.0 copy-start.1
  98.5 9.8 %copy-start.5 = (bf16[32,48,128]{2,1,0:T(8,128)(2,1)S(1)}, bf16[32,48,128]{2,1,0:T(8,128)(2,1)}, u32[]{:S(2)}) copy-start(bf16[32,48,128]{2,1,0:T(8,128)(2,1)} %copy-done.4) | copy-start | bytes 1179652
  104.3 4.1 %collective-permute-start.3 = (bf16[32,48,128]{2,1,0:T(8,128)(2,1)S(1)}, bf16[32,48,128]{2,1,0:T(8,128)(2,1)S(1)}, u32[]{:S(2)}, u32[]{:S(2)}) collective-permute-start(bf16[32,48,128]{2,1,0:T(8,128)(2,1)S(1)} %get-tuple-element.28), channel_id=1, source_target_pairs={{0,8},{8,0},{1,9},{9,1},{2,10},{10,2},{3,11},{11,3},{4,12},{12,4},... | collective-permute-start | bytes 1179656 | tf_op jit(solution)/shard_map/ppermute | solution.py:248

commit v10 on v9

--- a/solution.py
+++ b/solution.py
@@ -106,7 +106,7 @@
         w = jnp.concatenate(
             [jnp.concatenate([zero[c], zero[4 + c], one[c], one[4 + c]]) for c in range(4)], axis=1
         ).astype(BF16)
-        v = dot(w, x, 0, 0)
+        v = dot(w.T, x, 1, 0)
         square = v * v
         th = jnp.tanh(ROOT * (v + 0.044715 * (v * square)))
         slope = 0.5 * (1.0 + th) + (0.5 * ROOT) * v * (1.0 - th * th) * (1.0 + 0.134145 * square)
@@ -196,7 +196,7 @@
     for n in range(32):
         place = lax.rem(n % RUN + RUN // 2 * at_ref[1], RUN)
         turn = RUNS // 2 * at_ref[1] + RUNS // 4 * (n % RUN)
-        run = lax.rem(n % 16 // RUN + 2 * RUNS - turn, RUNS)
+        run = lax.rem((n % 16 // RUN - turn) * (1 - 2 * at_ref[1]) + 4 * RUNS, RUNS)
         to = lax.rem(n // 16 + at_ref[1], 2) * 16 + place * RUNS + run
         both_ref[to, :48, :] = (keep_in[n].astype(F32) + got_in[n].astype(F32)).astype(BF16)
         both_ref[to, 48:, :] = (keep_out[n].astype(F32) + got_out[n].astype(F32)).astype(BF16)
@@ -231,7 +231,7 @@
 ]
 FAR = [
     [
-        x * 32 + ((run + RUNS // 2 * core + RUNS // 4 * n) % RUNS * RUN + n) * 2 + core
+        x * 32 + ((run * (1 - 2 * core) + RUNS // 2 * core + RUNS // 4 * n) % RUNS * RUN + n) * 2 + core
         for run in range(RUNS)
     ]
     for x in range(2)

time: 147 us -> 147 us (level)
  the two profiles are of different devices: /device:TPU:1 before, /device:TPU:2 now
where the time goes in v10:
time: 147 us; the launch traced here: 146 us
  blocking collectives  79.6 us (54%)
  starting transfers between devices  28.2 us (19%)
  Pallas kernels  19.8 us (13%)
  waiting for transfers between devices  14.2 us (10%)
  local copies, waits for them, and re-layouts  3.9 us (3%)
    all_to_all x2, blocking collectives, exchange(): lax.all_to_all(value, axis, 0, 0, axis_index_groups=groups, tiled=True)  37.8 us
    all_gather x1, blocking collectives, on_device(): mine = lax.all_gather(pair, 'z', axis=0, tiled=False)  35.6 us
    all_to_all x3, starting transfers between devices, exchange(): lax.all_to_all(value, axis, 0, 0, axis_index_groups=groups, tiled=True)  20.4 us
    pallas_call x7, Pallas kernels, call(): pl.pallas_call(kernel, name=name, out_shape=[jax.ShapeDtypeStruct(shape,...  16.4 us
    all_to_all x3, waiting for transfers between devices, exchange(): lax.all_to_all(value, axis, 0, 0, axis_index_groups=groups, tiled=True)  10.9 us
    ppermute x4, starting transfers between devices, swap_cores(): return lax.ppermute(value, 'core', [(0, 1), (1, 0)])  7.76 us
    all_gather x1, blocking collectives, on_device(): pair = lax.all_gather(shard, 'x_hi', axis=0, tiled=False)  6.22 us
    unnamed x12, local copies, waits for them, and re-layouts  3.9 us
  transfers between devices with their start and end apart: 7, of which 4 were waited for; matrix products, arithmetic and copies ran while one was open for 0% of the time, Pallas kernels for 6%

profile of v10, /device:TPU:2, one launch (start us, length us, event | category | flops | bytes accessed | tf_op | source)
XLA Modules:
  0.0 146.5 jit_solution(16030348337199746122)
XLA Ops:
  0.6 3.4 %start.1 = (bf16[96,128]{1,0:T(8,128)(2,1)}, bf16[8,256,768]{2,1,0:T(8,128)(2,1)}) custom-call(bf16[6,2,512]{2,1,0:T(2,128)(2,1)} %bitcast.16, bf16[6,8,128]{2,1,0:T(8,128)(2,1)} %bitcast.17, bf16[256,768]{1,0:T(8,128)(2,1)} %x_ref.3), custom_call_target="tpu_custom_call" | custom-call | tf_op jit(solution)/shard_map/start/pallas_call | solution.py:253
  4.0 6.2 %all-gather = bf16[192,128]{1,0:T(8,128)(2,1)S(1)} all-gather(bf16[96,128]{1,0:T(8,128)(2,1)} %get-tuple-element.19), channel_id=2, replica_groups=mesh['x_hi'=2,'z'=16,'core'=2,'x_lo'=2,'y'=4] {'x_hi'}, dimensions={0}, use_global_device_ids=true | all-gather | bytes 73728 | tf_op jit(solution)/shard_map/all_gather | solution.py:265
  10.3 0.0 copy-start.2
  10.3 10.4 %all-to-all-start = ((bf16[8,256,768]{2,1,0:T(8,128)(2,1)}), bf16[8,256,768]{2,1,0:T(8,128)(2,1)}, u32[]{:S(2)}, u32[]{:S(2)}) async-start(bf16[8,256,768]{2,1,0:T(8,128)(2,1)} %get-tuple-element.21), calls=%async_computation | async-start | bytes 6291456 | tf_op jit(solution)/shard_map/all_to_all | solution.py:244
  20.6 35.6 %all-gather.1 = bf16[32,96,128]{2,1,0:T(8,128)(2,1)S(1)} all-gather(bf16[2,96,128]{2,1,0:T(8,128)(2,1)S(1)} %bitcast.15), channel_id=3, replica_groups=mesh['x_hi'=2,'z'=16,'core'=2,'x_lo'=2,'y'=4] {'z'}, dimensions={0}, use_global_device_ids=true | all-gather | bytes 835584 | tf_op jit(solution)/shard_map/all_gather | solution.py:268
  56.2 1.9 %collective-permute-start.1 = (bf16[16,2,96,128]{3,2,1,0:T(8,128)(2,1)S(1)}, bf16[16,2,96,128]{3,2,1,0:T(8,128)(2,1)S(1)}, u32[]{:S(2)}, u32[]{:S(2)}) collective-permute-start(bf16[16,2,96,128]{3,2,1,0:T(8,128)(2,1)S(1)} %bitcast.9), channel_id=1, source_target_pairs={{0,8},{8,0},{1,9},{9,1},{2,10},{10,2},{3,11},{11,3},{4,12},{12,4},... | collective-permute-start | bytes 2359304 | tf_op jit(solution)/shard_map/ppermute | solution.py:248
  58.1 1.0 columns.1
  59.1 0.0 all-to-all-done.x_ref
  59.1 5.5 %all-to-all-start.1 = ((bf16[8,3,64,128]{3,2,1,0:T(8,128)(2,1)}), bf16[8,3,64,128]{3,2,1,0:T(8,128)(2,1)S(1)}, u32[]{:S(2)}, u32[]{:S(2)}) async-start(bf16[8,3,64,128]{3,2,1,0:T(8,128)(2,1)} %columns.1), calls=%async_computation.1 | async-start | bytes 786432 | tf_op jit(solution)/shard_map/all_to_all | solution.py:244
  64.7 0.1 pad_add_fusion.at_ref
  64.8 0.0 collective-permute-done.1.wother_ref.other_ref
  64.8 0.0 copy-done.2
  64.8 1.6 %d_mixed.1 = bf16[8,24,16,256]{3,2,1,0:T(8,128)(2,1)S(1)} custom-call(s32[2]{0:T(128)S(1)} %pad_add_fusion.at_ref, bf16[16,2,96,128]{3,2,1,0:T(8,128)(2,1)S(1)} %bitcast.11, bf16[16,2,96,128]{3,2,1,0:T(8,128)(2,1)S(1)} %collective-permute-done.1.wother_ref.other_ref, bf16[256,768]{1,0:T(8,128)(2,1)S(1)} %copy-done.2), custom_call_target="tpu_custom_call" | custom-call | flops 201326592 | bytes 6000000 | tf_op jit(solution)/shard_map/d_mixed/pallas_call | solution.py:179
  66.4 0.0 copy-start
  66.4 1.1 copy-done
  67.6 5.0 %all-to-all-done.1.mine_ref = bf16[8,3,64,128]{3,2,1,0:T(8,128)(2,1)S(1)} async-done(((bf16[8,3,64,128]{3,2,1,0:T(8,128)(2,1)}), bf16[8,3,64,128]{3,2,1,0:T(8,128)(2,1)S(1)}, u32[]{:S(2)}, u32[]{:S(2)}) %all-to-all-start.1) | async-done | bytes 393248 | tf_op jit(solution)/shard_map/all_to_all | solution.py:244
  72.6 4.5 %all-to-all-start.2 = ((bf16[8,24,16,256]{3,2,1,0:T(8,128)(2,1)}), bf16[8,24,16,256]{3,2,1,0:T(8,128)(2,1)S(1)}, u32[]{:S(2)}, u32[]{:S(2)}) async-start(bf16[8,24,16,256]{3,2,1,0:T(8,128)(2,1)} %copy-done), calls=%async_computation.2 | async-start | bytes 3145728 | tf_op jit(solution)/shard_map/all_to_all | solution.py:244
  77.1 1.9 %collective-permute-start = (bf16[8,3,64,128]{3,2,1,0:T(8,128)(2,1)S(1)}, bf16[8,3,64,128]{3,2,1,0:T(8,128)(2,1)S(1)}, u32[]{:S(2)}, u32[]{:S(2)}) collective-permute-start(bf16[8,3,64,128]{3,2,1,0:T(8,128)(2,1)S(1)} %all-to-all-done.1.mine_ref), channel_id=1, source_target_pairs={{0,8},{8,0},{1,9},{9,1},{2,10},{10,2},{3,11},{11,3},{4,12},{12,4},... | collective-permute-start | bytes 1179656 | tf_op jit(solution)/shard_map/ppermute | solution.py:248
  79.0 1.7 %collective-permute-done.other_ref = bf16[8,3,64,128]{3,2,1,0:T(8,128)(2,1)S(1)} collective-permute-done((bf16[8,3,64,128]{3,2,1,0:T(8,128)(2,1)S(1)}, bf16[8,3,64,128]{3,2,1,0:T(8,128)(2,1)S(1)}, u32[]{:S(2)}, u32[]{:S(2)}) %collective-permute-start) | collective-permute-done | bytes 393248 | tf_op jit(solution)/shard_map/ppermute | solution.py:248
  80.7 0.0 copy-start.3
  80.7 1.0 copy-done.3
  81.7 6.5 %second_grad.1 = (bf16[256,768]{1,0:T(8,128)(2,1)}, bf16[32,48,128]{2,1,0:T(8,128)(2,1)S(1)}, bf16[32,48,128]{2,1,0:T(8,128)(2,1)}) custom-call(s32[2]{0:T(128)S(1)} %pad_add_fusion.at_ref, bf16[8,256,768]{2,1,0:T(8,128)(2,1)} %all-to-all-done.x_ref, bf16[8,3,64,128]{3,2,1,0:T(8,128)(2,1)S(1)} %all-to-all-done.1.mine_ref, ...), custom_call_target="tpu_custom_call" | custom-call | flops 201326592 | bytes 6000000 | tf_op jit(solution)/shard_map/second_grad/pallas_call | solution.py:179
  88.2 0.0 copy-start.4
  88.2 0.7 copy-done.4
  88.9 2.0 %collective-permute-start.2 = (bf16[32,48,128]{2,1,0:T(8,128)(2,1)}, bf16[32,48,128]{2,1,0:T(8,128)(2,1)S(1)}, u32[]{:S(2)}, u32[]{:S(2)}) collective-permute-start(bf16[32,48,128]{2,1,0:T(8,128)(2,1)} %get-tuple-element.25), channel_id=1, source_target_pairs={{0,8},{8,0},{1,9},{9,1},{2,10},{10,2},{3,11},{11,3},{4,12},{12,4},... | collective-permute-start | bytes 1179656 | tf_op jit(solution)/shard_map/ppermute | solution.py:248
  91.0 5.9 %all-to-all-done.2.back_ref = bf16[8,24,16,256]{3,2,1,0:T(8,128)(2,1)S(1)} async-done(((bf16[8,24,16,256]{3,2,1,0:T(8,128)(2,1)}), bf16[8,24,16,256]{3,2,1,0:T(8,128)(2,1)S(1)}, u32[]{:S(2)}, u32[]{:S(2)}) %all-to-all-start.2) | async-done | bytes 1572896 | tf_op jit(solution)/shard_map/all_to_all | solution.py:244
  96.8 0.0 collective-permute-done.2.after_ref.got_out
  96.8 0.0 copy-start.1
  96.8 1.0 copy-done.1
  97.8 0.0 copy-start.5
  97.8 5.7 %first_grad.1 = (bf16[256,768]{1,0:T(8,128)(2,1)}, bf16[32,48,128]{2,1,0:T(8,128)(2,1)S(1)}, bf16[32,48,128]{2,1,0:T(8,128)(2,1)S(1)}) custom-call(s32[2]{0:T(128)S(1)} %pad_add_fusion.at_ref, bf16[16,2,96,128]{3,2,1,0:T(8,128)(2,1)S(1)} %bitcast.13, bf16[16,2,96,128]{3,2,1,0:T(8,128)(2,1)S(1)} %collective-permute-done.1.wother_ref.other_ref, ...), custom_call_target="tpu_custom_call" | custom-call | flops 201326592 | bytes 6000000 | tf_op jit(solution)/shard_map/first_grad/pallas_call | solution.py:179
  103.6 1.9 %collective-permute-start.3 = (bf16[32,48,128]{2,1,0:T(8,128)(2,1)S(1)}, bf16[32,48,128]{2,1,0:T(8,128)(2,1)S(1)}, u32[]{:S(2)}, u32[]{:S(2)}) collective-permute-start(bf16[32,48,128]{2,1,0:T(8,128)(2,1)S(1)} %get-tuple-element.28), channel_id=1, source_target_pairs={{0,8},{8,0},{1,9},{9,1},{2,10},{10,2},{3,11},{11,3},{4,12},{12,4},... | collective-permute-start | bytes 1179656 | tf_op jit(solution)/shard_map/ppermute | solution.py:248
  105.5 1.7 %collective-permute-done.3.got_in = bf16[32,48,128]{2,1,0:T(8,128)(2,1)S(1)} collective-permute-done((bf16[32,48,128]{2,1,0:T(8,128)(2,1)S(1)}, bf16[32,48,128]{2,1,0:T(8,128)(2,1)S(1)}, u32[]{:S(2)}, u32[]{:S(2)}) %collective-permute-start.3) | collective-permute-done | bytes 393248 | tf_op jit(solution)/shard_map/ppermute | solution.py:248
  107.2 0.0 copy-done.5
  107.2 0.7 join.1
  107.9 16.3 %all_to_all.25.got_ref = bf16[4,8,96,128]{3,2,1,0:T(8,128)(2,1)S(1)} all-to-all(bf16[4,8,96,128]{3,2,1,0:T(8,128)(2,1)S(1)} %bitcast.14), channel_id=1, replica_groups={{0,16,256,272},{32,48,288,304},{64,80,320,336},{96,112,352,368},{128,14..., dimensions={0} | all-to-all | bytes 1572864 | tf_op jit(solution)/shard_map/all_to_all | solution.py:244
  124.2 0.1 part.1
  124.3 21.5 %all_to_all.26.got_ref = bf16[8,96,128]{2,1,0:T(8,128)(2,1)S(1)} all-to-all(bf16[8,96,128]{2,1,0:T(8,128)(2,1)S(1)} %part.1), channel_id=1, replica_groups={{0,32,64,96,128,160,192,224},{136,104,72,40,8,232,200,168},{80,112,144,..., dimensions={0} | all-to-all | bytes 393216 | tf_op jit(solution)/shard_map/all_to_all | solution.py:244
  145.8 0.6 total.1
Async XLA Ops:
  10.3 54.5 %copy-start.2 = (bf16[256,768]{1,0:T(8,128)(2,1)S(1)}, bf16[256,768]{1,0:T(8,128)(2,1)}, u32[]{:S(2)}) copy-start(bf16[256,768]{1,0:T(8,128)(2,1)} %c_ref.3) | copy-start | bytes 1179652
  10.3 48.9 %all-to-all-start = ((bf16[8,256,768]{2,1,0:T(8,128)(2,1)}), bf16[8,256,768]{2,1,0:T(8,128)(2,1)}, u32[]{:S(2)}, u32[]{:S(2)}) async-start(bf16[8,256,768]{2,1,0:T(8,128)(2,1)} %get-tuple-element.21), calls=%async_computation | async-start | bytes 6291456 | tf_op jit(solution)/shard_map/all_to_all | solution.py:244
  56.2 8.6 %collective-permute-start.1 = (bf16[16,2,96,128]{3,2,1,0:T(8,128)(2,1)S(1)}, bf16[16,2,96,128]{3,2,1,0:T(8,128)(2,1)S(1)}, u32[]{:S(2)}, u32[]{:S(2)}) collective-permute-start(bf16[16,2,96,128]{3,2,1,0:T(8,128)(2,1)S(1)} %bitcast.9), channel_id=1, source_target_pairs={{0,8},{8,0},{1,9},{9,1},{2,10},{10,2},{3,11},{11,3},{4,12},{12,4},... | collective-permute-start | bytes 2359304 | tf_op jit(solution)/shard_map/ppermute | solution.py:248
  59.1 13.4 %all-to-all-start.1 = ((bf16[8,3,64,128]{3,2,1,0:T(8,128)(2,1)}), bf16[8,3,64,128]{3,2,1,0:T(8,128)(2,1)S(1)}, u32[]{:S(2)}, u32[]{:S(2)}) async-start(bf16[8,3,64,128]{3,2,1,0:T(8,128)(2,1)} %columns.1), calls=%async_computation.1 | async-start | bytes 786432 | tf_op jit(solution)/shard_map/all_to_all | solution.py:244
  66.4 1.2 copy-start
  72.6 24.3 %all-to-all-start.2 = ((bf16[8,24,16,256]{3,2,1,0:T(8,128)(2,1)}), bf16[8,24,16,256]{3,2,1,0:T(8,128)(2,1)S(1)}, u32[]{:S(2)}, u32[]{:S(2)}) async-start(bf16[8,24,16,256]{3,2,1,0:T(8,128)(2,1)} %copy-done), calls=%async_computation.2 | async-start | bytes 3145728 | tf_op jit(solution)/shard_map/all_to_all | solution.py:244
  77.1 3.6 %collective-permute-start = (bf16[8,3,64,128]{3,2,1,0:T(8,128)(2,1)S(1)}, bf16[8,3,64,128]{3,2,1,0:T(8,128)(2,1)S(1)}, u32[]{:S(2)}, u32[]{:S(2)}) collective-permute-start(bf16[8,3,64,128]{3,2,1,0:T(8,128)(2,1)S(1)} %all-to-all-done.1.mine_ref), channel_id=1, source_target_pairs={{0,8},{8,0},{1,9},{9,1},{2,10},{10,2},{3,11},{11,3},{4,12},{12,4},... | collective-permute-start | bytes 1179656 | tf_op jit(solution)/shard_map/ppermute | solution.py:248
  80.7 1.0 copy-start.3
  88.2 0.7 copy-start.4
  88.9 7.9 %collective-permute-start.2 = (bf16[32,48,128]{2,1,0:T(8,128)(2,1)}, bf16[32,48,128]{2,1,0:T(8,128)(2,1)S(1)}, u32[]{:S(2)}, u32[]{:S(2)}) collective-permute-start(bf16[32,48,128]{2,1,0:T(8,128)(2,1)} %get-tuple-element.25), channel_id=1, source_target_pairs={{0,8},{8,0},{1,9},{9,1},{2,10},{10,2},{3,11},{11,3},{4,12},{12,4},... | collective-permute-start | bytes 1179656 | tf_op jit(solution)/shard_map/ppermute | solution.py:248
  96.8 1.0 copy-start.1
  97.8 9.3 %copy-start.5 = (bf16[32,48,128]{2,1,0:T(8,128)(2,1)S(1)}, bf16[32,48,128]{2,1,0:T(8,128)(2,1)}, u32[]{:S(2)}) copy-start(bf16[32,48,128]{2,1,0:T(8,128)(2,1)} %copy-done.4) | copy-start | bytes 1179652
  103.6 3.6 %collective-permute-start.3 = (bf16[32,48,128]{2,1,0:T(8,128)(2,1)S(1)}, bf16[32,48,128]{2,1,0:T(8,128)(2,1)S(1)}, u32[]{:S(2)}, u32[]{:S(2)}) collective-permute-start(bf16[32,48,128]{2,1,0:T(8,128)(2,1)S(1)} %get-tuple-element.28), channel_id=1, source_target_pairs={{0,8},{8,0},{1,9},{9,1},{2,10},{10,2},{3,11},{11,3},{4,12},{12,4},... | collective-permute-start | bytes 1179656 | tf_op jit(solution)/shard_map/ppermute | solution.py:248

commit v11 on v10

--- a/solution.py
+++ b/solution.py
@@ -70,7 +70,7 @@
         for n in range(2):
             cut = slice(n * 128, n * 128 + 128)
             part = jnp.swapaxes(wide[:, p * 24 : (p + 1) * 24, cut], 0, 1)
-            send_ref[p, :, :, cut] = part.astype(BF16)
+            send_ref[lax.rem(p + 4 * at_ref[1], 8), :, :, cut] = part.astype(BF16)
 
 
 def first_rows(ref, i):
@@ -78,14 +78,15 @@
     return jnp.swapaxes(both[:, i % 2 * 8 : i % 2 * 8 + 8], 0, 1)
 
 
-def columns_kernel(mine_ref, send_ref):
+def columns_kernel(at_ref, mine_ref, send_ref):
     for pair in range(NB // 2):
         blocks = [first_rows(mine_ref, pair * 2), first_rows(mine_ref, pair * 2 + 1)]
         for c in range(4):
             rows = [blocks[i][k * 4 + c] for i in range(2) for k in range(2)]
             turned = jnp.concatenate(rows, axis=0).T.astype(BF16)
             for q in range(8):
-                send_ref[q, pair, c * 16 : (c + 1) * 16, :] = turned[q * 16 : (q + 1) * 16]
+                to = lax.rem(q + 4 * at_ref[1], 8)
+                send_ref[to, pair, c * 16 : (c + 1) * 16, :] = turned[q * 16 : (q + 1) * 16]
 
 
 ROOT = 0.7978845608028654
@@ -110,7 +111,10 @@
         square = v * v
         th = jnp.tanh(ROOT * (v + 0.044715 * (v * square)))
         slope = 0.5 * (1.0 + th) + (0.5 * ROOT) * v * (1.0 - th * th) * (1.0 + 0.134145 * square)
-        back = jnp.concatenate([back_ref[:, i * 4 + c].reshape(128, ROWS) for c in range(4)])
+        low, high = pl.ds(4 * at_ref[1], 4), pl.ds(4 - 4 * at_ref[1], 4)
+        back = jnp.concatenate(
+            [back_ref[half, i * 4 + c].reshape(64, ROWS) for c in range(4) for half in (low, high)]
+        )
         d = (back.astype(F32) * slope).astype(BF16)
         gx = dot(w, d, 1, 0)
         grad = dot(x, d, 1, 1).reshape(4, 32, 512)
@@ -138,9 +142,10 @@
     col = lax.broadcasted_iota(jnp.int32, (256, 256), 1)
     target = (row // 64 % 2) * 128 + (row % 32) * 4 + (row // 128) * 2 + row // 32 % 2
     place = jnp.where(col == target, 1.0, 0.0).astype(BF16)
-    for p in range(8):
-        mine = mine_ref[p].reshape(192, 128).astype(F32)
-        other = other_ref[p].reshape(192, 128).astype(F32)
+    for s in range(8):
+        p = lax.rem(s + 4 * at_ref[1], 8)
+        mine = mine_ref[s].reshape(192, 128).astype(F32)
+        other = other_ref[(s + 4) % 8].reshape(192, 128).astype(F32)
         w = jnp.concatenate(
             [jnp.where(first, mine, other), jnp.where(first, other, mine)], axis=1
         ).astype(BF16)
@@ -148,12 +153,12 @@
         for i in range(NB):
             rows = slice(i // 2 * 64, i // 2 * 64 + 64)
             v = dot(
-                w[rows, i % 2 * 128 : i % 2 * 128 + 128], x_ref[p, :, i * 128 : (i + 1) * 128], 1, 1
+                w[rows, i % 2 * 128 : i % 2 * 128 + 128], x_ref[s, :, i * 128 : (i + 1) * 128], 1, 1
             )
             th = jnp.tanh(ROOT * (v + 0.044715 * (v * (v * v))))
             act = (0.5 * v) * (1.0 + th)
             start = (p * NB + i) * 4
-            wide[start : start + 4] = act.reshape(4, 16, ROWS)
+            wide[pl.ds(start, 4)] = act.reshape(4, 16, ROWS)
     for g in range(0, 192, 16):
         for n in range(2):
             cut = slice(n * 128, n * 128 + 128)
@@ -240,6 +245,10 @@
 ]
 
 
+ACROSS = ("core", "x_lo", "y")
+BLOCKS = [[core * 8 + (n + 4 * core) % 8 for n in range(8)] for core in range(2)]
+
+
 def exchange(value, axis, groups=None):
     return lax.all_to_all(value, axis, 0, 0, axis_index_groups=groups, tiled=True)
 
@@ -264,22 +273,22 @@
     )(w_in.transpose(1, 0, 2), w_out.transpose(1, 0, 2), tokens)
     pair = lax.all_gather(shard, "x_hi", axis=0, tiled=False)
     copies, pair = lax.optimization_barrier((copies, pair))
-    gathered = exchange(copies, MP)
+    gathered = exchange(copies, ACROSS, BLOCKS)
     mine = lax.all_gather(pair, "z", axis=0, tiled=False)
     other = swap_cores(mine)
 
     half = ((32, 48, 128), BF16)
     (column_send,) = call(
-        columns_kernel, "columns", (mine,), [((8, 3, 64, 128), BF16)]
+        columns_kernel, "columns", (at, mine), [((8, 3, 64, 128), BF16)]
     )
     column_send, gathered = lax.optimization_barrier((column_send, gathered))
-    columns = exchange(column_send, MP)
+    columns = exchange(column_send, ACROSS, BLOCKS)
     other_columns = swap_cores(columns)
     (back_send,) = call(
         back_kernel, "d_mixed", (at, mine, other, cotangent),
         [((8, 24, 16, ROWS), BF16)], [((16, 192, ROWS), F32)],
     )
-    back = exchange(back_send, MP)
+    back = exchange(back_send, ACROSS, BLOCKS)
     output, keep_out, send_out = call(
         second_grad_kernel, "second_grad",
         (at, gathered, columns, other_columns, cotangent, mine, other),

time: 147 us -> 147 us (level)
  transfers between devices with their start and end apart: 7 -> 7, of which waited for: 4 -> 4; matrix products, arithmetic and copies ran while one was open for 0% -> 0% of each run, Pallas kernels for 6% -> 7%
where the time goes in v11:
time: 147 us
  blocking collectives  79.9 us (54%)
  starting transfers between devices  28.3 us (19%)
  Pallas kernels  20.6 us (14%)
  waiting for transfers between devices  13.3 us (9%)
  local copies, waits for them, and re-layouts  3.9 us (3%)
    all_to_all x2, blocking collectives, exchange(): lax.all_to_all(value, axis, 0, 0, axis_index_groups=groups, tiled=True)  38 us
    all_gather x1, blocking collectives, on_device(): mine = lax.all_gather(pair, 'z', axis=0, tiled=False)  35.7 us
    all_to_all x3, starting transfers between devices, exchange(): lax.all_to_all(value, axis, 0, 0, axis_index_groups=groups, tiled=True)  20.5 us
    pallas_call x7, Pallas kernels, call(): pl.pallas_call(kernel, name=name, out_shape=[jax.ShapeDtypeStruct(shape,...  17.2 us
    all_to_all x3, waiting for transfers between devices, exchange(): lax.all_to_all(value, axis, 0, 0, axis_index_groups=groups, tiled=True)  9.91 us
    ppermute x4, starting transfers between devices, swap_cores(): return lax.ppermute(value, 'core', [(0, 1), (1, 0)])  7.76 us
    all_gather x1, blocking collectives, on_device(): pair = lax.all_gather(shard, 'x_hi', axis=0, tiled=False)  6.22 us
    unnamed x12, local copies, waits for them, and re-layouts  3.9 us
  transfers between devices with their start and end apart: 7, of which 4 were waited for; matrix products, arithmetic and copies ran while one was open for 0% of the time, Pallas kernels for 7%

profile of v11, /device:TPU:2, one launch (start us, length us, event | category | flops | bytes accessed | tf_op | source)
XLA Modules:
  0.0 146.7 jit_solution(2425535696800340935)
XLA Ops:
  0.6 3.4 %start.1 = (bf16[96,128]{1,0:T(8,128)(2,1)}, bf16[8,256,768]{2,1,0:T(8,128)(2,1)}) custom-call(bf16[6,2,512]{2,1,0:T(2,128)(2,1)} %bitcast.16, bf16[6,8,128]{2,1,0:T(8,128)(2,1)} %bitcast.17, bf16[256,768]{1,0:T(8,128)(2,1)} %x_ref.3), custom_call_target="tpu_custom_call" | custom-call | tf_op jit(solution)/shard_map/start/pallas_call | solution.py:262
  4.0 6.2 %all-gather = bf16[192,128]{1,0:T(8,128)(2,1)S(1)} all-gather(bf16[96,128]{1,0:T(8,128)(2,1)} %get-tuple-element.19), channel_id=2, replica_groups=mesh['x_hi'=2,'z'=16,'core'=2,'x_lo'=2,'y'=4] {'x_hi'}, dimensions={0}, use_global_device_ids=true | all-gather | bytes 73728 | tf_op jit(solution)/shard_map/all_gather | solution.py:274
  10.3 0.0 copy-start.2
  10.3 10.4 %all-to-all-start = ((bf16[8,256,768]{2,1,0:T(8,128)(2,1)}), bf16[8,256,768]{2,1,0:T(8,128)(2,1)}, u32[]{:S(2)}, u32[]{:S(2)}) async-start(bf16[8,256,768]{2,1,0:T(8,128)(2,1)} %get-tuple-element.21), calls=%async_computation | async-start | bytes 6291456 | tf_op jit(solution)/shard_map/all_to_all | solution.py:253
  20.6 35.7 %all-gather.1 = bf16[32,96,128]{2,1,0:T(8,128)(2,1)S(1)} all-gather(bf16[2,96,128]{2,1,0:T(8,128)(2,1)S(1)} %bitcast.15), channel_id=3, replica_groups=mesh['x_hi'=2,'z'=16,'core'=2,'x_lo'=2,'y'=4] {'z'}, dimensions={0}, use_global_device_ids=true | all-gather | bytes 835584 | tf_op jit(solution)/shard_map/all_gather | solution.py:277
  56.3 1.9 %collective-permute-start.1 = (bf16[16,2,96,128]{3,2,1,0:T(8,128)(2,1)S(1)}, bf16[16,2,96,128]{3,2,1,0:T(8,128)(2,1)S(1)}, u32[]{:S(2)}, u32[]{:S(2)}) collective-permute-start(bf16[16,2,96,128]{3,2,1,0:T(8,128)(2,1)S(1)} %bitcast.9), channel_id=1, source_target_pairs={{0,8},{8,0},{1,9},{9,1},{2,10},{10,2},{3,11},{11,3},{4,12},{12,4},... | collective-permute-start | bytes 2359304 | tf_op jit(solution)/shard_map/ppermute | solution.py:257
  58.2 0.1 pad_add_fusion.at_ref
  58.3 1.6 %columns.1 = bf16[8,3,64,128]{3,2,1,0:T(8,128)(2,1)} custom-call(s32[2]{0:T(128)S(1)} %pad_add_fusion.at_ref, bf16[16,2,96,128]{3,2,1,0:T(8,128)(2,1)S(1)} %bitcast.10), custom_call_target="tpu_custom_call" | custom-call | flops 201326592 | bytes 6000000 | tf_op jit(solution)/shard_map/columns/pallas_call | solution.py:184
  59.9 0.0 all-to-all-done.x_ref
  59.9 5.8 %all-to-all-start.1 = ((bf16[8,3,64,128]{3,2,1,0:T(8,128)(2,1)}), bf16[8,3,64,128]{3,2,1,0:T(8,128)(2,1)S(1)}, u32[]{:S(2)}, u32[]{:S(2)}) async-start(bf16[8,3,64,128]{3,2,1,0:T(8,128)(2,1)} %columns.1), calls=%async_computation.1 | async-start | bytes 786432 | tf_op jit(solution)/shard_map/all_to_all | solution.py:253
  65.6 0.0 collective-permute-done.1.wother_ref.other_ref
  65.7 0.0 copy-done.2
  65.7 1.7 %d_mixed.1 = bf16[8,24,16,256]{3,2,1,0:T(8,128)(2,1)S(1)} custom-call(s32[2]{0:T(128)S(1)} %pad_add_fusion.at_ref, bf16[16,2,96,128]{3,2,1,0:T(8,128)(2,1)S(1)} %bitcast.11, bf16[16,2,96,128]{3,2,1,0:T(8,128)(2,1)S(1)} %collective-permute-done.1.wother_ref.other_ref, bf16[256,768]{1,0:T(8,128)(2,1)S(1)} %copy-done.2), custom_call_target="tpu_custom_call" | custom-call | flops 201326592 | bytes 6000000 | tf_op jit(solution)/shard_map/d_mixed/pallas_call | solution.py:184
  67.4 0.0 copy-start
  67.4 1.1 copy-done
  68.6 4.7 %all-to-all-done.1.mine_ref = bf16[8,3,64,128]{3,2,1,0:T(8,128)(2,1)S(1)} async-done(((bf16[8,3,64,128]{3,2,1,0:T(8,128)(2,1)}), bf16[8,3,64,128]{3,2,1,0:T(8,128)(2,1)S(1)}, u32[]{:S(2)}, u32[]{:S(2)}) %all-to-all-start.1) | async-done | bytes 393248 | tf_op jit(solution)/shard_map/all_to_all | solution.py:253
  73.2 4.4 %all-to-all-start.2 = ((bf16[8,24,16,256]{3,2,1,0:T(8,128)(2,1)}), bf16[8,24,16,256]{3,2,1,0:T(8,128)(2,1)S(1)}, u32[]{:S(2)}, u32[]{:S(2)}) async-start(bf16[8,24,16,256]{3,2,1,0:T(8,128)(2,1)} %copy-done), calls=%async_computation.2 | async-start | bytes 3145728 | tf_op jit(solution)/shard_map/all_to_all | solution.py:253
  77.6 1.9 %collective-permute-start = (bf16[8,3,64,128]{3,2,1,0:T(8,128)(2,1)S(1)}, bf16[8,3,64,128]{3,2,1,0:T(8,128)(2,1)S(1)}, u32[]{:S(2)}, u32[]{:S(2)}) collective-permute-start(bf16[8,3,64,128]{3,2,1,0:T(8,128)(2,1)S(1)} %all-to-all-done.1.mine_ref), channel_id=1, source_target_pairs={{0,8},{8,0},{1,9},{9,1},{2,10},{10,2},{3,11},{11,3},{4,12},{12,4},... | collective-permute-start | bytes 1179656 | tf_op jit(solution)/shard_map/ppermute | solution.py:257
  79.5 1.7 %collective-permute-done.other_ref = bf16[8,3,64,128]{3,2,1,0:T(8,128)(2,1)S(1)} collective-permute-done((bf16[8,3,64,128]{3,2,1,0:T(8,128)(2,1)S(1)}, bf16[8,3,64,128]{3,2,1,0:T(8,128)(2,1)S(1)}, u32[]{:S(2)}, u32[]{:S(2)}) %collective-permute-start) | collective-permute-done | bytes 393248 | tf_op jit(solution)/shard_map/ppermute | solution.py:257
  81.2 0.0 copy-start.3
  81.2 1.0 copy-done.3
  82.2 6.7 %second_grad.1 = (bf16[256,768]{1,0:T(8,128)(2,1)}, bf16[32,48,128]{2,1,0:T(8,128)(2,1)S(1)}, bf16[32,48,128]{2,1,0:T(8,128)(2,1)}) custom-call(s32[2]{0:T(128)S(1)} %pad_add_fusion.at_ref, bf16[8,256,768]{2,1,0:T(8,128)(2,1)} %all-to-all-done.x_ref, bf16[8,3,64,128]{3,2,1,0:T(8,128)(2,1)S(1)} %all-to-all-done.1.mine_ref, ...), custom_call_target="tpu_custom_call" | custom-call | flops 201326592 | bytes 6000000 | tf_op jit(solution)/shard_map/second_grad/pallas_call | solution.py:184
  88.9 0.0 copy-start.4
  88.9 0.7 copy-done.4
  89.6 2.0 %collective-permute-start.2 = (bf16[32,48,128]{2,1,0:T(8,128)(2,1)}, bf16[32,48,128]{2,1,0:T(8,128)(2,1)S(1)}, u32[]{:S(2)}, u32[]{:S(2)}) collective-permute-start(bf16[32,48,128]{2,1,0:T(8,128)(2,1)} %get-tuple-element.25), channel_id=1, source_target_pairs={{0,8},{8,0},{1,9},{9,1},{2,10},{10,2},{3,11},{11,3},{4,12},{12,4},... | collective-permute-start | bytes 1179656 | tf_op jit(solution)/shard_map/ppermute | solution.py:257
  91.7 5.2 %all-to-all-done.2.back_ref = bf16[8,24,16,256]{3,2,1,0:T(8,128)(2,1)S(1)} async-done(((bf16[8,24,16,256]{3,2,1,0:T(8,128)(2,1)}), bf16[8,24,16,256]{3,2,1,0:T(8,128)(2,1)S(1)}, u32[]{:S(2)}, u32[]{:S(2)}) %all-to-all-start.2) | async-done | bytes 1572896 | tf_op jit(solution)/shard_map/all_to_all | solution.py:253
  96.9 0.0 collective-permute-done.2.after_ref.got_out
  96.9 0.0 copy-start.1
  96.9 1.0 copy-done.1
  97.9 0.0 copy-start.5
  97.9 5.7 %first_grad.1 = (bf16[256,768]{1,0:T(8,128)(2,1)}, bf16[32,48,128]{2,1,0:T(8,128)(2,1)S(1)}, bf16[32,48,128]{2,1,0:T(8,128)(2,1)S(1)}) custom-call(s32[2]{0:T(128)S(1)} %pad_add_fusion.at_ref, bf16[16,2,96,128]{3,2,1,0:T(8,128)(2,1)S(1)} %bitcast.13, bf16[16,2,96,128]{3,2,1,0:T(8,128)(2,1)S(1)} %collective-permute-done.1.wother_ref.other_ref, ...), custom_call_target="tpu_custom_call" | custom-call | flops 201326592 | bytes 6000000 | tf_op jit(solution)/shard_map/first_grad/pallas_call | solution.py:184
  103.6 1.9 %collective-permute-start.3 = (bf16[32,48,128]{2,1,0:T(8,128)(2,1)S(1)}, bf16[32,48,128]{2,1,0:T(8,128)(2,1)S(1)}, u32[]{:S(2)}, u32[]{:S(2)}) collective-permute-start(bf16[32,48,128]{2,1,0:T(8,128)(2,1)S(1)} %get-tuple-element.28), channel_id=1, source_target_pairs={{0,8},{8,0},{1,9},{9,1},{2,10},{10,2},{3,11},{11,3},{4,12},{12,4},... | collective-permute-start | bytes 1179656 | tf_op jit(solution)/shard_map/ppermute | solution.py:257
  105.6 1.7 %collective-permute-done.3.got_in = bf16[32,48,128]{2,1,0:T(8,128)(2,1)S(1)} collective-permute-done((bf16[32,48,128]{2,1,0:T(8,128)(2,1)S(1)}, bf16[32,48,128]{2,1,0:T(8,128)(2,1)S(1)}, u32[]{:S(2)}, u32[]{:S(2)}) %collective-permute-start.3) | collective-permute-done | bytes 393248 | tf_op jit(solution)/shard_map/ppermute | solution.py:257
  107.2 0.0 copy-done.5
  107.2 0.7 join.1
  108.0 16.3 %all_to_all.25.got_ref = bf16[4,8,96,128]{3,2,1,0:T(8,128)(2,1)S(1)} all-to-all(bf16[4,8,96,128]{3,2,1,0:T(8,128)(2,1)S(1)} %bitcast.14), channel_id=1, replica_groups={{0,16,256,272},{32,48,288,304},{64,80,320,336},{96,112,352,368},{128,14..., dimensions={0} | all-to-all | bytes 1572864 | tf_op jit(solution)/shard_map/all_to_all | solution.py:253
  124.3 0.1 part.1
  124.4 21.7 %all_to_all.26.got_ref = bf16[8,96,128]{2,1,0:T(8,128)(2,1)S(1)} all-to-all(bf16[8,96,128]{2,1,0:T(8,128)(2,1)S(1)} %part.1), channel_id=1, replica_groups={{0,32,64,96,128,160,192,224},{136,104,72,40,8,232,200,168},{80,112,144,..., dimensions={0} | all-to-all | bytes 393216 | tf_op jit(solution)/shard_map/all_to_all | solution.py:253
  146.1 0.6 total.1
Async XLA Ops:
  10.3 55.4 %copy-start.2 = (bf16[256,768]{1,0:T(8,128)(2,1)S(1)}, bf16[256,768]{1,0:T(8,128)(2,1)}, u32[]{:S(2)}) copy-start(bf16[256,768]{1,0:T(8,128)(2,1)} %c_ref.3) | copy-start | bytes 1179652
  10.3 49.6 %all-to-all-start = ((bf16[8,256,768]{2,1,0:T(8,128)(2,1)}), bf16[8,256,768]{2,1,0:T(8,128)(2,1)}, u32[]{:S(2)}, u32[]{:S(2)}) async-start(bf16[8,256,768]{2,1,0:T(8,128)(2,1)} %get-tuple-element.21), calls=%async_computation | async-start | bytes 6291456 | tf_op jit(solution)/shard_map/all_to_all | solution.py:253
  56.3 9.3 %collective-permute-start.1 = (bf16[16,2,96,128]{3,2,1,0:T(8,128)(2,1)S(1)}, bf16[16,2,96,128]{3,2,1,0:T(8,128)(2,1)S(1)}, u32[]{:S(2)}, u32[]{:S(2)}) collective-permute-start(bf16[16,2,96,128]{3,2,1,0:T(8,128)(2,1)S(1)} %bitcast.9), channel_id=1, source_target_pairs={{0,8},{8,0},{1,9},{9,1},{2,10},{10,2},{3,11},{11,3},{4,12},{12,4},... | collective-permute-start | bytes 2359304 | tf_op jit(solution)/shard_map/ppermute | solution.py:257
  59.9 13.3 %all-to-all-start.1 = ((bf16[8,3,64,128]{3,2,1,0:T(8,128)(2,1)}), bf16[8,3,64,128]{3,2,1,0:T(8,128)(2,1)S(1)}, u32[]{:S(2)}, u32[]{:S(2)}) async-start(bf16[8,3,64,128]{3,2,1,0:T(8,128)(2,1)} %columns.1), calls=%async_computation.1 | async-start | bytes 786432 | tf_op jit(solution)/shard_map/all_to_all | solution.py:253
  67.4 1.2 copy-start
  73.2 23.7 %all-to-all-start.2 = ((bf16[8,24,16,256]{3,2,1,0:T(8,128)(2,1)}), bf16[8,24,16,256]{3,2,1,0:T(8,128)(2,1)S(1)}, u32[]{:S(2)}, u32[]{:S(2)}) async-start(bf16[8,24,16,256]{3,2,1,0:T(8,128)(2,1)} %copy-done), calls=%async_computation.2 | async-start | bytes 3145728 | tf_op jit(solution)/shard_map/all_to_all | solution.py:253
  77.6 3.6 %collective-permute-start = (bf16[8,3,64,128]{3,2,1,0:T(8,128)(2,1)S(1)}, bf16[8,3,64,128]{3,2,1,0:T(8,128)(2,1)S(1)}, u32[]{:S(2)}, u32[]{:S(2)}) collective-permute-start(bf16[8,3,64,128]{3,2,1,0:T(8,128)(2,1)S(1)} %all-to-all-done.1.mine_ref), channel_id=1, source_target_pairs={{0,8},{8,0},{1,9},{9,1},{2,10},{10,2},{3,11},{11,3},{4,12},{12,4},... | collective-permute-start | bytes 1179656 | tf_op jit(solution)/shard_map/ppermute | solution.py:257
  81.2 1.0 copy-start.3
  88.9 0.7 copy-start.4
  89.6 7.3 %collective-permute-start.2 = (bf16[32,48,128]{2,1,0:T(8,128)(2,1)}, bf16[32,48,128]{2,1,0:T(8,128)(2,1)S(1)}, u32[]{:S(2)}, u32[]{:S(2)}) collective-permute-start(bf16[32,48,128]{2,1,0:T(8,128)(2,1)} %get-tuple-element.25), channel_id=1, source_target_pairs={{0,8},{8,0},{1,9},{9,1},{2,10},{10,2},{3,11},{11,3},{4,12},{12,4},... | collective-permute-start | bytes 1179656 | tf_op jit(solution)/shard_map/ppermute | solution.py:257
  96.9 1.0 copy-start.1
  97.9 9.4 %copy-start.5 = (bf16[32,48,128]{2,1,0:T(8,128)(2,1)S(1)}, bf16[32,48,128]{2,1,0:T(8,128)(2,1)}, u32[]{:S(2)}) copy-start(bf16[32,48,128]{2,1,0:T(8,128)(2,1)} %copy-done.4) | copy-start | bytes 1179652
  103.6 3.6 %collective-permute-start.3 = (bf16[32,48,128]{2,1,0:T(8,128)(2,1)S(1)}, bf16[32,48,128]{2,1,0:T(8,128)(2,1)S(1)}, u32[]{:S(2)}, u32[]{:S(2)}) collective-permute-start(bf16[32,48,128]{2,1,0:T(8,128)(2,1)S(1)} %get-tuple-element.28), channel_id=1, source_target_pairs={{0,8},{8,0},{1,9},{9,1},{2,10},{10,2},{3,11},{11,3},{4,12},{12,4},... | collective-permute-start | bytes 1179656 | tf_op jit(solution)/shard_map/ppermute | solution.py:257
